TPU v7x, 32 devices: a whole 2x2x4 slice. The times are simulated.
32 devices in a mesh: seq: 8 (over y, x, core), tensor: 4 (over z).
Axes of the slice: x: 2, y: 2, z: 4, core: 2. Of those that a mesh axis runs over, the one named last changes fastest.
Arguments:
- tokens: bfloat16 [2048, 1024], P('seq'), may hold values from -12 to 12
- cache_keys: bfloat16 [2048, 1024], P('seq', 'tensor'), may hold values from -700 to 700
- cache_values: bfloat16 [2048, 1024], P('seq', 'tensor'), may hold values from -6 to 6
- joined_weight: float32 [1024, 3072], P(('seq', 'tensor')), may hold values from -0.1875 to 0.1875
- output_weight: float32 [1024, 1024], P(('seq', 'tensor')), may hold values from -0.1875 to 0.1875
- upward_weight: float32 [1024, 4096], P(('seq', 'tensor')), may hold values from -0.1875 to 0.1875
- downward_weight: float32 [1024, 4096], P(('seq', 'tensor')), may hold values from -0.09375 to 0.09375
- first_gain: float32 [1024], replicated, may hold values from 0.1 to 1.9
- second_gain: float32 [1024], replicated, may hold values from 0.1 to 1.9
- bias_table: float32 [32, 16], P(None, 'tensor'), may hold values from -4 to 4
- bucket_index: int32 [1023], replicated, may hold values from 0 to 31, as said below
- cached_lengths: int32 [8], replicated, may hold values from 0 to 256, as said below
- new_counts: int32 [8], replicated, may hold values from 1 to 256, as said below
- extend_flags: int32 [8], replicated, may hold values 0 or 1
Outputs:
- layer_out: bfloat16 [2048, 1024], P(('seq', 'tensor'))
Inputs may be any that keep to these rules, and one draw needn't show every extreme that they name: `cached_lengths`: some request has exactly 256 cached tokens. `new_counts`: slots of a request past its count are padding; some request fills all 256. `bucket_index`: entry 511 + o is the bucket of offset o; offsets o <= 0 take buckets below 16, offsets o > 0 the others, and on each side the bucket never falls as the distance grows.
All inputs are finite; a program needn't handle non-finite values.
Results may differ from a plain program's by a relative error of at most 0.015.
Values may be sent and summed in bfloat16 or wider, within the bound.
No kernel may reach another device: no remote copies, remote signals or barrier semaphores. Data moves between devices by JAX's collectives and lax.ppermute only.
A program may use at most 128 MiB of HBM per device.

v0:
```python
import jax
import jax.numpy as jnp
from jax import lax
from jax.sharding import PartitionSpec as P

EPSILON = 1e-06
FLOOR_SCORE = -1e30


def rms_rows(rows, gain):
    rows = rows.astype(jnp.float32)
    mean_square = jnp.mean(rows * rows, axis=-1, keepdims=True)
    return (rows * lax.rsqrt(mean_square + EPSILON) * gain).astype(jnp.bfloat16)


def row_adder(left_rows, block_rows):
    return jnp.dot(left_rows, block_rows, preferred_element_type=jnp.float32)


def column_maker(left_rows, block_rows):
    return lax.dot_general(
        left_rows, block_rows, (((1,), (1,)), ((), ())), preferred_element_type=jnp.float32
    )


def attend_block(
    carry_state, query_rows, query_pos, key_rows, value_rows, key_pos, key_ok, rel_rows
):
    row_top, row_total, weighted = carry_state
    head_count = rel_rows.shape[0]
    query_count = query_rows.shape[0]
    query_heads = query_rows.reshape(query_count, head_count, -1)
    key_heads = key_rows.reshape(key_rows.shape[0], head_count, -1)
    value_heads = value_rows.reshape(value_rows.shape[0], head_count, -1)
    span_size = (rel_rows.shape[1] + 1) // 2
    scores = jnp.einsum("qhd,khd->hqk", query_heads, key_heads, preferred_element_type=jnp.float32)
    offset = key_pos[None, :] - query_pos[:, None] + (span_size - 1)
    scores = scores + jnp.take(rel_rows, offset, axis=1)
    allowed = key_ok[None, None, :]
    new_top = jnp.maximum(row_top, jnp.max(jnp.where(allowed, scores, FLOOR_SCORE), axis=2))
    weights = jnp.where(allowed, jnp.exp(scores - new_top[:, :, None]), 0.0)
    rescale = jnp.exp(row_top - new_top)
    row_total = row_total * rescale + jnp.sum(weights, axis=2)
    update = jnp.einsum(
        "hqk,khd->qhd",
        weights.astype(jnp.bfloat16),
        value_heads,
        preferred_element_type=jnp.float32,
    )
    weighted = (
        weighted.reshape(query_count, head_count, -1) * jnp.transpose(rescale)[:, :, None] + update
    )
    return (new_top, row_total, weighted.reshape(query_count, -1))


def visit_block(
    carry_state, query_rows, query_pos, key_rows, value_rows, key_pos, key_ok, rel_rows
):
    return attend_block(
        carry_state, query_rows, query_pos, key_rows, value_rows, key_pos, key_ok, rel_rows
    )


def local_keys(
    carry_state,
    query_rows,
    query_pos,
    cache_rows,
    cache_vals,
    cache_pos,
    cache_ok,
    new_rows,
    new_vals,
    new_pos,
    new_ok,
    rel_rows,
):
    total_rows = cache_rows.shape[0]
    block_size = min(512, total_rows)
    block_count = total_rows // block_size

    def scan_step(carried, block_item):
        block_keys, block_values, block_pos, block_ok = block_item
        return (
            visit_block(
                carried,
                query_rows,
                query_pos,
                block_keys,
                block_values,
                block_pos,
                block_ok,
                rel_rows,
            ),
            None,
        )

    blocks = (
        cache_rows.reshape(block_count, block_size, -1),
        cache_vals.reshape(block_count, block_size, -1),
        cache_pos.reshape(block_count, block_size),
        cache_ok.reshape(block_count, block_size),
    )
    carry_state, unused = lax.scan(scan_step, carry_state, blocks)
    return visit_block(
        carry_state, query_rows, query_pos, new_rows, new_vals, new_pos, new_ok, rel_rows
    )


def shards(
    tokens,
    cache_keys,
    cache_values,
    joined_weight,
    output_weight,
    upward_weight,
    downward_weight,
    first_gain,
    second_gain,
    bias_table,
    bucket_index,
    cached_lengths,
    new_counts,
    extend_flags,
):
    tensor_size = lax.axis_size("tensor")
    seq_index = lax.axis_index("seq")
    tensor_index = lax.axis_index("tensor")
    new_rows = tokens.shape[0]
    cache_count = cache_keys.shape[0]
    used_len = cached_lengths[seq_index] * extend_flags[seq_index]
    new_count = new_counts[seq_index]
    attn_width = output_weight.shape[1]
    local_width = attn_width // tensor_size
    head_count = bias_table.shape[1]
    trainer_rows = joined_weight.shape[0]
    joined_send = joined_weight.reshape(trainer_rows, 3, tensor_size, local_width)
    joined_send = (
        jnp.transpose(joined_send, (0, 2, 1, 3))
        .reshape(trainer_rows, 3 * attn_width)
        .astype(jnp.bfloat16)
    )
    joined_mine, output_mine, upward_mine, downward_mine = (
        lax.all_to_all(joined_send, "tensor", split_axis=1, concat_axis=0, tiled=True),
        lax.all_to_all(
            output_weight.astype(jnp.bfloat16), "tensor", split_axis=1, concat_axis=0, tiled=True
        ),
        lax.all_to_all(
            upward_weight.astype(jnp.bfloat16), "tensor", split_axis=1, concat_axis=0, tiled=True
        ),
        lax.all_to_all(
            downward_weight.astype(jnp.bfloat16), "tensor", split_axis=1, concat_axis=0, tiled=True
        ),
    )
    normed = rms_rows(tokens, first_gain)
    projected = row_adder(normed, lax.all_gather(joined_mine, "seq", axis=0, tiled=True)).astype(
        jnp.bfloat16
    )
    query_rows = projected[:, :local_width]
    key_new = projected[:, local_width : 2 * local_width]
    value_new = projected[:, 2 * local_width :]
    bucket_hot = (
        bucket_index[:, None] == jnp.arange(bias_table.shape[0], dtype=jnp.int32)[None, :]
    ).astype(jnp.float32)
    rel_rows = jnp.einsum("bh,lb->hl", bias_table, bucket_hot, precision=lax.Precision.HIGHEST)
    cache_pos = jnp.arange(cache_count, dtype=jnp.int32)
    cache_ok = cache_pos < used_len
    new_slots = jnp.arange(new_rows, dtype=jnp.int32)
    new_pos = used_len + new_slots
    new_ok = new_slots < new_count
    empty_state = (
        jnp.full((head_count, new_rows), FLOOR_SCORE, jnp.float32),
        jnp.zeros((head_count, new_rows), jnp.float32),
        jnp.zeros((new_rows, local_width), jnp.float32),
    )
    final_top, final_total, final_sum = local_keys(
        empty_state,
        query_rows,
        new_pos,
        cache_keys,
        cache_values,
        cache_pos,
        cache_ok,
        key_new,
        value_new,
        new_pos,
        new_ok,
        rel_rows,
    )
    attention = final_sum.reshape(new_rows, head_count, -1) / jnp.transpose(final_total)[:, :, None]
    attention = attention.reshape(new_rows, local_width).astype(jnp.bfloat16)
    attended = column_maker(attention, lax.all_gather(output_mine, "seq", axis=0, tiled=True))
    share_rows = new_rows // tensor_size
    row_start = tensor_index * share_rows
    summed = lax.psum(attended.astype(jnp.bfloat16), "tensor").astype(jnp.float32)
    hidden = tokens.astype(jnp.float32) + summed
    normed_mid = rms_rows(hidden, second_gain)
    hidden_mine = lax.dynamic_slice_in_dim(hidden, row_start, share_rows, 0)
    inner = row_adder(normed_mid, lax.all_gather(upward_mine, "seq", axis=0, tiled=True))
    active = jax.nn.relu(inner).astype(jnp.bfloat16)
    feed_out = column_maker(active, lax.all_gather(downward_mine, "seq", axis=0, tiled=True))
    feed_mine = lax.psum_scatter(
        feed_out.astype(jnp.bfloat16), "tensor", scatter_dimension=0, tiled=True
    ).astype(jnp.float32)
    return (hidden_mine + feed_mine).astype(jnp.bfloat16)


def solution(mesh):
    return jax.shard_map(
        shards,
        mesh=mesh,
        in_specs=(
            P("seq", None),
            P("seq", "tensor"),
            P("seq", "tensor"),
            P(("seq", "tensor"), None),
            P(("seq", "tensor"), None),
            P(("seq", "tensor"), None),
            P(("seq", "tensor"), None),
            P(),
            P(),
            P(None, "tensor"),
            P(),
            P(),
            P(),
            P(),
        ),
        out_specs=P(("seq", "tensor"), None),
        check_vma=False,
    )
```

profile of v0, /device:TPU:0, one launch (start us, length us, event | category | flops | bytes accessed | tf_op | source)
XLA Modules:
  0.0 660.5 jit_solution(6525563530860254248)
XLA Ops:
  6.5 1.1 convert_element_type.69
  7.9 0.9 convert_element_type.72
  8.8 6.3 all-to-all-start
  15.7 0.6 dynamic_slice.24
  18.6 4.0 all-to-all-done
  22.6 3.3 all-to-all-start.1
  26.0 0.7 all-gather.4.cloned.1.call-update
  27.4 217.1 %gather_fusion = f32[65536,4]{1,0:T(8,128)} fusion(f32[4,1023]{0,1:T(8,128)S(1)} %copy.64, s32[65536]{0:T(1024)S(1)} %broadcast_clamp_fusion.1), kind=kCustom, calls=%fused_computation.clone | custom fusion | bytes 2359296 | tf_op jit(solution)/shard_map/while/body/eval_jaxpr/jit(_take)/gather | solution.py:38
  244.5 19.0 %copy.66 = f32[256,256,4]{0,1,2:T(8,128)S(1)} copy(f32[256,256,4]{2,1,0:T(8,128)} %bitcast.99) | data formatting | bytes 2097152 | tf_op jit(solution)/shard_map/while/body/eval_jaxpr/jit(_take)/gather | solution.py:38
  263.8 0.8 copy.63
  264.5 0.8 copy.62
  265.5 217.1 %gather_fusion.1 = f32[65536,4]{1,0:T(8,128)} fusion(f32[4,1023]{0,1:T(8,128)S(1)} %copy.64, s32[65536]{0:T(1024)S(1)} %broadcast_clamp_fusion), kind=kCustom, calls=%fused_computation.1.clone | custom fusion | bytes 2359296 | tf_op jit(solution)/shard_map/jit(_take)/gather | solution.py:38
  482.6 19.1 %copy.73 = f32[256,256,4]{0,1,2:T(8,128)S(1)} copy(f32[256,256,4]{2,1,0:T(8,128)} %bitcast.98) | data formatting | bytes 2097152 | tf_op jit(solution)/shard_map/jit(_take)/gather | solution.py:38
  501.7 0.8 copy.70
  503.1 0.8 copy.67
  504.7 9.9 %all_gather.13 = bf16[1024,256]{1,0:T(8,128)(2,1)S(1)} all-gather(bf16[128,256]{1,0:T(8,128)(2,1)S(1)} %bitcast.115), channel_id=1, replica_groups=mesh['seq'=8,'tensor'=4] {'seq'}, dimensions={0}, use_global_device_ids=true | all-gather | bytes 589824 | tf_op jit(solution)/shard_map/all_gather | solution.py:192
  514.5 2.0 convolution_convert_fusion.2
  516.6 0.7 fusion.47
  517.2 1.0 copy.61
  518.3 0.8 copy.69
  519.0 0.7 copy.74
  519.8 1.4 select_reduce_fusion.1
  522.9 1.2 convolution_convert_fusion
  524.2 20.1 %all_to_all.73 = bf16[32,4,1024]{2,0,1:T(8,128)(2,1)} all-to-all(bf16[32,4,1024]{2,0,1:T(8,128)(2,1)S(1)} %bitcast.109), channel_id=1, replica_groups=mesh['seq'=8,'tensor'=4] {'tensor'}, dimensions={1} | all-to-all | bytes 524288 | tf_op jit(solution)/shard_map/all_to_all | solution.py:148
  544.4 11.8 %all_to_all.74 = bf16[32,4,1024]{2,0,1:T(8,128)(2,1)} all-to-all(bf16[32,4,1024]{2,0,1:T(8,128)(2,1)S(1)} %bitcast.110), channel_id=1, replica_groups=mesh['seq'=8,'tensor'=4] {'tensor'}, dimensions={1} | all-to-all | bytes 524288 | tf_op jit(solution)/shard_map/all_to_all | solution.py:151
  556.2 10.4 %all-reduce.2.cloned.1.call-done = bf16[256,1024]{1,0:T(8,128)(2,1)} async-done(((bf16[256,1024]{1,0:T(8,128)(2,1)}), bf16[256,1024]{1,0:T(8,128)(2,1)}) %all-reduce.2.cloned.1.call-update) | async-done | bytes 524304 | tf_op jit(solution)/shard_map/psum | solution.py:195
  566.6 1.4 convert_add_fusion
  568.0 28.4 %all-gather.6.cloned.1.call-done = bf16[1024,1024]{1,0:T(8,128)(2,1)} async-done(((bf16[128,1024]{1,0:T(8,128)(2,1)}), bf16[1024,1024]{1,0:T(8,128)(2,1)}) %all-gather.6.cloned.1.call-update) | async-done | bytes 2097168 | tf_op jit(solution)/shard_map/all_gather | solution.py:199
  596.5 29.7 %all-gather.8.cloned.1.call-done = bf16[1024,1024]{1,0:T(8,128)(2,1)} async-done(((bf16[128,1024]{1,0:T(8,128)(2,1)}), bf16[1024,1024]{1,0:T(8,128)(2,1)}) %all-gather.8.cloned.1.call-update) | async-done | bytes 2097168 | tf_op jit(solution)/shard_map/all_gather | solution.py:201
  626.1 4.4 convolution_convert_fusion.1
  630.6 21.8 %reduce-scatter.2.cloned.1.call-done = bf16[64,1024]{1,0:T(8,128)(2,1)} async-done(((bf16[256,1024]{1,0:T(8,128)(2,1)}), bf16[64,1024]{1,0:T(8,128)(2,1)}) %reduce-scatter.2.cloned.1.call-update) | async-done | bytes 131088 | tf_op jit(solution)/shard_map/reduce_scatter | solution.py:202
  652.4 1.6 add_convert_fusion
  (81 shorter events, 6.4 us)
Async XLA Ops:
  6.5 20.1 %copy-start = (f32[32,4]{0,1:T(4,128)S(1)}, f32[32,4]{0,1:T(4,128)}, u32[]{:S(2)}) copy-start(f32[32,4]{0,1:T(4,128)} %param.25) | copy-start | bytes 1540
  6.5 8.6 %copy-start.17 = (s32[8]{0:T(128)S(1)}, s32[8]{0:T(128)}, u32[]{:S(2)}) copy-start(s32[8]{0:T(128)} %param.27) | copy-start | bytes 100
  6.5 9.1 %copy-start.18 = (s32[8]{0:T(128)S(1)}, s32[8]{0:T(128)}, u32[]{:S(2)}) copy-start(s32[8]{0:T(128)} %param.29) | copy-start | bytes 100
  6.5 11.4 %copy-start.10 = (f32[32,1024]{1,0:T(8,128)S(1)}, f32[32,1024]{1,0:T(8,128)}, u32[]{:S(2)}) copy-start(f32[32,1024]{1,0:T(8,128)} %param.20) | copy-start | bytes 393220
  7.6 19.1 %copy-start.14 = (s32[1023]{0:T(1024)S(1)}, s32[1023]{0:T(1024)}, u32[]{:S(2)}) copy-start(s32[1023]{0:T(1024)} %param.26) | copy-start | bytes 12280
  8.8 13.8 %all-to-all-start = ((bf16[32,4,768]{2,0,1:T(8,128)(2,1)}), bf16[32,4,768]{2,0,1:T(8,128)(2,1)S(1)}, u32[]{:S(2)}, u32[]{:S(2)}) async-start(bf16[32,4,768]{2,0,1:T(8,128)(2,1)} %convert_element_type.72), calls=%async_computation | async-start | bytes 393216 | tf_op jit(solution)/shard_map/all_to_all | solution.py:144
  22.6 3.3 copy-start.3
  22.6 482.1 %all-to-all-start.1 = ((bf16[32,4,256]{2,0,1:T(8,128)(2,1)}), bf16[32,4,256]{2,0,1:T(8,128)(2,1)S(1)}, u32[]{:S(2)}, u32[]{:S(2)}) async-start(bf16[32,4,256]{2,0,1:T(8,128)(2,1)} %bitcast.97), calls=%async_computation.1 | async-start | bytes 131072 | tf_op jit(solution)/shard_map/all_to_all | solution.py:145
  25.9 488.6 %all-gather.4.cloned.1.call-start = ((), (), s32[]{:S(2)}) async-start(), calls=%async_computation.5 | async-start | bytes 1769472 | tf_op jit(solution)/shard_map/all_gather | solution.py:156
  26.6 540.0 %all-reduce.2.cloned.1.call-start = ((), (), s32[]{:S(2)}) async-start(), calls=%async_computation.6 | async-start | bytes 1048576 | tf_op jit(solution)/shard_map/psum | solution.py:195
  244.5 20.1 %copy-start.11 = (bf16[256,256]{1,0:T(8,128)(2,1)S(1)}, bf16[256,256]{1,0:T(8,128)(2,1)}, u32[]{:S(2)}) copy-start(bf16[256,256]{1,0:T(8,128)(2,1)} %param.17) | copy-start | bytes 393220
  482.6 19.9 %copy-start.19 = (s32[8]{0:T(128)S(1)}, s32[8]{0:T(128)}, u32[]{:S(2)}) copy-start(s32[8]{0:T(128)} %param.28) | copy-start | bytes 100
  482.6 20.5 %copy-start.12 = (bf16[256,256]{1,0:T(8,128)(2,1)S(1)}, bf16[256,256]{1,0:T(8,128)(2,1)}, u32[]{:S(2)}) copy-start(bf16[256,256]{1,0:T(8,128)(2,1)} %param.18) | copy-start | bytes 393220
  482.6 21.2 %copy-start.2 = (bf16[256,1024]{1,0:T(8,128)(2,1)S(1)}, bf16[256,1024]{1,0:T(8,128)(2,1)}, u32[]{:S(2)}) copy-start(bf16[256,1024]{1,0:T(8,128)(2,1)} %param.16) | copy-start | bytes 1572868
  482.6 31.9 %copy-start.15 = (f32[1024]{0:T(1024)S(1)}, f32[1024]{0:T(1024)}, u32[]{:S(2)}) copy-start(f32[1024]{0:T(1024)} %param.23) | copy-start | bytes 12292
  519.0 2.1 copy-start.8
  519.8 1.4 copy-start.9
  521.2 0.9 copy-start.7
  521.6 0.9 copy-start.13
  522.4 1.7 copy-start.4
  522.8 21.5 %copy-start.5 = (f32[32,4096]{1,0:T(8,128)S(1)}, f32[32,4096]{1,0:T(8,128)}, u32[]{:S(2)}) copy-start(f32[32,4096]{1,0:T(8,128)} %param.22) | copy-start | bytes 1572868
  524.0 72.4 %all-gather.6.cloned.1.call-start = ((), (), s32[]{:S(2)}) async-start(), calls=%async_computation.7 | async-start | bytes 2359296 | tf_op jit(solution)/shard_map/all_gather | solution.py:199
  544.3 81.8 %copy-start.16 = (f32[1024]{0:T(1024)S(1)}, f32[1024]{0:T(1024)}, u32[]{:S(2)}) copy-start(f32[1024]{0:T(1024)} %param.24) | copy-start | bytes 12292
  544.3 81.8 %all-gather.8.cloned.1.call-start = ((), (), s32[]{:S(2)}) async-start(), calls=%async_computation.8 | async-start | bytes 2359296 | tf_op jit(solution)/shard_map/all_gather | solution.py:201
  556.2 96.2 %reduce-scatter.2.cloned.1.call-start = ((), (), s32[]{:S(2)}) async-start(), calls=%async_computation.9 | async-start | bytes 655360 | tf_op jit(solution)/shard_map/reduce_scatter | solution.py:202
  566.6 59.5 %copy-start.6 = (bf16[256,1024]{1,0:T(8,128)(2,1)S(1)}, bf16[256,1024]{1,0:T(8,128)(2,1)}, u32[]{:S(2)}) copy-start(bf16[256,1024]{1,0:T(8,128)(2,1)} %all-reduce.2.cloned.1.call-done) | copy-start | bytes 1572868
  626.1 27.8 %copy-start.1 = (f32[32,4]{0,1:T(4,128)S(1)}, f32[32,4]{0,1:T(4,128)}, u32[]{:S(2)}) copy-start(f32[32,4]{0,1:T(4,128)} %param.25) | copy-start | bytes 1540
Sparse Core Ops, SparseCore 0:
  28.6 27.1 all-gather.3
  524.2 42.4 all-reduce.1
  568.5 27.8 all-gather.5
  598.2 27.8 all-gather.7
  630.7 21.6 reduce-scatter.1
where the time goes:
time: 661 us; the launch traced here: 660 us
  local copies, waits for them, and re-layouts  483 us (73%)
  waiting for transfers between devices  95 us (14%)
  blocking collectives  41.7 us (6%)
  between operations  14.8 us (2%)
  matrix products  10.4 us (2%)
  starting transfers between devices  9.81 us (1%)
    gather x4, local copies, waits for them, and re-layouts, attend_block(): scores = scores + jnp.take(rel_rows, offset, axis=1)  472 us
    all_gather x1, waiting for transfers between devices, shards(): lax.all_gather(downward_mine, 'seq', axis=0, tiled=True)  29.7 us
    all_gather x1, waiting for transfers between devices, shards(): lax.all_gather(upward_mine, 'seq', axis=0, tiled=True)  28.4 us
    reduce_scatter x1, waiting for transfers between devices, shards(): lax.psum_scatter(feed_out.astype(jnp.bfloat16), 'tensor', scatter_dimensi...  21.8 us
    all_to_all x1, blocking collectives, shards(): lax.all_to_all(upward_weight.astype(jnp.bfloat16), 'tensor', split_axis=1...  20.1 us
  transfers between devices with their start and end apart: 7, of which 5 were waited for; matrix products, arithmetic and copies ran while one was open for 73% of the time, Pallas kernels for 0%

commit v1 on v0

v1 whole, which is shorter than its diff:
```python
import functools

import jax
import jax.numpy as jnp
from jax import lax
from jax.experimental import pallas as pl
from jax.experimental.pallas import tpu as pltpu
from jax.sharding import PartitionSpec as P

EPSILON = 1e-06
FLOOR_SCORE = -1e30
HALF = jnp.bfloat16
FULL = jnp.float32

VMEM = pl.BlockSpec(memory_space=pltpu.VMEM)
SMEM = pl.BlockSpec(memory_space=pltpu.SMEM)
ANY = pl.BlockSpec(memory_space=pl.ANY)


def params(megabytes):
    return pltpu.CompilerParams(vmem_limit_bytes=megabytes * 1024 * 1024)


def cost(flops, bytes_accessed):
    return pl.CostEstimate(flops=flops, bytes_accessed=bytes_accessed, transcendentals=0)


def swap(array, axis, mask):
    size = lax.axis_size(axis)
    return lax.ppermute(array, axis, [(i, i ^ mask) for i in range(size)])


def dot(left, right):
    return jnp.dot(left, right, preferred_element_type=FULL)


def dot_nt(left, right):
    return lax.dot_general(left, right, (((1,), (1,)), ((), ())), preferred_element_type=FULL)


def joined_kernel(ids, joined, *outs):
    mine = ids[0]
    ways = len(outs)
    width = outs[0].shape[1] // 3
    for k in range(ways):
        owner = mine ^ k
        for part in range(3):
            start = pl.multiple_of((part * ways + owner) * width, 128)
            outs[k][:, part * width : (part + 1) * width] = joined[:, pl.ds(start, width)].astype(HALF)


def forward_kernel(ids, output, upward, downward, *outs):
    mine = ids[0]
    ways = len(outs) // 2
    attn_width = output.shape[1]
    width = upward.shape[1] // ways
    output_half = output[...].astype(HALF)
    for k in range(ways):
        start = pl.multiple_of((mine ^ k) * width, 128)
        outs[k][:, :attn_width] = output_half
        outs[k][:, attn_width:] = upward[:, pl.ds(start, width)].astype(HALF)
        outs[ways + k][...] = downward[:, pl.ds(start, width)].astype(HALF)


def rms_rows(rows, gain):
    mean_square = jnp.mean(rows * rows, axis=-1, keepdims=True)
    return (rows * lax.rsqrt(mean_square + EPSILON) * gain).astype(HALF)


def prepare_kernel(ids, tokens, gain, table, buckets, normed, bias):
    used, count = ids[2], ids[3]
    normed[...] = rms_rows(tokens[...].astype(FULL), gain[...])
    heads, rows, keys = bias.shape
    cached = keys - rows
    spread = buckets.shape[1]
    hot = lax.broadcasted_iota(jnp.int32, (table.shape[0], spread), 0) == buckets[...]
    slots = lax.broadcasted_iota(jnp.int32, (rows, rows), 1)
    old_slots = lax.broadcasted_iota(jnp.int32, (rows, cached), 1)
    for h in range(heads):
        rel = jnp.sum(jnp.where(hot, table[:, h : h + 1], 0.0), axis=0, keepdims=True)
        rel = jnp.broadcast_to(rel, (8, spread))
        middle = spread // 2
        old_row = pltpu.roll(rel, used + (spread - (middle - rows)), 1)[:1, : rows + cached]
        new_row = rel[:1, middle - rows : middle + rows]
        old = jnp.broadcast_to(old_row, (rows, rows + cached))
        old = pltpu.roll(old, cached + 1, 1, stride=1, stride_axis=0)[:, :cached]
        new = jnp.broadcast_to(new_row, (rows, 2 * rows))
        new = pltpu.roll(new, rows + 1, 1, stride=1, stride_axis=0)[:, :rows]
        bias[h, :, :cached] = jnp.where(old_slots < used, old, FLOOR_SCORE)
        bias[h, :, cached:] = jnp.where(slots < count, new, FLOOR_SCORE)


def gather_copies(ids, sources, target, sems, columns=None):
    copies = []
    if len(sources) == 1:
        copies.append(pltpu.make_async_copy(sources[0], target, sems.at[0]))
        return copies
    mine, place = ids[0], ids[1]
    for j, source in enumerate(sources):
        for k in range(source.shape[0]):
            piece = source.at[k] if columns is None else source.at[k, :, columns]
            copies.append(
                pltpu.make_async_copy(
                    piece, target.at[place ^ j, mine ^ k], sems.at[j * source.shape[0] + k]
                )
            )
    return copies


def attend_kernel(pieces, ids, normed, old_keys, old_values, bias, *refs):
    sources, (out, weight, sems) = refs[:pieces], refs[pieces:]
    copies = gather_copies(ids, sources, weight, sems)
    for copy in copies:
        copy.start()
    for copy in copies:
        copy.wait()
    rows, features = normed.shape
    heads = bias.shape[0]
    width = out.shape[1]
    size = width // heads
    projected = dot(normed[...], weight[...].reshape(features, 3 * width)).astype(HALF)
    queries = projected[:, :width]
    new_keys = projected[:, width : 2 * width]
    new_values = projected[:, 2 * width :]
    cached = old_keys.shape[0]
    lanes = lax.broadcasted_iota(jnp.int32, (rows, width), 1)
    result = jnp.zeros((rows, width), FULL)
    for h in range(heads):
        inside = (lanes >= h * size) & (lanes < (h + 1) * size)
        query = jnp.where(inside, queries, jnp.zeros_like(queries))
        old = dot_nt(query, old_keys[...]) + bias[h, :, :cached]
        new = dot_nt(query, new_keys) + bias[h, :, cached:]
        top = jnp.maximum(
            jnp.max(old, axis=1, keepdims=True), jnp.max(new, axis=1, keepdims=True)
        )
        old = jnp.exp(old - top)
        new = jnp.exp(new - top)
        total = jnp.sum(old, axis=1, keepdims=True) + jnp.sum(new, axis=1, keepdims=True)
        mixed = dot(old.astype(HALF), old_values[...]) + dot(new.astype(HALF), new_values)
        result = jnp.where(inside, mixed / total, result)
    out[...] = result.astype(HALF)


def layer_kernel(pieces, ways, ids, tokens, gain, *refs):
    attended, refs = refs[:ways], refs[ways:]
    first, refs = refs[:pieces], refs[pieces:]
    second, refs = refs[:pieces], refs[pieces:]
    own, sends, refs = refs[0], refs[1:ways], refs[ways:]
    first_weight, second_weight, attention, feed, first_sems, second_sems = refs
    mine = ids[0]
    first_copies = gather_copies(ids, first, first_weight, first_sems)
    second_copies = gather_copies(ids, second, second_weight, second_sems)
    for copy in first_copies + second_copies:
        copy.start()
    rows, features = tokens.shape
    width = attended[0].shape[1]
    hidden_units = second_weight.shape[-1]
    for k in range(ways):
        start = pl.multiple_of((mine ^ k) * width, 128)
        attention[:, pl.ds(start, width)] = attended[k][...]
    for copy in first_copies:
        copy.wait()
    weight = first_weight[...].reshape(features, ways * width + hidden_units)
    hidden = tokens[...].astype(FULL) + dot_nt(attention[...], weight[:, : ways * width])
    inner = dot(rms_rows(hidden, gain[...]), weight[:, ways * width :])
    active = jnp.maximum(inner, 0.0).astype(HALF)
    for copy in second_copies:
        copy.wait()
    feed[0] = hidden
    feed[1] = dot_nt(active, second_weight[...].reshape(features, hidden_units))
    share = rows // ways
    for k in range(ways):
        start = pl.multiple_of((mine ^ k) * share, 8)
        if k == 0:
            own[...] = feed[0, pl.ds(start, share), :] + feed[1, pl.ds(start, share), :]
        else:
            sends[k - 1][...] = feed[1, pl.ds(start, share), :].astype(HALF)


def exchange(blocks):
    return [blocks[0]] + [swap(block, "tensor", k) for k, block in enumerate(blocks) if k]


def natural_gather(blocks):
    ways = len(blocks)
    mine = lax.axis_index("tensor")
    rows = jnp.concatenate([lax.select_n(mine ^ p, *blocks) for p in range(ways)])
    return [lax.all_gather(rows, "seq", axis=0, tiled=True)]


def plane_gather(blocks, near, far):
    block = jnp.stack(blocks)
    near_block = swap(block, "seq", near)
    far_block = swap(block, "seq", far)
    both_block = swap(near_block, "seq", far)
    held = {0: block, near: near_block, far: far_block, near | far: both_block}
    for j in (0, near, far, near | far):
        held[j | 1] = swap(held[j], "seq", 1)
    return [held[j] for j in range(8)]


def shards(
    tokens,
    cache_keys,
    cache_values,
    joined_weight,
    output_weight,
    upward_weight,
    downward_weight,
    first_gain,
    second_gain,
    bias_table,
    bucket_index,
    cached_lengths,
    new_counts,
    extend_flags,
):
    ways = lax.axis_size("tensor")
    places = lax.axis_size("seq")
    mine = lax.axis_index("tensor")
    place = lax.axis_index("seq")
    rows, features = tokens.shape
    cached = cache_keys.shape[0]
    heads = bias_table.shape[1]
    width = cache_keys.shape[1]
    trainer_rows = joined_weight.shape[0]
    hidden_units = upward_weight.shape[1] // ways
    attn_width = output_weight.shape[1]
    span = bucket_index.shape[0] + 1
    by_swaps = places == 8
    used = cached_lengths[place] * extend_flags[place]
    ids = jnp.stack([mine, place, used, new_counts[place]]).astype(jnp.int32)

    joined_blocks = pl.pallas_call(
        joined_kernel,
        name="cut_joined",
        out_shape=[jax.ShapeDtypeStruct((trainer_rows, 3 * width), HALF)] * ways,
        in_specs=[SMEM, VMEM],
        out_specs=[VMEM] * ways,
        compiler_params=params(16),
    )(ids, joined_weight)
    joined_blocks = exchange(joined_blocks)
    forward_blocks = pl.pallas_call(
        forward_kernel,
        name="cut_forward",
        out_shape=[jax.ShapeDtypeStruct((trainer_rows, attn_width + hidden_units), HALF)] * ways
        + [jax.ShapeDtypeStruct((trainer_rows, hidden_units), HALF)] * ways,
        in_specs=[SMEM, VMEM, VMEM, VMEM],
        out_specs=[VMEM] * (2 * ways),
        compiler_params=params(16),
    )(ids, output_weight, upward_weight, downward_weight)
    first_blocks = exchange(forward_blocks[:ways])
    second_blocks = exchange(forward_blocks[ways:])

    normed, bias = pl.pallas_call(
        prepare_kernel,
        name="prepare",
        out_shape=[
            jax.ShapeDtypeStruct((rows, features), HALF),
            jax.ShapeDtypeStruct((heads, rows, cached + rows), FULL),
        ],
        in_specs=[SMEM, VMEM, VMEM, VMEM, VMEM],
        out_specs=[VMEM, VMEM],
        compiler_params=params(24),
        cost_estimate=cost(10**8, 4 * 10**6),
    )(
        ids,
        tokens,
        first_gain.reshape(1, features),
        bias_table,
        jnp.pad(bucket_index, (0, 1)).reshape(1, span),
    )

    if by_swaps:
        joined_all = plane_gather(joined_blocks, 4, 2)
        first_all = plane_gather(first_blocks, 2, 4)
        second_all = plane_gather(second_blocks, 4, 2)
        lead = (places, ways, trainer_rows)
    else:
        joined_all = natural_gather(joined_blocks)
        first_all = natural_gather(first_blocks)
        second_all = natural_gather(second_blocks)
        lead = (features,)
    pieces = len(joined_all)
    sems = pltpu.SemaphoreType.DMA((pieces * ways,))

    attention = pl.pallas_call(
        functools.partial(attend_kernel, pieces),
        name="attend",
        out_shape=jax.ShapeDtypeStruct((rows, width), HALF),
        in_specs=[SMEM, VMEM, VMEM, VMEM, VMEM] + [ANY] * pieces,
        out_specs=VMEM,
        scratch_shapes=[pltpu.VMEM(lead + (3 * width,), HALF), sems],
        compiler_params=params(24),
        cost_estimate=cost(10**9, 6 * 10**6),
    )(ids, normed, cache_keys, cache_values, bias, *joined_all)

    attended = [attention] + [swap(attention, "tensor", k) for k in range(1, ways)]
    share = rows // ways
    own, *sends = pl.pallas_call(
        functools.partial(layer_kernel, pieces, ways),
        name="layer",
        out_shape=[jax.ShapeDtypeStruct((share, features), FULL)]
        + [jax.ShapeDtypeStruct((share, features), HALF)] * (ways - 1),
        in_specs=[SMEM, VMEM, VMEM] + [VMEM] * ways + [ANY] * (2 * pieces),
        out_specs=[VMEM] * ways,
        scratch_shapes=[
            pltpu.VMEM(lead + (attn_width + hidden_units,), HALF),
            pltpu.VMEM(lead + (hidden_units,), HALF),
            pltpu.VMEM((rows, attn_width), HALF),
            pltpu.VMEM((2, rows, features), FULL),
            sems,
            sems,
        ],
        compiler_params=params(32),
        cost_estimate=cost(2 * 10**9, 8 * 10**6),
    )(ids, tokens, second_gain.reshape(1, features), *attended, *first_all, *second_all)

    total = own
    for k, send in enumerate(sends, 1):
        total = total + swap(send, "tensor", k).astype(FULL)
    return total.astype(HALF)


def solution(mesh):
    return jax.shard_map(
        shards,
        mesh=mesh,
        in_specs=(
            P("seq", None),
            P("seq", "tensor"),
            P("seq", "tensor"),
            P(("seq", "tensor"), None),
            P(("seq", "tensor"), None),
            P(("seq", "tensor"), None),
            P(("seq", "tensor"), None),
            P(),
            P(),
            P(None, "tensor"),
            P(),
            P(),
            P(),
            P(),
        ),
        out_specs=P(("seq", "tensor"), None),
        check_vma=False,
    )
```

time: 661 us -> 124 us (0.19)
  local copies, waits for them, and re-layouts: 483 us -> 10.2 us
  blocking collectives: 41.7 us -> 0 us
  waiting for transfers between devices: 95 us -> 55.7 us
  starting transfers between devices: 9.81 us -> 40.3 us
  Pallas kernels: 0 us -> 14.7 us
  between operations: 14.8 us -> 1.59 us
  matrix products: 10.4 us -> 0 us
    gather x4 -> x0, local copies, waits for them, and re-layouts: 472 us -> none  [attend_block(): scores = scores + jnp.take(rel_rows, offset, axis=1)]
    all_gather x3 -> x0, waiting for transfers between devices: 58.1 us -> none  [the longest x1 29.7 us: shards(): lax.all_gather(downward_mine, 'seq', axis=0, tiled=True)]
    ppermute x0 -> x36, waiting for transfers between devices: none -> 55.7 us  [swap(): return lax.ppermute(array, axis, [(i, i ^ mask) for i in range(size)])]
    ppermute x0 -> x36, starting transfers between devices: none -> 40.3 us  [swap(): return lax.ppermute(array, axis, [(i, i ^ mask) for i in range(size)])]
    all_to_all x2 -> x0, blocking collectives: 31.8 us -> none  [the longest x1 20.1 us: shards(): lax.all_to_all(upward_weight.astype(jnp.bfloat16), 'tensor', split_axis=1...]
    reduce_scatter x1 -> x0, waiting for transfers between devices: 21.8 us -> none  [shards(): lax.psum_scatter(feed_out.astype(jnp.bfloat16), 'tensor', scatter_dimensi...]
    pallas_call x0 -> x5, Pallas kernels: none -> 14.7 us  [the longest x1 6.94 us: shards(): pl.pallas_call(functools.partial(layer_kernel, pieces, ways), name='layer...]
    dot_general x8 -> x0, matrix products: 10.4 us -> none  [the longest x2 5.55 us: column_maker(): lax.dot_general(left_rows, block_rows, (((1,), (1,)), ((), ())), preferre...]
  transfers between devices with their start and end apart: 7 -> 36, of which waited for: 5 -> 13; matrix products, arithmetic and copies ran while one was open for 73% -> 0% of each run, Pallas kernels for 0% -> 6%
where the time goes in v1:
time: 124 us
  waiting for transfers between devices  55.7 us (45%)
  starting transfers between devices  40.3 us (32%)
  Pallas kernels  14.7 us (12%)
  local copies, waits for them, and re-layouts  10.2 us (8%)
  other arithmetic  1.61 us (1%)
  between operations  1.59 us (1%)
    ppermute x36, waiting for transfers between devices, swap(): return lax.ppermute(array, axis, [(i, i ^ mask) for i in range(size)])  55.7 us
    ppermute x36, starting transfers between devices, swap(): return lax.ppermute(array, axis, [(i, i ^ mask) for i in range(size)])  40.3 us
    pallas_call x1, Pallas kernels, shards(): pl.pallas_call(functools.partial(layer_kernel, pieces, ways), name='layer...  6.94 us
    unnamed x35, local copies, waits for them, and re-layouts  6.24 us
    pallas_call x1, Pallas kernels, shards(): pl.pallas_call(functools.partial(attend_kernel, pieces), name='attend', o...  4.64 us
    dynamic_slice x2, local copies, waits for them, and re-layouts, shards(): used = cached_lengths[place] * extend_flags[place]  2.57 us
  transfers between devices with their start and end apart: 36, of which 13 were waited for; matrix products, arithmetic and copies ran while one was open for 0% of the time, Pallas kernels for 6%

profile of v1, /device:TPU:0, one launch (start us, length us, event | category | flops | bytes accessed | tf_op | source)
XLA Modules:
  0.0 124.1 jit_solution(11584919666500616505)
XLA Ops:
  0.0 1.4 %dynamic_slice.11 = s32[1]{0:T(128)} dynamic-slice(s32[8]{0:T(128)} %param.26, s32[]{:T(128)S(6)} %select_n.2), dynamic_slice_sizes={1} | dynamic-slice | bytes 12 | tf_op jit(solution)/shard_map/dynamic_slice | solution.py:232
  2.6 1.3 %dynamic_slice.10 = s32[1]{0:T(128)} dynamic-slice(s32[8]{0:T(128)} %param.27, s32[]{:T(128)S(6)} %select_n.2), dynamic_slice_sizes={1} | dynamic-slice | bytes 12 | tf_op jit(solution)/shard_map/dynamic_slice | solution.py:231
  9.6 5.1 %collective-permute-start.15 = (bf16[32,2048]{1,0:T(8,128)(2,1)S(1)}, bf16[32,2048]{1,0:T(8,128)(2,1)S(1)}, u32[]{:S(2)}, u32[]{:S(2)}) collective-permute-start(bf16[32,2048]{1,0:T(8,128)(2,1)S(1)} %get-tuple-element.32), channel_id=1, source_target_pairs={{0,3},{1,2},{2,1},{3,0},{4,7},{5,6},{6,5},{7,4},{8,11},{9,10},{10,... | collective-permute-start | bytes 393224 | tf_op jit(solution)/shard_map/ppermute | solution.py:30
  17.0 3.8 %collective-permute-start.2 = (bf16[32,768]{1,0:T(8,128)(2,1)S(1)}, bf16[32,768]{1,0:T(8,128)(2,1)S(1)}, u32[]{:S(2)}, u32[]{:S(2)}) collective-permute-start(bf16[32,768]{1,0:T(8,128)(2,1)S(1)} %get-tuple-element.28), channel_id=1, source_target_pairs={{0,3},{1,2},{2,1},{3,0},{4,7},{5,6},{6,5},{7,4},{8,11},{9,10},{10,... | collective-permute-start | bytes 147464 | tf_op jit(solution)/shard_map/ppermute | solution.py:30
  20.8 4.6 %collective-permute-start = (bf16[32,768]{1,0:T(8,128)(2,1)S(1)}, bf16[32,768]{1,0:T(8,128)(2,1)S(1)}, u32[]{:S(2)}, u32[]{:S(2)}) collective-permute-start(bf16[32,768]{1,0:T(8,128)(2,1)S(1)} %get-tuple-element.26), channel_id=1, source_target_pairs={{0,1},{1,0},{2,3},{3,2},{4,5},{5,4},{6,7},{7,6},{8,9},{9,8},{10,11... | collective-permute-start | bytes 147464 | tf_op jit(solution)/shard_map/ppermute | solution.py:30
  25.4 3.5 %collective-permute-done.14 = bf16[32,2048]{1,0:T(8,128)(2,1)S(1)} collective-permute-done((bf16[32,2048]{1,0:T(8,128)(2,1)S(1)}, bf16[32,2048]{1,0:T(8,128)(2,1)S(1)}, u32[]{:S(2)}, u32[]{:S(2)}) %collective-permute-start.14) | collective-permute-done | bytes 131104 | tf_op jit(solution)/shard_map/ppermute | solution.py:30
  28.9 2.7 %collective-permute-start.25 = (bf16[32,1024]{1,0:T(8,128)(2,1)S(1)}, bf16[32,1024]{1,0:T(8,128)(2,1)S(1)}, u32[]{:S(2)}, u32[]{:S(2)}) collective-permute-start(bf16[32,1024]{1,0:T(8,128)(2,1)S(1)} %get-tuple-element.36), channel_id=1, source_target_pairs={{0,3},{1,2},{2,1},{3,0},{4,7},{5,6},{6,5},{7,4},{8,11},{9,10},{10,... | collective-permute-start | bytes 196616 | tf_op jit(solution)/shard_map/ppermute | solution.py:30
  31.6 1.8 %collective-permute-start.23 = (bf16[32,1024]{1,0:T(8,128)(2,1)S(1)}, bf16[32,1024]{1,0:T(8,128)(2,1)S(1)}, u32[]{:S(2)}, u32[]{:S(2)}) collective-permute-start(bf16[32,1024]{1,0:T(8,128)(2,1)S(1)} %get-tuple-element.34), channel_id=1, source_target_pairs={{0,1},{1,0},{2,3},{3,2},{4,5},{5,4},{6,7},{7,6},{8,9},{9,8},{10,11... | collective-permute-start | bytes 196616 | tf_op jit(solution)/shard_map/ppermute | solution.py:30
  33.4 1.6 %collective-permute-start.17 = (bf16[4,32,2048]{2,1,0:T(8,128)(2,1)S(1)}, bf16[4,32,2048]{2,1,0:T(8,128)(2,1)}, u32[]{:S(2)}, u32[]{:S(2)}) collective-permute-start(bf16[4,32,2048]{2,1,0:T(8,128)(2,1)S(1)} %pad_maximum_fusion.refs_4_), channel_id=1, source_target_pairs={{0,8},{4,12},{8,0},{12,4},{16,24},{20,28},{24,16},{28,20},{1,9},{5... | collective-permute-start | bytes 1572872 | tf_op jit(solution)/shard_map/ppermute | solution.py:30
  35.1 1.4 %collective-permute-start.4 = (bf16[4,32,768]{2,1,0:T(8,128)(2,1)S(1)}, bf16[4,32,768]{2,1,0:T(8,128)(2,1)S(1)}, u32[]{:S(2)}, u32[]{:S(2)}) collective-permute-start(bf16[4,32,768]{2,1,0:T(8,128)(2,1)S(1)} %pad_maximum_fusion.2.refs_0_), channel_id=1, source_target_pairs={{0,8},{4,12},{8,0},{12,4},{16,24},{20,28},{24,16},{28,20},{1,9},{5... | collective-permute-start | bytes 589832 | tf_op jit(solution)/shard_map/ppermute | solution.py:30
  36.7 1.5 %collective-permute-start.6 = (bf16[4,32,768]{2,1,0:T(8,128)(2,1)S(1)}, bf16[4,32,768]{2,1,0:T(8,128)(2,1)S(1)}, u32[]{:S(2)}, u32[]{:S(2)}) collective-permute-start(bf16[4,32,768]{2,1,0:T(8,128)(2,1)S(1)} %pad_maximum_fusion.2.refs_0_), channel_id=1, source_target_pairs={{0,16},{4,20},{8,24},{12,28},{16,0},{20,4},{24,8},{28,12},{1,17},{... | collective-permute-start | bytes 589832 | tf_op jit(solution)/shard_map/ppermute | solution.py:30
  38.4 1.6 %collective-permute-start.27 = (bf16[4,32,1024]{2,1,0:T(8,128)(2,1)S(1)}, bf16[4,32,1024]{2,1,0:T(8,128)(2,1)S(1)}, u32[]{:S(2)}, u32[]{:S(2)}) collective-permute-start(bf16[4,32,1024]{2,1,0:T(8,128)(2,1)S(1)} %pad_maximum_fusion.1.refs_12_), channel_id=1, source_target_pairs={{0,8},{4,12},{8,0},{12,4},{16,24},{20,28},{24,16},{28,20},{1,9},{5... | collective-permute-start | bytes 786440 | tf_op jit(solution)/shard_map/ppermute | solution.py:30
  39.9 11.7 %collective-permute-done.4.refs_2_ = bf16[4,32,768]{2,1,0:T(8,128)(2,1)S(1)} collective-permute-done((bf16[4,32,768]{2,1,0:T(8,128)(2,1)S(1)}, bf16[4,32,768]{2,1,0:T(8,128)(2,1)S(1)}, u32[]{:S(2)}, u32[]{:S(2)}) %collective-permute-start.4) | collective-permute-done | bytes 196640 | tf_op jit(solution)/shard_map/ppermute | solution.py:30
  51.6 1.5 %collective-permute-start.29 = (bf16[4,32,1024]{2,1,0:T(8,128)(2,1)S(1)}, bf16[4,32,1024]{2,1,0:T(8,128)(2,1)}, u32[]{:S(2)}, u32[]{:S(2)}) collective-permute-start(bf16[4,32,1024]{2,1,0:T(8,128)(2,1)S(1)} %pad_maximum_fusion.1.refs_12_), channel_id=1, source_target_pairs={{0,16},{4,20},{8,24},{12,28},{16,0},{20,4},{24,8},{28,12},{1,17},{... | collective-permute-start | bytes 786440 | tf_op jit(solution)/shard_map/ppermute | solution.py:30
  54.4 1.5 %collective-permute-start.19 = (bf16[4,32,2048]{2,1,0:T(8,128)(2,1)S(1)}, bf16[4,32,2048]{2,1,0:T(8,128)(2,1)}, u32[]{:S(2)}, u32[]{:S(2)}) collective-permute-start(bf16[4,32,2048]{2,1,0:T(8,128)(2,1)S(1)} %pad_maximum_fusion.refs_4_), channel_id=1, source_target_pairs={{0,16},{4,20},{8,24},{12,28},{16,0},{20,4},{24,8},{28,12},{1,17},{... | collective-permute-start | bytes 1572872 | tf_op jit(solution)/shard_map/ppermute | solution.py:30
  56.5 3.3 %collective-permute-done.29.refs_16_ = bf16[4,32,1024]{2,1,0:T(8,128)(2,1)} collective-permute-done((bf16[4,32,1024]{2,1,0:T(8,128)(2,1)S(1)}, bf16[4,32,1024]{2,1,0:T(8,128)(2,1)}, u32[]{:S(2)}, u32[]{:S(2)}) %collective-permute-start.29) | collective-permute-done | bytes 262176 | tf_op jit(solution)/shard_map/ppermute | solution.py:30
  59.7 1.5 %collective-permute-start.8 = (bf16[4,32,768]{2,1,0:T(8,128)(2,1)S(1)}, bf16[4,32,768]{2,1,0:T(8,128)(2,1)S(1)}, u32[]{:S(2)}, u32[]{:S(2)}) collective-permute-start(bf16[4,32,768]{2,1,0:T(8,128)(2,1)S(1)} %collective-permute-done.6.refs_4_), channel_id=1, source_target_pairs={{0,8},{4,12},{8,0},{12,4},{16,24},{20,28},{24,16},{28,20},{1,9},{5... | collective-permute-start | bytes 589832 | tf_op jit(solution)/shard_map/ppermute | solution.py:30
  62.5 3.0 %collective-permute-done.8.refs_6_ = bf16[4,32,768]{2,1,0:T(8,128)(2,1)S(1)} collective-permute-done((bf16[4,32,768]{2,1,0:T(8,128)(2,1)S(1)}, bf16[4,32,768]{2,1,0:T(8,128)(2,1)S(1)}, u32[]{:S(2)}, u32[]{:S(2)}) %collective-permute-start.8) | collective-permute-done | bytes 196640 | tf_op jit(solution)/shard_map/ppermute | solution.py:30
  67.4 1.5 %collective-permute-start.31 = (bf16[4,32,1024]{2,1,0:T(8,128)(2,1)}, bf16[4,32,1024]{2,1,0:T(8,128)(2,1)}, u32[]{:S(2)}, u32[]{:S(2)}) collective-permute-start(bf16[4,32,1024]{2,1,0:T(8,128)(2,1)} %collective-permute-done.29.refs_16_), channel_id=1, source_target_pairs={{0,8},{4,12},{8,0},{12,4},{16,24},{20,28},{24,16},{28,20},{1,9},{5... | collective-permute-start | bytes 786440 | tf_op jit(solution)/shard_map/ppermute | solution.py:30
  68.9 2.1 %collective-permute-done.19.refs_8_ = bf16[4,32,2048]{2,1,0:T(8,128)(2,1)} collective-permute-done((bf16[4,32,2048]{2,1,0:T(8,128)(2,1)S(1)}, bf16[4,32,2048]{2,1,0:T(8,128)(2,1)}, u32[]{:S(2)}, u32[]{:S(2)}) %collective-permute-start.19) | collective-permute-done | bytes 524320 | tf_op jit(solution)/shard_map/ppermute | solution.py:30
  71.0 9.6 %collective-permute-done.21.refs_10_ = bf16[4,32,2048]{2,1,0:T(8,128)(2,1)} collective-permute-done((bf16[4,32,2048]{2,1,0:T(8,128)(2,1)}, bf16[4,32,2048]{2,1,0:T(8,128)(2,1)}, u32[]{:S(2)}, u32[]{:S(2)}) %collective-permute-start.21) | collective-permute-done | bytes 524320 | tf_op jit(solution)/shard_map/ppermute | solution.py:30
  80.7 1.9 %prepare.1 = (bf16[256,1024]{1,0:T(8,128)(2,1)S(1)}, f32[4,256,512]{2,1,0:T(8,128)S(1)}) custom-call(s32[4]{0:T(128)S(1)} %pad_add_fusion.ids, bf16[256,1024]{1,0:T(8,128)(2,1)S(1)} %copy-done, f32[1,1024]{1,0:T(1,128)S(1)} %bitcast.21, f32[32,4]{1,0:T(8,128)S(1)} %copy.15.table, s32[1,1024]{1,0:T(1,128)S(1)} %bitcast.20), custom_call_target="tpu_custom_call" | custom-call | flops 100000000 | bytes 4000000 | tf_op jit(solution)/shard_map/prepare/pallas_call | solution.py:255
  82.7 4.6 %attend.1.refs_0_ = bf16[256,256]{1,0:T(8,128)(2,1)S(1)} custom-call(s32[4]{0:T(128)S(1)} %pad_add_fusion.ids, bf16[256,1024]{1,0:T(8,128)(2,1)S(1)} %get-tuple-element.23.normed, bf16[256,256]{1,0:T(8,128)(2,1)S(1)} %copy-done.5, bf16[256,256]{1,0:T(8,128)(2,1)S(1)} %copy-done.6, f32[4,256,512]{2,1,0:T(8,128)S(1)} %get-tuple-element.24.bias, ...), custom_call_target="tpu_custom_call" | custom-call | flops 1000000000 | bytes 6000000 | tf_op jit(solution)/shard_map/attend/pallas_call | solution.py:287
  89.0 5.9 %collective-permute-done.10.refs_1_ = bf16[256,256]{1,0:T(8,128)(2,1)S(1)} collective-permute-done((bf16[256,256]{1,0:T(8,128)(2,1)S(1)}, bf16[256,256]{1,0:T(8,128)(2,1)S(1)}, u32[]{:S(2)}, u32[]{:S(2)}) %collective-permute-start.10) | collective-permute-done | bytes 131104 | tf_op jit(solution)/shard_map/ppermute | solution.py:30
  94.9 2.2 %collective-permute-done.11.refs_2_ = bf16[256,256]{1,0:T(8,128)(2,1)S(1)} collective-permute-done((bf16[256,256]{1,0:T(8,128)(2,1)S(1)}, bf16[256,256]{1,0:T(8,128)(2,1)S(1)}, u32[]{:S(2)}, u32[]{:S(2)}) %collective-permute-start.11) | collective-permute-done | bytes 131104 | tf_op jit(solution)/shard_map/ppermute | solution.py:30
  97.2 1.4 %collective-permute-start.12 = (bf16[256,256]{1,0:T(8,128)(2,1)S(1)}, bf16[256,256]{1,0:T(8,128)(2,1)S(1)}, u32[]{:S(2)}, u32[]{:S(2)}) collective-permute-start(bf16[256,256]{1,0:T(8,128)(2,1)S(1)} %attend.1.refs_0_), channel_id=1, source_target_pairs={{0,3},{1,2},{2,1},{3,0},{4,7},{5,6},{6,5},{7,4},{8,11},{9,10},{10,... | collective-permute-start | bytes 393224 | tf_op jit(solution)/shard_map/ppermute | solution.py:30
  98.6 5.4 %collective-permute-done.12.refs_3_ = bf16[256,256]{1,0:T(8,128)(2,1)S(1)} collective-permute-done((bf16[256,256]{1,0:T(8,128)(2,1)S(1)}, bf16[256,256]{1,0:T(8,128)(2,1)S(1)}, u32[]{:S(2)}, u32[]{:S(2)}) %collective-permute-start.12) | collective-permute-done | bytes 131104 | tf_op jit(solution)/shard_map/ppermute | solution.py:30
  104.0 6.9 %layer.1 = (f32[64,1024]{1,0:T(8,128)S(1)}, bf16[64,1024]{1,0:T(8,128)(2,1)S(1)}, bf16[64,1024]{1,0:T(8,128)(2,1)S(1)}, bf16[64,1024]{1,0:T(8,128)(2,1)S(1)}) custom-call(s32[4]{0:T(128)S(1)} %pad_add_fusion.ids, bf16[256,1024]{1,0:T(8,128)(2,1)S(1)} %copy-done, f32[1,1024]{1,0:T(1,128)S(1)} %bitcast.22, bf16[256,256]{1,0:T(8,128)(2,1)S(1)} %attend.1.refs_0_, ...), custom_call_target="tpu_custom_call" | custom-call | flops 2000000000 | bytes 8000000 | tf_op jit(solution)/shard_map/layer/pallas_call | solution.py:300
  111.0 1.6 %collective-permute-start.35 = (bf16[64,1024]{1,0:T(8,128)(2,1)S(1)}, bf16[64,1024]{1,0:T(8,128)(2,1)S(1)}, u32[]{:S(2)}, u32[]{:S(2)}) collective-permute-start(bf16[64,1024]{1,0:T(8,128)(2,1)S(1)} %get-tuple-element.40), channel_id=1, source_target_pairs={{0,3},{1,2},{2,1},{3,0},{4,7},{5,6},{6,5},{7,4},{8,11},{9,10},{10,... | collective-permute-start | bytes 393224 | tf_op jit(solution)/shard_map/ppermute | solution.py:30
  112.6 2.8 %collective-permute-start.33 = (bf16[64,1024]{1,0:T(8,128)(2,1)S(1)}, bf16[64,1024]{1,0:T(8,128)(2,1)S(1)}, u32[]{:S(2)}, u32[]{:S(2)}) collective-permute-start(bf16[64,1024]{1,0:T(8,128)(2,1)S(1)} %get-tuple-element.38), channel_id=1, source_target_pairs={{0,1},{1,0},{2,3},{3,2},{4,5},{5,4},{6,7},{7,6},{8,9},{9,8},{10,11... | collective-permute-start | bytes 393224 | tf_op jit(solution)/shard_map/ppermute | solution.py:30
  115.4 3.8 %collective-permute-done.35 = bf16[64,1024]{1,0:T(8,128)(2,1)S(1)} collective-permute-done((bf16[64,1024]{1,0:T(8,128)(2,1)S(1)}, bf16[64,1024]{1,0:T(8,128)(2,1)S(1)}, u32[]{:S(2)}, u32[]{:S(2)}) %collective-permute-start.35) | collective-permute-done | bytes 131104 | tf_op jit(solution)/shard_map/ppermute | solution.py:30
  119.3 4.1 %collective-permute-done.34 = bf16[64,1024]{1,0:T(8,128)(2,1)S(1)} collective-permute-done((bf16[64,1024]{1,0:T(8,128)(2,1)S(1)}, bf16[64,1024]{1,0:T(8,128)(2,1)S(1)}, u32[]{:S(2)}, u32[]{:S(2)}) %collective-permute-start.34) | collective-permute-done | bytes 131104 | tf_op jit(solution)/shard_map/ppermute | solution.py:30
  (89 shorter events, 15.8 us)
Async XLA Ops:
  9.6 11.2 %collective-permute-start.15 = (bf16[32,2048]{1,0:T(8,128)(2,1)S(1)}, bf16[32,2048]{1,0:T(8,128)(2,1)S(1)}, u32[]{:S(2)}, u32[]{:S(2)}) collective-permute-start(bf16[32,2048]{1,0:T(8,128)(2,1)S(1)} %get-tuple-element.32), channel_id=1, source_target_pairs={{0,3},{1,2},{2,1},{3,0},{4,7},{5,6},{6,5},{7,4},{8,11},{9,10},{10,... | collective-permute-start | bytes 393224 | tf_op jit(solution)/shard_map/ppermute | solution.py:30
  14.7 14.1 %collective-permute-start.14 = (bf16[32,2048]{1,0:T(8,128)(2,1)S(1)}, bf16[32,2048]{1,0:T(8,128)(2,1)S(1)}, u32[]{:S(2)}, u32[]{:S(2)}) collective-permute-start(bf16[32,2048]{1,0:T(8,128)(2,1)S(1)} %get-tuple-element.31), channel_id=1, source_target_pairs={{0,2},{1,3},{2,0},{3,1},{4,6},{5,7},{6,4},{7,5},{8,10},{9,11},{10,... | collective-permute-start | bytes 393224 | tf_op jit(solution)/shard_map/ppermute | solution.py:30
  14.7 16.8 %collective-permute-start.13 = (bf16[32,2048]{1,0:T(8,128)(2,1)S(1)}, bf16[32,2048]{1,0:T(8,128)(2,1)S(1)}, u32[]{:S(2)}, u32[]{:S(2)}) collective-permute-start(bf16[32,2048]{1,0:T(8,128)(2,1)S(1)} %get-tuple-element.30), channel_id=1, source_target_pairs={{0,1},{1,0},{2,3},{3,2},{4,5},{5,4},{6,7},{7,6},{8,9},{9,8},{10,11... | collective-permute-start | bytes 393224 | tf_op jit(solution)/shard_map/ppermute | solution.py:30
  17.0 14.7 %collective-permute-start.2 = (bf16[32,768]{1,0:T(8,128)(2,1)S(1)}, bf16[32,768]{1,0:T(8,128)(2,1)S(1)}, u32[]{:S(2)}, u32[]{:S(2)}) collective-permute-start(bf16[32,768]{1,0:T(8,128)(2,1)S(1)} %get-tuple-element.28), channel_id=1, source_target_pairs={{0,3},{1,2},{2,1},{3,0},{4,7},{5,6},{6,5},{7,4},{8,11},{9,10},{10,... | collective-permute-start | bytes 147464 | tf_op jit(solution)/shard_map/ppermute | solution.py:30
  20.8 12.7 %collective-permute-start.1 = (bf16[32,768]{1,0:T(8,128)(2,1)S(1)}, bf16[32,768]{1,0:T(8,128)(2,1)S(1)}, u32[]{:S(2)}, u32[]{:S(2)}) collective-permute-start(bf16[32,768]{1,0:T(8,128)(2,1)S(1)} %get-tuple-element.27), channel_id=1, source_target_pairs={{0,2},{1,3},{2,0},{3,1},{4,6},{5,7},{6,4},{7,5},{8,10},{9,11},{10,... | collective-permute-start | bytes 147464 | tf_op jit(solution)/shard_map/ppermute | solution.py:30
  20.8 14.2 %collective-permute-start = (bf16[32,768]{1,0:T(8,128)(2,1)S(1)}, bf16[32,768]{1,0:T(8,128)(2,1)S(1)}, u32[]{:S(2)}, u32[]{:S(2)}) collective-permute-start(bf16[32,768]{1,0:T(8,128)(2,1)S(1)} %get-tuple-element.26), channel_id=1, source_target_pairs={{0,1},{1,0},{2,3},{3,2},{4,5},{5,4},{6,7},{7,6},{8,9},{9,8},{10,11... | collective-permute-start | bytes 147464 | tf_op jit(solution)/shard_map/ppermute | solution.py:30
  28.9 6.2 %collective-permute-start.25 = (bf16[32,1024]{1,0:T(8,128)(2,1)S(1)}, bf16[32,1024]{1,0:T(8,128)(2,1)S(1)}, u32[]{:S(2)}, u32[]{:S(2)}) collective-permute-start(bf16[32,1024]{1,0:T(8,128)(2,1)S(1)} %get-tuple-element.36), channel_id=1, source_target_pairs={{0,3},{1,2},{2,1},{3,0},{4,7},{5,6},{6,5},{7,4},{8,11},{9,10},{10,... | collective-permute-start | bytes 196616 | tf_op jit(solution)/shard_map/ppermute | solution.py:30
  31.5 5.2 %collective-permute-start.24 = (bf16[32,1024]{1,0:T(8,128)(2,1)S(1)}, bf16[32,1024]{1,0:T(8,128)(2,1)S(1)}, u32[]{:S(2)}, u32[]{:S(2)}) collective-permute-start(bf16[32,1024]{1,0:T(8,128)(2,1)S(1)} %get-tuple-element.35), channel_id=1, source_target_pairs={{0,2},{1,3},{2,0},{3,1},{4,6},{5,7},{6,4},{7,5},{8,10},{9,11},{10,... | collective-permute-start | bytes 196616 | tf_op jit(solution)/shard_map/ppermute | solution.py:30
  31.6 6.6 %collective-permute-start.23 = (bf16[32,1024]{1,0:T(8,128)(2,1)S(1)}, bf16[32,1024]{1,0:T(8,128)(2,1)S(1)}, u32[]{:S(2)}, u32[]{:S(2)}) collective-permute-start(bf16[32,1024]{1,0:T(8,128)(2,1)S(1)} %get-tuple-element.34), channel_id=1, source_target_pairs={{0,1},{1,0},{2,3},{3,2},{4,5},{5,4},{6,7},{7,6},{8,9},{9,8},{10,11... | collective-permute-start | bytes 196616 | tf_op jit(solution)/shard_map/ppermute | solution.py:30
  33.4 22.5 %collective-permute-start.17 = (bf16[4,32,2048]{2,1,0:T(8,128)(2,1)S(1)}, bf16[4,32,2048]{2,1,0:T(8,128)(2,1)}, u32[]{:S(2)}, u32[]{:S(2)}) collective-permute-start(bf16[4,32,2048]{2,1,0:T(8,128)(2,1)S(1)} %pad_maximum_fusion.refs_4_), channel_id=1, source_target_pairs={{0,8},{4,12},{8,0},{12,4},{16,24},{20,28},{24,16},{28,20},{1,9},{5... | collective-permute-start | bytes 1572872 | tf_op jit(solution)/shard_map/ppermute | solution.py:30
  35.1 16.5 %collective-permute-start.4 = (bf16[4,32,768]{2,1,0:T(8,128)(2,1)S(1)}, bf16[4,32,768]{2,1,0:T(8,128)(2,1)S(1)}, u32[]{:S(2)}, u32[]{:S(2)}) collective-permute-start(bf16[4,32,768]{2,1,0:T(8,128)(2,1)S(1)} %pad_maximum_fusion.2.refs_0_), channel_id=1, source_target_pairs={{0,8},{4,12},{8,0},{12,4},{16,24},{20,28},{24,16},{28,20},{1,9},{5... | collective-permute-start | bytes 589832 | tf_op jit(solution)/shard_map/ppermute | solution.py:30
  36.7 16.4 %collective-permute-start.6 = (bf16[4,32,768]{2,1,0:T(8,128)(2,1)S(1)}, bf16[4,32,768]{2,1,0:T(8,128)(2,1)S(1)}, u32[]{:S(2)}, u32[]{:S(2)}) collective-permute-start(bf16[4,32,768]{2,1,0:T(8,128)(2,1)S(1)} %pad_maximum_fusion.2.refs_0_), channel_id=1, source_target_pairs={{0,16},{4,20},{8,24},{12,28},{16,0},{20,4},{24,8},{28,12},{1,17},{... | collective-permute-start | bytes 589832 | tf_op jit(solution)/shard_map/ppermute | solution.py:30
  38.3 14.9 %collective-permute-start.26 = (bf16[4,32,1024]{2,1,0:T(8,128)(2,1)S(1)}, bf16[4,32,1024]{2,1,0:T(8,128)(2,1)S(1)}, u32[]{:S(2)}, u32[]{:S(2)}) collective-permute-start(bf16[4,32,1024]{2,1,0:T(8,128)(2,1)S(1)} %pad_maximum_fusion.1.refs_12_), channel_id=1, source_target_pairs={{0,4},{4,0},{8,12},{12,8},{16,20},{20,16},{24,28},{28,24},{1,5},{5... | collective-permute-start | bytes 786440 | tf_op jit(solution)/shard_map/ppermute | solution.py:30
  38.4 16.1 %collective-permute-start.27 = (bf16[4,32,1024]{2,1,0:T(8,128)(2,1)S(1)}, bf16[4,32,1024]{2,1,0:T(8,128)(2,1)S(1)}, u32[]{:S(2)}, u32[]{:S(2)}) collective-permute-start(bf16[4,32,1024]{2,1,0:T(8,128)(2,1)S(1)} %pad_maximum_fusion.1.refs_12_), channel_id=1, source_target_pairs={{0,8},{4,12},{8,0},{12,4},{16,24},{20,28},{24,16},{28,20},{1,9},{5... | collective-permute-start | bytes 786440 | tf_op jit(solution)/shard_map/ppermute | solution.py:30
  51.6 8.1 %collective-permute-start.29 = (bf16[4,32,1024]{2,1,0:T(8,128)(2,1)S(1)}, bf16[4,32,1024]{2,1,0:T(8,128)(2,1)}, u32[]{:S(2)}, u32[]{:S(2)}) collective-permute-start(bf16[4,32,1024]{2,1,0:T(8,128)(2,1)S(1)} %pad_maximum_fusion.1.refs_12_), channel_id=1, source_target_pairs={{0,16},{4,20},{8,24},{12,28},{16,0},{20,4},{24,8},{28,12},{1,17},{... | collective-permute-start | bytes 786440 | tf_op jit(solution)/shard_map/ppermute | solution.py:30
  53.1 8.1 %collective-permute-start.5 = (bf16[4,32,768]{2,1,0:T(8,128)(2,1)S(1)}, bf16[4,32,768]{2,1,0:T(8,128)(2,1)S(1)}, u32[]{:S(2)}, u32[]{:S(2)}) collective-permute-start(bf16[4,32,768]{2,1,0:T(8,128)(2,1)S(1)} %collective-permute-done.4.refs_2_), channel_id=1, source_target_pairs={{0,4},{4,0},{8,12},{12,8},{16,20},{20,16},{24,28},{28,24},{1,5},{5... | collective-permute-start | bytes 589832 | tf_op jit(solution)/shard_map/ppermute | solution.py:30
  53.2 8.8 %collective-permute-start.7 = (bf16[4,32,768]{2,1,0:T(8,128)(2,1)S(1)}, bf16[4,32,768]{2,1,0:T(8,128)(2,1)S(1)}, u32[]{:S(2)}, u32[]{:S(2)}) collective-permute-start(bf16[4,32,768]{2,1,0:T(8,128)(2,1)S(1)} %collective-permute-done.6.refs_4_), channel_id=1, source_target_pairs={{0,4},{4,0},{8,12},{12,8},{16,20},{20,16},{24,28},{28,24},{1,5},{5... | collective-permute-start | bytes 589832 | tf_op jit(solution)/shard_map/ppermute | solution.py:30
  54.4 16.6 %collective-permute-start.19 = (bf16[4,32,2048]{2,1,0:T(8,128)(2,1)S(1)}, bf16[4,32,2048]{2,1,0:T(8,128)(2,1)}, u32[]{:S(2)}, u32[]{:S(2)}) collective-permute-start(bf16[4,32,2048]{2,1,0:T(8,128)(2,1)S(1)} %pad_maximum_fusion.refs_4_), channel_id=1, source_target_pairs={{0,16},{4,20},{8,24},{12,28},{16,0},{20,4},{24,8},{28,12},{1,17},{... | collective-permute-start | bytes 1572872 | tf_op jit(solution)/shard_map/ppermute | solution.py:30
  56.0 24.6 %collective-permute-start.21 = (bf16[4,32,2048]{2,1,0:T(8,128)(2,1)}, bf16[4,32,2048]{2,1,0:T(8,128)(2,1)}, u32[]{:S(2)}, u32[]{:S(2)}) collective-permute-start(bf16[4,32,2048]{2,1,0:T(8,128)(2,1)} %collective-permute-done.17.refs_6_), channel_id=1, source_target_pairs={{0,16},{4,20},{8,24},{12,28},{16,0},{20,4},{24,8},{28,12},{1,17},{... | collective-permute-start | bytes 1572872 | tf_op jit(solution)/shard_map/ppermute | solution.py:30
  59.7 5.7 %collective-permute-start.8 = (bf16[4,32,768]{2,1,0:T(8,128)(2,1)S(1)}, bf16[4,32,768]{2,1,0:T(8,128)(2,1)S(1)}, u32[]{:S(2)}, u32[]{:S(2)}) collective-permute-start(bf16[4,32,768]{2,1,0:T(8,128)(2,1)S(1)} %collective-permute-done.6.refs_4_), channel_id=1, source_target_pairs={{0,8},{4,12},{8,0},{12,4},{16,24},{20,28},{24,16},{28,20},{1,9},{5... | collective-permute-start | bytes 589832 | tf_op jit(solution)/shard_map/ppermute | solution.py:30
  65.4 22.4 %collective-permute-start.16 = (bf16[4,32,2048]{2,1,0:T(8,128)(2,1)S(1)}, bf16[4,32,2048]{2,1,0:T(8,128)(2,1)}, u32[]{:S(2)}, u32[]{:S(2)}) collective-permute-start(bf16[4,32,2048]{2,1,0:T(8,128)(2,1)S(1)} %pad_maximum_fusion.refs_4_), channel_id=1, source_target_pairs={{0,4},{4,0},{8,12},{12,8},{16,20},{20,16},{24,28},{28,24},{1,5},{5... | collective-permute-start | bytes 1572872 | tf_op jit(solution)/shard_map/ppermute | solution.py:30
  67.4 20.0 %collective-permute-start.31 = (bf16[4,32,1024]{2,1,0:T(8,128)(2,1)}, bf16[4,32,1024]{2,1,0:T(8,128)(2,1)}, u32[]{:S(2)}, u32[]{:S(2)}) collective-permute-start(bf16[4,32,1024]{2,1,0:T(8,128)(2,1)} %collective-permute-done.29.refs_16_), channel_id=1, source_target_pairs={{0,8},{4,12},{8,0},{12,4},{16,24},{20,28},{24,16},{28,20},{1,9},{5... | collective-permute-start | bytes 786440 | tf_op jit(solution)/shard_map/ppermute | solution.py:30
  68.9 35.1 %collective-permute-start.18 = (bf16[4,32,2048]{2,1,0:T(8,128)(2,1)}, bf16[4,32,2048]{2,1,0:T(8,128)(2,1)}, u32[]{:S(2)}, u32[]{:S(2)}) collective-permute-start(bf16[4,32,2048]{2,1,0:T(8,128)(2,1)} %collective-permute-done.17.refs_6_), channel_id=1, source_target_pairs={{0,4},{4,0},{8,12},{12,8},{16,20},{20,16},{24,28},{28,24},{1,5},{5... | collective-permute-start | bytes 1572872 | tf_op jit(solution)/shard_map/ppermute | solution.py:30
  71.0 33.0 %collective-permute-start.20 = (bf16[4,32,2048]{2,1,0:T(8,128)(2,1)}, bf16[4,32,2048]{2,1,0:T(8,128)(2,1)}, u32[]{:S(2)}, u32[]{:S(2)}) collective-permute-start(bf16[4,32,2048]{2,1,0:T(8,128)(2,1)} %collective-permute-done.19.refs_8_), channel_id=1, source_target_pairs={{0,4},{4,0},{8,12},{12,8},{16,20},{20,16},{24,28},{28,24},{1,5},{5... | collective-permute-start | bytes 1572872 | tf_op jit(solution)/shard_map/ppermute | solution.py:30
  80.6 23.4 %collective-permute-start.22 = (bf16[4,32,2048]{2,1,0:T(8,128)(2,1)}, bf16[4,32,2048]{2,1,0:T(8,128)(2,1)}, u32[]{:S(2)}, u32[]{:S(2)}) collective-permute-start(bf16[4,32,2048]{2,1,0:T(8,128)(2,1)} %collective-permute-done.21.refs_10_), channel_id=1, source_target_pairs={{0,4},{4,0},{8,12},{12,8},{16,20},{20,16},{24,28},{28,24},{1,5},{5... | collective-permute-start | bytes 1572872 | tf_op jit(solution)/shard_map/ppermute | solution.py:30
  87.4 7.6 %collective-permute-start.10 = (bf16[256,256]{1,0:T(8,128)(2,1)S(1)}, bf16[256,256]{1,0:T(8,128)(2,1)S(1)}, u32[]{:S(2)}, u32[]{:S(2)}) collective-permute-start(bf16[256,256]{1,0:T(8,128)(2,1)S(1)} %attend.1.refs_0_), channel_id=1, source_target_pairs={{0,1},{1,0},{2,3},{3,2},{4,5},{5,4},{6,7},{7,6},{8,9},{9,8},{10,11... | collective-permute-start | bytes 393224 | tf_op jit(solution)/shard_map/ppermute | solution.py:30
  87.8 9.4 %collective-permute-start.11 = (bf16[256,256]{1,0:T(8,128)(2,1)S(1)}, bf16[256,256]{1,0:T(8,128)(2,1)S(1)}, u32[]{:S(2)}, u32[]{:S(2)}) collective-permute-start(bf16[256,256]{1,0:T(8,128)(2,1)S(1)} %attend.1.refs_0_), channel_id=1, source_target_pairs={{0,2},{1,3},{2,0},{3,1},{4,6},{5,7},{6,4},{7,5},{8,10},{9,11},{10,... | collective-permute-start | bytes 393224 | tf_op jit(solution)/shard_map/ppermute | solution.py:30
  94.9 9.0 %collective-permute-start.32 = (bf16[4,32,1024]{2,1,0:T(8,128)(2,1)}, bf16[4,32,1024]{2,1,0:T(8,128)(2,1)S(1)}, u32[]{:S(2)}, u32[]{:S(2)}) collective-permute-start(bf16[4,32,1024]{2,1,0:T(8,128)(2,1)} %collective-permute-done.31.refs_18_), channel_id=1, source_target_pairs={{0,4},{4,0},{8,12},{12,8},{16,20},{20,16},{24,28},{28,24},{1,5},{5... | collective-permute-start | bytes 786440 | tf_op jit(solution)/shard_map/ppermute | solution.py:30
  97.2 6.8 %collective-permute-start.12 = (bf16[256,256]{1,0:T(8,128)(2,1)S(1)}, bf16[256,256]{1,0:T(8,128)(2,1)S(1)}, u32[]{:S(2)}, u32[]{:S(2)}) collective-permute-start(bf16[256,256]{1,0:T(8,128)(2,1)S(1)} %attend.1.refs_0_), channel_id=1, source_target_pairs={{0,3},{1,2},{2,1},{3,0},{4,7},{5,6},{6,5},{7,4},{8,11},{9,10},{10,... | collective-permute-start | bytes 393224 | tf_op jit(solution)/shard_map/ppermute | solution.py:30
  111.0 8.3 %collective-permute-start.35 = (bf16[64,1024]{1,0:T(8,128)(2,1)S(1)}, bf16[64,1024]{1,0:T(8,128)(2,1)S(1)}, u32[]{:S(2)}, u32[]{:S(2)}) collective-permute-start(bf16[64,1024]{1,0:T(8,128)(2,1)S(1)} %get-tuple-element.40), channel_id=1, source_target_pairs={{0,3},{1,2},{2,1},{3,0},{4,7},{5,6},{6,5},{7,4},{8,11},{9,10},{10,... | collective-permute-start | bytes 393224 | tf_op jit(solution)/shard_map/ppermute | solution.py:30
  112.5 10.8 %collective-permute-start.34 = (bf16[64,1024]{1,0:T(8,128)(2,1)S(1)}, bf16[64,1024]{1,0:T(8,128)(2,1)S(1)}, u32[]{:S(2)}, u32[]{:S(2)}) collective-permute-start(bf16[64,1024]{1,0:T(8,128)(2,1)S(1)} %get-tuple-element.39), channel_id=1, source_target_pairs={{0,2},{1,3},{2,0},{3,1},{4,6},{5,7},{6,4},{7,5},{8,10},{9,11},{10,... | collective-permute-start | bytes 393224 | tf_op jit(solution)/shard_map/ppermute | solution.py:30
  112.6 10.8 %collective-permute-start.33 = (bf16[64,1024]{1,0:T(8,128)(2,1)S(1)}, bf16[64,1024]{1,0:T(8,128)(2,1)S(1)}, u32[]{:S(2)}, u32[]{:S(2)}) collective-permute-start(bf16[64,1024]{1,0:T(8,128)(2,1)S(1)} %get-tuple-element.38), channel_id=1, source_target_pairs={{0,1},{1,0},{2,3},{3,2},{4,5},{5,4},{6,7},{7,6},{8,9},{9,8},{10,11... | collective-permute-start | bytes 393224 | tf_op jit(solution)/shard_map/ppermute | solution.py:30
  (21 other events, 549.3 us)

commit v2 on v1

v2 whole, which is shorter than its diff:
```python
import functools

import jax
import jax.numpy as jnp
from jax import lax
from jax.experimental import pallas as pl
from jax.experimental.pallas import tpu as pltpu
from jax.sharding import PartitionSpec as P

EPSILON = 1e-06
FLOOR_SCORE = -1e30
HALF = jnp.bfloat16
FULL = jnp.float32
VMEM_GRANT = 60
ATTEND_COST = 2 * 10**10

VMEM = pl.BlockSpec(memory_space=pltpu.VMEM)
SMEM = pl.BlockSpec(memory_space=pltpu.SMEM)
HBM = pl.BlockSpec(memory_space=pltpu.HBM)
ANY = pl.BlockSpec(memory_space=pl.ANY)


def params(megabytes):
    return pltpu.CompilerParams(vmem_limit_bytes=megabytes * 1024 * 1024)


def cost(flops, bytes_accessed):
    return pl.CostEstimate(flops=flops, bytes_accessed=bytes_accessed, transcendentals=0)


def swap(array, axis, mask):
    size = lax.axis_size(axis)
    return lax.ppermute(array, axis, [(i, i ^ mask) for i in range(size)])


def dot(left, right):
    return jnp.dot(left, right, preferred_element_type=FULL)


def dot_nt(left, right):
    return lax.dot_general(left, right, (((1,), (1,)), ((), ())), preferred_element_type=FULL)


def here():
    return lax.axis_index("tensor"), lax.axis_index("seq")


def load(sources, targets, sems):
    copies = [
        pltpu.make_async_copy(source, target, sems.at[i])
        for i, (source, target) in enumerate(zip(sources, targets))
    ]
    for copy in copies:
        copy.start()
    for copy in copies:
        copy.wait()


def joined_kernel(joined_source, *refs):
    outs, (joined, sems) = refs[:-2], refs[-2:]
    load([joined_source], [joined], sems)
    mine, _ = here()
    ways = len(outs)
    width = outs[0].shape[1] // 3
    for k in range(ways):
        owner = mine ^ k
        for part in range(3):
            start = pl.multiple_of((part * ways + owner) * width, 128)
            outs[k][:, part * width : (part + 1) * width] = joined[:, pl.ds(start, width)].astype(HALF)


def forward_kernel(*refs):
    sources, (blocks, output, upward, downward, sems) = refs[-8:-5], refs[-5:]
    load(sources, [output, upward, downward], sems)
    ways = blocks.shape[0]
    whole = output.shape[1]
    width = upward.shape[1] // ways
    output_half = output[...].astype(HALF)
    for t in range(ways):
        blocks[t, :, :whole] = output_half
        blocks[t, :, whole : whole + width] = upward[:, t * width : (t + 1) * width].astype(HALF)
        blocks[t, :, whole + width :] = downward[:, t * width : (t + 1) * width].astype(HALF)


def rms_rows(rows, gain):
    mean_square = jnp.mean(rows * rows, axis=-1, keepdims=True)
    return (rows * lax.rsqrt(mean_square + EPSILON) * gain).astype(HALF)


def prepare_kernel(after, lengths, flags, counts, tokens, gain, table, buckets, normed, bias, *refs):
    numbers, padded, sems = refs
    load([lengths, flags, counts], [numbers.at[i] for i in range(3)], sems)
    _, place = here()
    used = numbers[0, place] * numbers[1, place]
    count = numbers[2, place]
    padded[...] = jnp.zeros_like(padded)
    padded[:, : buckets.shape[1]] = buckets[...]
    normed[...] = rms_rows(tokens[...].astype(FULL), gain[...])
    heads, rows, keys = bias.shape
    cached = keys - rows
    spread = padded.shape[1]
    hot = lax.broadcasted_iota(jnp.int32, (table.shape[1], spread), 0) == padded[...]
    rows_of_heads = jnp.dot(
        table[...],
        hot.astype(FULL),
        precision=lax.Precision.HIGHEST,
        preferred_element_type=FULL,
    )
    slots = lax.broadcasted_iota(jnp.int32, (rows, rows), 1)
    old_slots = lax.broadcasted_iota(jnp.int32, (rows, cached), 1)
    for h in range(heads):
        rel = jnp.broadcast_to(rows_of_heads[h : h + 1], (8, spread))
        middle = spread // 2
        old_row = pltpu.roll(rel, used + (spread - (middle - rows)), 1)[:1, : rows + cached]
        new_row = rel[:1, middle - rows : middle + rows]
        old = jnp.broadcast_to(old_row, (rows, rows + cached))
        old = pltpu.roll(old, cached + 1, 1, stride=1, stride_axis=0)[:, :cached]
        new = jnp.broadcast_to(new_row, (rows, 2 * rows))
        new = pltpu.roll(new, rows + 1, 1, stride=1, stride_axis=0)[:, :rows]
        bias[h, :, :cached] = jnp.where(old_slots < used, old, FLOOR_SCORE)
        bias[h, :, cached:] = jnp.where(slots < count, new, FLOOR_SCORE)


def stack_kernel(ways, *refs):
    target, sems = refs[-2:]
    mine, _ = here()
    load(refs[:ways], [target.at[mine ^ k] for k in range(ways)], sems)


def stack(blocks, *after):
    ways = len(blocks)
    return pl.pallas_call(
        functools.partial(stack_kernel, ways),
        name="stack",
        out_shape=jax.ShapeDtypeStruct((ways,) + blocks[0].shape, HALF),
        in_specs=[HBM] * ways + [ANY] * len(after),
        out_specs=VMEM,
        scratch_shapes=[pltpu.SemaphoreType.DMA((ways,))],
        compiler_params=params(VMEM_GRANT),
    )(*blocks, *after)


def gather_copies(pieces, sources, start, target, sems):
    width = target.shape[-1]
    if len(sources) == 1:
        source = sources[0].at[:, start : start + width]
        return [pltpu.make_async_copy(source, target, sems.at[0])]
    _, place = here()
    copies = []
    for i, ((j, t), source) in enumerate(zip(pieces, sources)):
        block = target.at[place ^ j, t : t + source.shape[0]]
        source = source.at[:, :, start : start + width]
        copies.append(pltpu.make_async_copy(source, block, sems.at[i]))
    return copies


def attend_kernel(pieces, normed, old_keys, old_values, bias, *refs):
    sources, (out, weight, sems) = refs[: len(pieces)], refs[len(pieces) :]
    copies = gather_copies(pieces, sources, 0, weight, sems)
    for copy in copies:
        copy.start()
    for copy in copies:
        copy.wait()
    rows, features = normed.shape
    heads = bias.shape[0]
    width = out.shape[1]
    size = width // heads
    projected = dot(normed[...], weight[...].reshape(features, 3 * width)).astype(HALF)
    queries = projected[:, :width]
    new_keys = projected[:, width : 2 * width]
    new_values = projected[:, 2 * width :]
    cached = old_keys.shape[0]
    lanes = lax.broadcasted_iota(jnp.int32, (rows, width), 1)
    result = jnp.zeros((rows, width), FULL)
    for h in range(heads):
        inside = (lanes >= h * size) & (lanes < (h + 1) * size)
        query = jnp.where(inside, queries, jnp.zeros_like(queries))
        old = dot_nt(query, old_keys[...]) + bias[h, :, :cached]
        new = dot_nt(query, new_keys) + bias[h, :, cached:]
        top = jnp.maximum(
            jnp.max(old, axis=1, keepdims=True), jnp.max(new, axis=1, keepdims=True)
        )
        old = jnp.exp(old - top)
        new = jnp.exp(new - top)
        total = jnp.sum(old, axis=1, keepdims=True) + jnp.sum(new, axis=1, keepdims=True)
        mixed = dot(old.astype(HALF), old_values[...]) + dot(new.astype(HALF), new_values)
        result = jnp.where(inside, mixed / total, result)
    out[...] = result.astype(HALF)


def layer_kernel(pieces, ways, tokens, gain, *refs):
    attended, refs = refs[:ways], refs[ways:]
    sources, refs = refs[: len(pieces)], refs[len(pieces) :]
    outs, (output, upward, downward, attention, hidden, feed, sems) = refs[:ways], refs[ways:]
    features = tokens.shape[1]
    copies, start = [], 0
    for i, weight in enumerate((output, upward, downward)):
        copies.append(gather_copies(pieces, sources, start, weight, sems.at[i]))
        start += weight.shape[-1]
        for copy in copies[-1]:
            copy.start()
    mine, _ = here()
    width = attended[0].shape[1]
    for k in range(ways):
        attention[:, pl.ds(pl.multiple_of((mine ^ k) * width, 128), width)] = attended[k][...]

    def arrived(i, weight):
        for copy in copies[i]:
            copy.wait()
        return weight[...].reshape(features, -1)

    hidden[...] = tokens[...].astype(FULL) + dot_nt(attention[...], arrived(0, output))
    inner = dot(rms_rows(hidden[...], gain[...]), arrived(1, upward))
    active = jnp.maximum(inner, 0.0).astype(HALF)
    feed[...] = dot_nt(active, arrived(2, downward))
    share = tokens.shape[0] // ways
    for k in range(ways):
        rows_of = pl.ds(pl.multiple_of((mine ^ k) * share, 8), share)
        if k == 0:
            outs[0][...] = hidden[rows_of, :] + feed[rows_of, :]
        else:
            outs[k][...] = feed[rows_of, :].astype(HALF)


def exchange(blocks):
    return [blocks[0]] + [swap(block, "tensor", k) for k, block in enumerate(blocks) if k]


def natural_gather(rows):
    return lax.all_gather(rows.reshape(-1, rows.shape[-1]), "seq", axis=0, tiled=True)


def together(*arrays):
    return lax.optimization_barrier(arrays)


NEAR, FAR = 4, 2


def first_hops(block):
    return together(swap(block, "seq", NEAR), swap(block, "seq", FAR))


def with_cores(held):
    for (j, t), piece in list(held.items()):
        held[j | 1, t] = swap(piece, "seq", 1)
    return list(held), list(held.values())


def whole_hop(block, near, far):
    held = {(0, 0): block, (NEAR, 0): near, (FAR, 0): far}
    held[NEAR | FAR, 0] = swap(near, "seq", FAR)
    return held


def half_hops(block, near, far):
    half = block.shape[0] // 2
    held = {(0, 0): block, (NEAR, 0): near, (FAR, 0): far}
    held[NEAR | FAR, 0] = swap(near[:half], "seq", FAR)
    held[NEAR | FAR, half] = swap(far[half:], "seq", NEAR)
    return held


def owners_blocks(blocks):
    return lax.all_to_all(blocks, "tensor", split_axis=0, concat_axis=0, tiled=True)


def shards(
    tokens,
    cache_keys,
    cache_values,
    joined_weight,
    output_weight,
    upward_weight,
    downward_weight,
    first_gain,
    second_gain,
    bias_table,
    bucket_index,
    cached_lengths,
    new_counts,
    extend_flags,
):
    ways = lax.axis_size("tensor")
    places = lax.axis_size("seq")
    mine = lax.axis_index("tensor")
    rows, features = tokens.shape
    cached = cache_keys.shape[0]
    heads = bias_table.shape[1]
    width = cache_keys.shape[1]
    trainer_rows = joined_weight.shape[0]
    hidden_units = upward_weight.shape[1] // ways
    attn_width = output_weight.shape[1]
    columns = attn_width + 2 * hidden_units
    span = bucket_index.shape[0] + 1

    joined_blocks = pl.pallas_call(
        joined_kernel,
        name="cut_joined",
        out_shape=[jax.ShapeDtypeStruct((trainer_rows, 3 * width), HALF)] * ways,
        in_specs=[HBM],
        out_specs=[VMEM] * ways,
        scratch_shapes=[
            pltpu.VMEM(joined_weight.shape, FULL),
            pltpu.SemaphoreType.DMA((1,)),
        ],
        compiler_params=params(VMEM_GRANT),
    )(joined_weight)
    forward = pl.pallas_call(
        forward_kernel,
        name="cut_forward",
        out_shape=jax.ShapeDtypeStruct((ways, trainer_rows, columns), HALF),
        in_specs=[ANY, HBM, HBM, HBM],
        out_specs=VMEM,
        scratch_shapes=[
            pltpu.VMEM(weight.shape, FULL)
            for weight in (output_weight, upward_weight, downward_weight)
        ]
        + [pltpu.SemaphoreType.DMA((3,))],
        compiler_params=params(VMEM_GRANT),
    )(joined_blocks[0], output_weight, upward_weight, downward_weight)
    own_joined, joined_blocks = joined_blocks[0], exchange(joined_blocks)

    normed, bias = pl.pallas_call(
        prepare_kernel,
        name="prepare",
        out_shape=[
            jax.ShapeDtypeStruct((rows, features), HALF),
            jax.ShapeDtypeStruct((heads, rows, cached + rows), FULL),
        ],
        in_specs=[ANY, HBM, HBM, HBM, VMEM, VMEM, VMEM, VMEM],
        out_specs=[VMEM, VMEM],
        scratch_shapes=[
            pltpu.SMEM((3,) + new_counts.shape, jnp.int32),
            pltpu.VMEM((1, span), jnp.int32),
            pltpu.SemaphoreType.DMA((3,)),
        ],
        compiler_params=params(VMEM_GRANT),
        cost_estimate=cost(10**8, 4 * 10**6),
    )(
        own_joined,
        cached_lengths,
        extend_flags,
        new_counts,
        tokens,
        first_gain.reshape(1, features),
        bias_table.T,
        bucket_index.reshape(1, span - 1),
    )

    if places == 8:
        lead = (places, ways, trainer_rows)
        joined = stack(joined_blocks, normed, forward)
        forward, joined = together(forward, joined)
        held = whole_hop(joined, *first_hops(joined))
        joined_pieces, joined_all = with_cores(held)
    else:
        lead = (features,)
        natural = [lax.select_n(mine ^ t, *joined_blocks) for t in range(ways)]
        joined_pieces, joined_all = [None], [natural_gather(jnp.stack(natural))]
    forward = owners_blocks(forward)

    attention = pl.pallas_call(
        functools.partial(attend_kernel, joined_pieces),
        name="attend",
        out_shape=jax.ShapeDtypeStruct((rows, width), HALF),
        in_specs=[VMEM, VMEM, VMEM, VMEM] + [ANY] * len(joined_all),
        out_specs=VMEM,
        scratch_shapes=[pltpu.VMEM(lead + (3 * width,), HALF), pltpu.SemaphoreType.DMA((8,))],
        compiler_params=params(VMEM_GRANT),
        cost_estimate=cost(ATTEND_COST, 6 * 10**6),
    )(normed, cache_keys, cache_values, bias, *joined_all)

    attended = [attention] + [swap(attention, "tensor", k) for k in range(1, ways)]
    if places == 8:
        forward_pieces, forward_all = with_cores(half_hops(forward, *first_hops(forward)))
    else:
        forward_pieces, forward_all = [None], [natural_gather(forward)]
    share = rows // ways
    own, *sends = pl.pallas_call(
        functools.partial(layer_kernel, forward_pieces, ways),
        name="layer",
        out_shape=[jax.ShapeDtypeStruct((share, features), FULL)]
        + [jax.ShapeDtypeStruct((share, features), HALF)] * (ways - 1),
        in_specs=[VMEM, VMEM] + [VMEM] * ways + [ANY] * len(forward_all),
        out_specs=[VMEM] * ways,
        scratch_shapes=[
            pltpu.VMEM(lead + (attn_width,), HALF),
            pltpu.VMEM(lead + (hidden_units,), HALF),
            pltpu.VMEM(lead + (hidden_units,), HALF),
            pltpu.VMEM((rows, attn_width), HALF),
            pltpu.VMEM((rows, features), FULL),
            pltpu.VMEM((rows, features), FULL),
            pltpu.SemaphoreType.DMA((3, len(forward_all))),
        ],
        compiler_params=params(VMEM_GRANT),
        cost_estimate=cost(2 * 10**9, 8 * 10**6),
    )(tokens, second_gain.reshape(1, features), *attended, *forward_all)

    total = own
    for k, send in enumerate(sends, 1):
        total = total + swap(send, "tensor", k).astype(FULL)
    return total.astype(HALF)


def solution(mesh):
    return jax.shard_map(
        shards,
        mesh=mesh,
        in_specs=(
            P("seq", None),
            P("seq", "tensor"),
            P("seq", "tensor"),
            P(("seq", "tensor"), None),
            P(("seq", "tensor"), None),
            P(("seq", "tensor"), None),
            P(("seq", "tensor"), None),
            P(),
            P(),
            P(None, "tensor"),
            P(),
            P(),
            P(),
            P(),
        ),
        out_specs=P(("seq", "tensor"), None),
        check_vma=False,
    )
```

time: 124 us -> 97.3 us (0.78)
  waiting for transfers between devices: 55.7 us -> 40.5 us
  starting transfers between devices: 40.3 us -> 29.4 us
  Pallas kernels: 14.7 us -> 21.7 us
  local copies, waits for them, and re-layouts: 10.2 us -> 3.32 us
  between operations: 1.59 us -> 0.28 us
    ppermute x36 -> x25, waiting for transfers between devices: 55.7 us -> 34.3 us  [swap(): return lax.ppermute(array, axis, [(i, i ^ mask) for i in range(size)])]
    ppermute x36 -> x25, starting transfers between devices: 40.3 us -> 24.3 us  [swap(): return lax.ppermute(array, axis, [(i, i ^ mask) for i in range(size)])]
    all_to_all x0 -> x1, waiting for transfers between devices: none -> 6.22 us  [owners_blocks(): lax.all_to_all(blocks, 'tensor', split_axis=0, concat_axis=0, tiled=True)]
    all_to_all x0 -> x1, starting transfers between devices: none -> 5.1 us  [owners_blocks(): lax.all_to_all(blocks, 'tensor', split_axis=0, concat_axis=0, tiled=True)]
    dynamic_slice x3 -> x0, local copies, waits for them, and re-layouts: 3.92 us -> none  [the longest x2 2.57 us: shards(): used = cached_lengths[place] * extend_flags[place]]
    pallas_call x3 -> x4, Pallas kernels: 12.2 us -> 15.8 us  [the longest x1 6.35 us: shards(): pl.pallas_call(functools.partial(layer_kernel, forward_pieces, ways), nam...]
    unnamed x35 -> x44, local copies, waits for them, and re-layouts: 6.24 us -> 3.26 us
    pallas_call x1, Pallas kernels: 1.95 us -> 4.13 us  [shards(): pl.pallas_call(prepare_kernel, name='prepare', out_shape=[jax.ShapeDtypeS...]
  transfers between devices with their start and end apart: 36 -> 26, of which waited for: 13 -> 12; matrix products, arithmetic and copies ran while one was open for 0% -> 0% of each run, Pallas kernels for 6% -> 12%
where the time goes in v2:
time: 97.3 us; the launch traced here: 96.8 us
  waiting for transfers between devices  40.5 us (42%)
  starting transfers between devices  29.4 us (30%)
  Pallas kernels  21.7 us (22%)
  local copies, waits for them, and re-layouts  3.32 us (3%)
  other arithmetic  1.67 us (2%)
    ppermute x25, waiting for transfers between devices, swap(): return lax.ppermute(array, axis, [(i, i ^ mask) for i in range(size)])  34.3 us
    ppermute x25, starting transfers between devices, swap(): return lax.ppermute(array, axis, [(i, i ^ mask) for i in range(size)])  24.3 us
    pallas_call x1, Pallas kernels, shards(): pl.pallas_call(functools.partial(layer_kernel, forward_pieces, ways), nam...  6.35 us
    all_to_all x1, waiting for transfers between devices, owners_blocks(): lax.all_to_all(blocks, 'tensor', split_axis=0, concat_axis=0, tiled=True)  6.22 us
    pallas_call x1, Pallas kernels, shards(): pl.pallas_call(functools.partial(attend_kernel, joined_pieces), name='att...  5.69 us
    all_to_all x1, starting transfers between devices, owners_blocks(): lax.all_to_all(blocks, 'tensor', split_axis=0, concat_axis=0, tiled=True)  5.1 us
    pallas_call x1, Pallas kernels, shards(): pl.pallas_call(prepare_kernel, name='prepare', out_shape=[jax.ShapeDtypeS...  4.13 us
    unnamed x44, local copies, waits for them, and re-layouts  3.26 us
  transfers between devices with their start and end apart: 26, of which 12 were waited for; matrix products, arithmetic and copies ran while one was open for 0% of the time, Pallas kernels for 12%

profile of v2, /device:TPU:0, one launch (start us, length us, event | category | flops | bytes accessed | tf_op | source)
XLA Modules:
  0.0 96.8 jit_solution(16376469425684354907)
XLA Ops:
  0.0 1.7 %cut_joined.1 = (bf16[32,768]{1,0:T(8,128)(2,1)}, bf16[32,768]{1,0:T(8,128)(2,1)}, bf16[32,768]{1,0:T(8,128)(2,1)}, bf16[32,768]{1,0:T(8,128)(2,1)}) custom-call(f32[32,3072]{1,0:T(8,128)} %joined_source.1), custom_call_target="tpu_custom_call" | custom-call | tf_op jit(solution)/shard_map/cut_joined/pallas_call | solution.py:297
  1.7 3.1 %collective-permute-start = (bf16[32,768]{1,0:T(8,128)(2,1)}, bf16[32,768]{1,0:T(8,128)(2,1)S(1)}, u32[]{:S(2)}, u32[]{:S(2)}) collective-permute-start(bf16[32,768]{1,0:T(8,128)(2,1)} %get-tuple-element.24), channel_id=1, source_target_pairs={{0,1},{1,0},{2,3},{3,2},{4,5},{5,4},{6,7},{7,6},{8,9},{9,8},{10,11... | collective-permute-start | bytes 147464 | tf_op jit(solution)/shard_map/ppermute | solution.py:33
  4.8 2.6 %collective-permute-start.1 = (bf16[32,768]{1,0:T(8,128)(2,1)}, bf16[32,768]{1,0:T(8,128)(2,1)S(1)}, u32[]{:S(2)}, u32[]{:S(2)}) collective-permute-start(bf16[32,768]{1,0:T(8,128)(2,1)} %get-tuple-element.25), channel_id=1, source_target_pairs={{0,2},{1,3},{2,0},{3,1},{4,6},{5,7},{6,4},{7,5},{8,10},{9,11},{10,... | collective-permute-start | bytes 147464 | tf_op jit(solution)/shard_map/ppermute | solution.py:33
  7.4 2.2 %cut_forward.1.refs_5_ = bf16[4,32,3072]{2,1,0:T(8,128)(2,1)} custom-call(bf16[32,768]{1,0:T(8,128)(2,1)} %get-tuple-element.21.after.refs_0_, f32[32,1024]{1,0:T(8,128)} %refs_1_.1, f32[32,4096]{1,0:T(8,128)} %refs_2_.1, f32[32,4096]{1,0:T(8,128)} %refs_3_.1), custom_call_target="tpu_custom_call" | custom-call | tf_op jit(solution)/shard_map/cut_forward/pallas_call | solution.py:309
  9.6 4.1 %prepare.1 = (bf16[256,1024]{1,0:T(8,128)(2,1)}, f32[4,256,512]{2,1,0:T(8,128)}) custom-call(bf16[32,768]{1,0:T(8,128)(2,1)} %get-tuple-element.21.after.refs_0_, s32[8]{0:T(128)} %lengths.1, s32[8]{0:T(128)} %flags.1, s32[8]{0:T(128)} %counts.1, bf16[256,1024]{1,0:T(8,128)(2,1)} %tokens.3, f32[1,1024]{1,0:T(1,128)} %bitcast.4, f32[4,32]{1,0:T(4,128)} %bitcast.6, ...), custom_call_target="tpu_custom_call" | custom-call | flops 100000000 | bytes 4000000 | tf_op jit(solution)/shard_map/prepare/pallas_call | solution.py:324
  14.4 1.6 %stack.1.refs_0_ = bf16[4,32,768]{2,1,0:T(8,128)(2,1)} custom-call(bf16[32,768]{1,0:T(8,128)(2,1)} %get-tuple-element.21.after.refs_0_, bf16[32,768]{1,0:T(8,128)(2,1)} %copy-done.3, bf16[32,768]{1,0:T(8,128)(2,1)} %copy-done.4, bf16[32,768]{1,0:T(8,128)(2,1)} %copy-done.5, bf16[256,1024]{1,0:T(8,128)(2,1)} %get-tuple-element.22.refs_4_.normed, ...), custom_call_target="tpu_custom_call" | custom-call | tf_op jit(solution)/shard_map/stack/pallas_call | solution.py:132
  16.0 5.1 %all-to-all-start = ((bf16[4,32,3072]{2,1,0:T(8,128)(2,1)}), bf16[4,32,3072]{2,1,0:T(8,128)(2,1)S(1)}, u32[]{:S(2)}, u32[]{:S(2)}) async-start(bf16[4,32,3072]{2,1,0:T(8,128)(2,1)} %cut_forward.1.refs_5_), calls=%async_computation | async-start | bytes 1572864 | tf_op jit(solution)/shard_map/all_to_all | solution.py:265
  21.1 1.5 %collective-permute-start.4 = (bf16[4,32,768]{2,1,0:T(8,128)(2,1)}, bf16[4,32,768]{2,1,0:T(8,128)(2,1)S(1)}, u32[]{:S(2)}, u32[]{:S(2)}) collective-permute-start(bf16[4,32,768]{2,1,0:T(8,128)(2,1)} %stack.1.refs_0_), channel_id=1, source_target_pairs={{0,8},{4,12},{8,0},{12,4},{16,24},{20,28},{24,16},{28,20},{1,9},{5... | collective-permute-start | bytes 589832 | tf_op jit(solution)/shard_map/ppermute | solution.py:33
  22.6 1.5 %collective-permute-start.3 = (bf16[4,32,768]{2,1,0:T(8,128)(2,1)}, bf16[4,32,768]{2,1,0:T(8,128)(2,1)S(1)}, u32[]{:S(2)}, u32[]{:S(2)}) collective-permute-start(bf16[4,32,768]{2,1,0:T(8,128)(2,1)} %stack.1.refs_0_), channel_id=1, source_target_pairs={{0,16},{4,20},{8,24},{12,28},{16,0},{20,4},{24,8},{28,12},{1,17},{... | collective-permute-start | bytes 589832 | tf_op jit(solution)/shard_map/ppermute | solution.py:33
  24.1 2.9 %collective-permute-done.4.refs_2_ = bf16[4,32,768]{2,1,0:T(8,128)(2,1)S(1)} collective-permute-done((bf16[4,32,768]{2,1,0:T(8,128)(2,1)}, bf16[4,32,768]{2,1,0:T(8,128)(2,1)S(1)}, u32[]{:S(2)}, u32[]{:S(2)}) %collective-permute-start.4) | collective-permute-done | bytes 196640 | tf_op jit(solution)/shard_map/ppermute | solution.py:33
  27.0 1.5 %collective-permute-done.3.refs_1_ = bf16[4,32,768]{2,1,0:T(8,128)(2,1)S(1)} collective-permute-done((bf16[4,32,768]{2,1,0:T(8,128)(2,1)}, bf16[4,32,768]{2,1,0:T(8,128)(2,1)S(1)}, u32[]{:S(2)}, u32[]{:S(2)}) %collective-permute-start.3) | collective-permute-done | bytes 196640 | tf_op jit(solution)/shard_map/ppermute | solution.py:33
  29.5 4.6 %collective-permute-done.5.refs_3_ = bf16[4,32,768]{2,1,0:T(8,128)(2,1)S(1)} collective-permute-done((bf16[4,32,768]{2,1,0:T(8,128)(2,1)S(1)}, bf16[4,32,768]{2,1,0:T(8,128)(2,1)S(1)}, u32[]{:S(2)}, u32[]{:S(2)}) %collective-permute-start.5) | collective-permute-done | bytes 196640 | tf_op jit(solution)/shard_map/ppermute | solution.py:33
  34.2 6.2 %all-to-all-done.refs_4_ = bf16[4,32,3072]{2,1,0:T(8,128)(2,1)S(1)} async-done(((bf16[4,32,3072]{2,1,0:T(8,128)(2,1)}), bf16[4,32,3072]{2,1,0:T(8,128)(2,1)S(1)}, u32[]{:S(2)}, u32[]{:S(2)}) %all-to-all-start) | async-done | bytes 786464 | tf_op jit(solution)/shard_map/all_to_all | solution.py:265
  40.4 1.5 %collective-permute-start.14 = (bf16[4,32,3072]{2,1,0:T(8,128)(2,1)S(1)}, bf16[4,32,3072]{2,1,0:T(8,128)(2,1)S(1)}, u32[]{:S(2)}, u32[]{:S(2)}) collective-permute-start(bf16[4,32,3072]{2,1,0:T(8,128)(2,1)S(1)} %all-to-all-done.refs_4_), channel_id=1, source_target_pairs={{0,8},{4,12},{8,0},{12,4},{16,24},{20,28},{24,16},{28,20},{1,9},{5... | collective-permute-start | bytes 2359304 | tf_op jit(solution)/shard_map/ppermute | solution.py:33
  41.9 1.5 %collective-permute-start.13 = (bf16[4,32,3072]{2,1,0:T(8,128)(2,1)S(1)}, bf16[4,32,3072]{2,1,0:T(8,128)(2,1)S(1)}, u32[]{:S(2)}, u32[]{:S(2)}) collective-permute-start(bf16[4,32,3072]{2,1,0:T(8,128)(2,1)S(1)} %all-to-all-done.refs_4_), channel_id=1, source_target_pairs={{0,16},{4,20},{8,24},{12,28},{16,0},{20,4},{24,8},{28,12},{1,17},{... | collective-permute-start | bytes 2359304 | tf_op jit(solution)/shard_map/ppermute | solution.py:33
  44.2 5.7 %attend.1.refs_0_ = bf16[256,256]{1,0:T(8,128)(2,1)} custom-call(bf16[256,1024]{1,0:T(8,128)(2,1)} %get-tuple-element.22.refs_4_.normed, bf16[256,256]{1,0:T(8,128)(2,1)} %old_keys.1, bf16[256,256]{1,0:T(8,128)(2,1)} %old_values.1, f32[4,256,512]{2,1,0:T(8,128)} %get-tuple-element.23.bias, bf16[4,32,768]{2,1,0:T(8,128)(2,1)} %stack.1.refs_0_, ...), custom_call_target="tpu_custom_call" | custom-call | flops 20000000000 | bytes 6000000 | tf_op jit(solution)/shard_map/attend/pallas_call | solution.py:363
  49.9 1.5 %collective-permute-start.12 = (bf16[256,256]{1,0:T(8,128)(2,1)}, bf16[256,256]{1,0:T(8,128)(2,1)S(1)}, u32[]{:S(2)}, u32[]{:S(2)}) collective-permute-start(bf16[256,256]{1,0:T(8,128)(2,1)} %attend.1.refs_0_), channel_id=1, source_target_pairs={{0,3},{1,2},{2,1},{3,0},{4,7},{5,6},{6,5},{7,4},{8,11},{9,10},{10,... | collective-permute-start | bytes 393224 | tf_op jit(solution)/shard_map/ppermute | solution.py:33
  51.4 2.9 %collective-permute-start.10 = (bf16[256,256]{1,0:T(8,128)(2,1)}, bf16[256,256]{1,0:T(8,128)(2,1)S(1)}, u32[]{:S(2)}, u32[]{:S(2)}) collective-permute-start(bf16[256,256]{1,0:T(8,128)(2,1)} %attend.1.refs_0_), channel_id=1, source_target_pairs={{0,1},{1,0},{2,3},{3,2},{4,5},{5,4},{6,7},{7,6},{8,9},{9,8},{10,11... | collective-permute-start | bytes 393224 | tf_op jit(solution)/shard_map/ppermute | solution.py:33
  54.3 4.6 %collective-permute-done.14.refs_6_ = bf16[4,32,3072]{2,1,0:T(8,128)(2,1)S(1)} collective-permute-done((bf16[4,32,3072]{2,1,0:T(8,128)(2,1)S(1)}, bf16[4,32,3072]{2,1,0:T(8,128)(2,1)S(1)}, u32[]{:S(2)}, u32[]{:S(2)}) %collective-permute-start.14) | collective-permute-done | bytes 786464 | tf_op jit(solution)/shard_map/ppermute | solution.py:33
  58.9 1.2 %collective-permute-done.13.refs_5_ = bf16[4,32,3072]{2,1,0:T(8,128)(2,1)S(1)} collective-permute-done((bf16[4,32,3072]{2,1,0:T(8,128)(2,1)S(1)}, bf16[4,32,3072]{2,1,0:T(8,128)(2,1)S(1)}, u32[]{:S(2)}, u32[]{:S(2)}) %collective-permute-start.13) | collective-permute-done | bytes 786464 | tf_op jit(solution)/shard_map/ppermute | solution.py:33
  60.2 1.6 %collective-permute-start.16 = (bf16[2,32,3072]{2,1,0:T(8,128)(2,1)S(1)}, bf16[2,32,3072]{2,1,0:T(8,128)(2,1)S(1)}, u32[]{:S(2)}, u32[]{:S(2)}) collective-permute-start(bf16[2,32,3072]{2,1,0:T(8,128)(2,1)S(1)} %slice.7), channel_id=1, source_target_pairs={{0,16},{4,20},{8,24},{12,28},{16,0},{20,4},{24,8},{28,12},{1,17},{... | collective-permute-start | bytes 1179656 | tf_op jit(solution)/shard_map/ppermute | solution.py:33
  62.8 7.7 %collective-permute-done.16.refs_8_ = bf16[2,32,3072]{2,1,0:T(8,128)(2,1)S(1)} collective-permute-done((bf16[2,32,3072]{2,1,0:T(8,128)(2,1)S(1)}, bf16[2,32,3072]{2,1,0:T(8,128)(2,1)S(1)}, u32[]{:S(2)}, u32[]{:S(2)}) %collective-permute-start.16) | collective-permute-done | bytes 393248 | tf_op jit(solution)/shard_map/ppermute | solution.py:33
  70.6 1.2 %collective-permute-done.15.refs_7_ = bf16[2,32,3072]{2,1,0:T(8,128)(2,1)S(1)} collective-permute-done((bf16[2,32,3072]{2,1,0:T(8,128)(2,1)S(1)}, bf16[2,32,3072]{2,1,0:T(8,128)(2,1)S(1)}, u32[]{:S(2)}, u32[]{:S(2)}) %collective-permute-start.15) | collective-permute-done | bytes 393248 | tf_op jit(solution)/shard_map/ppermute | solution.py:33
  72.3 1.2 %collective-permute-done.20.refs_12_ = bf16[2,32,3072]{2,1,0:T(8,128)(2,1)S(1)} collective-permute-done((bf16[2,32,3072]{2,1,0:T(8,128)(2,1)S(1)}, bf16[2,32,3072]{2,1,0:T(8,128)(2,1)S(1)}, u32[]{:S(2)}, u32[]{:S(2)}) %collective-permute-start.20) | collective-permute-done | bytes 393248 | tf_op jit(solution)/shard_map/ppermute | solution.py:33
  73.6 0.7 copy-done.12
  74.6 0.9 copy-done.8
  75.5 6.3 %layer.1 = (f32[64,1024]{1,0:T(8,128)}, bf16[64,1024]{1,0:T(8,128)(2,1)}, bf16[64,1024]{1,0:T(8,128)(2,1)}, bf16[64,1024]{1,0:T(8,128)(2,1)}) custom-call(bf16[256,1024]{1,0:T(8,128)(2,1)} %tokens.3, f32[1,1024]{1,0:T(1,128)} %bitcast.7, bf16[256,256]{1,0:T(8,128)(2,1)} %attend.1.refs_0_, bf16[256,256]{1,0:T(8,128)(2,1)} %copy-done.21, ...), custom_call_target="tpu_custom_call" | custom-call | flops 2000000000 | bytes 8000000 | tf_op jit(solution)/shard_map/layer/pallas_call | solution.py:380
  81.9 0.7 collective-permute-start.23
  82.6 3.7 %collective-permute-start.24 = (bf16[64,1024]{1,0:T(8,128)(2,1)}, bf16[64,1024]{1,0:T(8,128)(2,1)S(1)}, u32[]{:S(2)}, u32[]{:S(2)}) collective-permute-start(bf16[64,1024]{1,0:T(8,128)(2,1)} %get-tuple-element.36), channel_id=1, source_target_pairs={{0,3},{1,2},{2,1},{3,0},{4,7},{5,6},{6,5},{7,4},{8,11},{9,10},{10,... | collective-permute-start | bytes 393224 | tf_op jit(solution)/shard_map/ppermute | solution.py:33
  86.3 2.6 %collective-permute-done.22 = bf16[64,1024]{1,0:T(8,128)(2,1)S(1)} collective-permute-done((bf16[64,1024]{1,0:T(8,128)(2,1)}, bf16[64,1024]{1,0:T(8,128)(2,1)S(1)}, u32[]{:S(2)}, u32[]{:S(2)}) %collective-permute-start.22) | collective-permute-done | bytes 131104 | tf_op jit(solution)/shard_map/ppermute | solution.py:33
  88.9 6.2 %collective-permute-done.23 = bf16[64,1024]{1,0:T(8,128)(2,1)S(1)} collective-permute-done((bf16[64,1024]{1,0:T(8,128)(2,1)}, bf16[64,1024]{1,0:T(8,128)(2,1)S(1)}, u32[]{:S(2)}, u32[]{:S(2)}) %collective-permute-start.23) | collective-permute-done | bytes 131104 | tf_op jit(solution)/shard_map/ppermute | solution.py:33
  95.1 1.7 %add_convert_fusion = bf16[64,1024]{1,0:T(8,128)(2,1)} fusion(bf16[64,1024]{1,0:T(8,128)(2,1)S(1)} %collective-permute-done.24, bf16[64,1024]{1,0:T(8,128)(2,1)S(1)} %collective-permute-done.23, f32[64,1024]{1,0:T(8,128)} %get-tuple-element.33, bf16[64,1024]{1,0:T(8,128)(2,1)S(1)} %collective-permute-done.22), kind=kLoop, calls=%fused_computation | loop fusion | flops 458752 | bytes 786432 | tf_op jit(solution)/shard_map/convert_element_type | solution.py:403
  (73 shorter events, 4.3 us)
Async XLA Ops:
  1.7 12.1 %collective-permute-start = (bf16[32,768]{1,0:T(8,128)(2,1)}, bf16[32,768]{1,0:T(8,128)(2,1)S(1)}, u32[]{:S(2)}, u32[]{:S(2)}) collective-permute-start(bf16[32,768]{1,0:T(8,128)(2,1)} %get-tuple-element.24), channel_id=1, source_target_pairs={{0,1},{1,0},{2,3},{3,2},{4,5},{5,4},{6,7},{7,6},{8,9},{9,8},{10,11... | collective-permute-start | bytes 147464 | tf_op jit(solution)/shard_map/ppermute | solution.py:33
  4.8 9.0 %collective-permute-start.1 = (bf16[32,768]{1,0:T(8,128)(2,1)}, bf16[32,768]{1,0:T(8,128)(2,1)S(1)}, u32[]{:S(2)}, u32[]{:S(2)}) collective-permute-start(bf16[32,768]{1,0:T(8,128)(2,1)} %get-tuple-element.25), channel_id=1, source_target_pairs={{0,2},{1,3},{2,0},{3,1},{4,6},{5,7},{6,4},{7,5},{8,10},{9,11},{10,... | collective-permute-start | bytes 147464 | tf_op jit(solution)/shard_map/ppermute | solution.py:33
  7.4 6.4 %collective-permute-start.2 = (bf16[32,768]{1,0:T(8,128)(2,1)}, bf16[32,768]{1,0:T(8,128)(2,1)S(1)}, u32[]{:S(2)}, u32[]{:S(2)}) collective-permute-start(bf16[32,768]{1,0:T(8,128)(2,1)} %get-tuple-element.26), channel_id=1, source_target_pairs={{0,3},{1,2},{2,1},{3,0},{4,7},{5,6},{6,5},{7,4},{8,11},{9,10},{10,... | collective-permute-start | bytes 147464 | tf_op jit(solution)/shard_map/ppermute | solution.py:33
  16.0 24.4 %all-to-all-start = ((bf16[4,32,3072]{2,1,0:T(8,128)(2,1)}), bf16[4,32,3072]{2,1,0:T(8,128)(2,1)S(1)}, u32[]{:S(2)}, u32[]{:S(2)}) async-start(bf16[4,32,3072]{2,1,0:T(8,128)(2,1)} %cut_forward.1.refs_5_), calls=%async_computation | async-start | bytes 1572864 | tf_op jit(solution)/shard_map/all_to_all | solution.py:265
  21.1 5.9 %collective-permute-start.4 = (bf16[4,32,768]{2,1,0:T(8,128)(2,1)}, bf16[4,32,768]{2,1,0:T(8,128)(2,1)S(1)}, u32[]{:S(2)}, u32[]{:S(2)}) collective-permute-start(bf16[4,32,768]{2,1,0:T(8,128)(2,1)} %stack.1.refs_0_), channel_id=1, source_target_pairs={{0,8},{4,12},{8,0},{12,4},{16,24},{20,28},{24,16},{28,20},{1,9},{5... | collective-permute-start | bytes 589832 | tf_op jit(solution)/shard_map/ppermute | solution.py:33
  22.6 5.9 %collective-permute-start.3 = (bf16[4,32,768]{2,1,0:T(8,128)(2,1)}, bf16[4,32,768]{2,1,0:T(8,128)(2,1)S(1)}, u32[]{:S(2)}, u32[]{:S(2)}) collective-permute-start(bf16[4,32,768]{2,1,0:T(8,128)(2,1)} %stack.1.refs_0_), channel_id=1, source_target_pairs={{0,16},{4,20},{8,24},{12,28},{16,0},{20,4},{24,8},{28,12},{1,17},{... | collective-permute-start | bytes 589832 | tf_op jit(solution)/shard_map/ppermute | solution.py:33
  27.0 16.4 %copy-start.13 = (bf16[4,32,768]{2,1,0:T(8,128)(2,1)}, bf16[4,32,768]{2,1,0:T(8,128)(2,1)S(1)}, u32[]{:S(2)}) copy-start(bf16[4,32,768]{2,1,0:T(8,128)(2,1)S(1)} %collective-permute-done.4.refs_2_) | copy-start | bytes 589828
  28.5 15.0 %copy-start.14 = (bf16[4,32,768]{2,1,0:T(8,128)(2,1)}, bf16[4,32,768]{2,1,0:T(8,128)(2,1)S(1)}, u32[]{:S(2)}) copy-start(bf16[4,32,768]{2,1,0:T(8,128)(2,1)S(1)} %collective-permute-done.3.refs_1_) | copy-start | bytes 589828
  28.5 5.7 %collective-permute-start.5 = (bf16[4,32,768]{2,1,0:T(8,128)(2,1)S(1)}, bf16[4,32,768]{2,1,0:T(8,128)(2,1)S(1)}, u32[]{:S(2)}, u32[]{:S(2)}) collective-permute-start(bf16[4,32,768]{2,1,0:T(8,128)(2,1)S(1)} %collective-permute-done.3.refs_1_), channel_id=1, source_target_pairs={{0,8},{4,12},{8,0},{12,4},{16,24},{20,28},{24,16},{28,20},{1,9},{5... | collective-permute-start | bytes 589832 | tf_op jit(solution)/shard_map/ppermute | solution.py:33
  29.0 12.9 %collective-permute-start.6 = (bf16[4,32,768]{2,1,0:T(8,128)(2,1)}, bf16[4,32,768]{2,1,0:T(8,128)(2,1)S(1)}, u32[]{:S(2)}, u32[]{:S(2)}) collective-permute-start(bf16[4,32,768]{2,1,0:T(8,128)(2,1)} %stack.1.refs_0_), channel_id=1, source_target_pairs={{0,4},{4,0},{8,12},{12,8},{16,20},{20,16},{24,28},{28,24},{1,5},{5... | collective-permute-start | bytes 589832 | tf_op jit(solution)/shard_map/ppermute | solution.py:33
  29.0 14.4 %collective-permute-start.7 = (bf16[4,32,768]{2,1,0:T(8,128)(2,1)S(1)}, bf16[4,32,768]{2,1,0:T(8,128)(2,1)S(1)}, u32[]{:S(2)}, u32[]{:S(2)}) collective-permute-start(bf16[4,32,768]{2,1,0:T(8,128)(2,1)S(1)} %collective-permute-done.3.refs_1_), channel_id=1, source_target_pairs={{0,4},{4,0},{8,12},{12,8},{16,20},{20,16},{24,28},{28,24},{1,5},{5... | collective-permute-start | bytes 589832 | tf_op jit(solution)/shard_map/ppermute | solution.py:33
  29.5 13.9 %collective-permute-start.8 = (bf16[4,32,768]{2,1,0:T(8,128)(2,1)S(1)}, bf16[4,32,768]{2,1,0:T(8,128)(2,1)S(1)}, u32[]{:S(2)}, u32[]{:S(2)}) collective-permute-start(bf16[4,32,768]{2,1,0:T(8,128)(2,1)S(1)} %collective-permute-done.4.refs_2_), channel_id=1, source_target_pairs={{0,4},{4,0},{8,12},{12,8},{16,20},{20,16},{24,28},{28,24},{1,5},{5... | collective-permute-start | bytes 589832 | tf_op jit(solution)/shard_map/ppermute | solution.py:33
  34.2 9.3 %collective-permute-start.9 = (bf16[4,32,768]{2,1,0:T(8,128)(2,1)S(1)}, bf16[4,32,768]{2,1,0:T(8,128)(2,1)}, u32[]{:S(2)}, u32[]{:S(2)}) collective-permute-start(bf16[4,32,768]{2,1,0:T(8,128)(2,1)S(1)} %collective-permute-done.5.refs_3_), channel_id=1, source_target_pairs={{0,4},{4,0},{8,12},{12,8},{16,20},{20,16},{24,28},{28,24},{1,5},{5... | collective-permute-start | bytes 589832 | tf_op jit(solution)/shard_map/ppermute | solution.py:33
  40.4 18.5 %copy-start = (bf16[4,32,3072]{2,1,0:T(8,128)(2,1)}, bf16[4,32,3072]{2,1,0:T(8,128)(2,1)S(1)}, u32[]{:S(2)}) copy-start(bf16[4,32,3072]{2,1,0:T(8,128)(2,1)S(1)} %all-to-all-done.refs_4_) | copy-start | bytes 2359300
  40.4 18.5 %collective-permute-start.14 = (bf16[4,32,3072]{2,1,0:T(8,128)(2,1)S(1)}, bf16[4,32,3072]{2,1,0:T(8,128)(2,1)S(1)}, u32[]{:S(2)}, u32[]{:S(2)}) collective-permute-start(bf16[4,32,3072]{2,1,0:T(8,128)(2,1)S(1)} %all-to-all-done.refs_4_), channel_id=1, source_target_pairs={{0,8},{4,12},{8,0},{12,4},{16,24},{20,28},{24,16},{28,20},{1,9},{5... | collective-permute-start | bytes 2359304 | tf_op jit(solution)/shard_map/ppermute | solution.py:33
  41.9 18.2 %collective-permute-start.13 = (bf16[4,32,3072]{2,1,0:T(8,128)(2,1)S(1)}, bf16[4,32,3072]{2,1,0:T(8,128)(2,1)S(1)}, u32[]{:S(2)}, u32[]{:S(2)}) collective-permute-start(bf16[4,32,3072]{2,1,0:T(8,128)(2,1)S(1)} %all-to-all-done.refs_4_), channel_id=1, source_target_pairs={{0,16},{4,20},{8,24},{12,28},{16,0},{20,4},{24,8},{28,12},{1,17},{... | collective-permute-start | bytes 2359304 | tf_op jit(solution)/shard_map/ppermute | solution.py:33
  49.9 11.9 %collective-permute-start.12 = (bf16[256,256]{1,0:T(8,128)(2,1)}, bf16[256,256]{1,0:T(8,128)(2,1)S(1)}, u32[]{:S(2)}, u32[]{:S(2)}) collective-permute-start(bf16[256,256]{1,0:T(8,128)(2,1)} %attend.1.refs_0_), channel_id=1, source_target_pairs={{0,3},{1,2},{2,1},{3,0},{4,7},{5,6},{6,5},{7,4},{8,11},{9,10},{10,... | collective-permute-start | bytes 393224 | tf_op jit(solution)/shard_map/ppermute | solution.py:33
  51.4 10.9 %collective-permute-start.11 = (bf16[256,256]{1,0:T(8,128)(2,1)}, bf16[256,256]{1,0:T(8,128)(2,1)S(1)}, u32[]{:S(2)}, u32[]{:S(2)}) collective-permute-start(bf16[256,256]{1,0:T(8,128)(2,1)} %attend.1.refs_0_), channel_id=1, source_target_pairs={{0,2},{1,3},{2,0},{3,1},{4,6},{5,7},{6,4},{7,5},{8,10},{9,11},{10,... | collective-permute-start | bytes 393224 | tf_op jit(solution)/shard_map/ppermute | solution.py:33
  51.4 10.9 %collective-permute-start.10 = (bf16[256,256]{1,0:T(8,128)(2,1)}, bf16[256,256]{1,0:T(8,128)(2,1)S(1)}, u32[]{:S(2)}, u32[]{:S(2)}) collective-permute-start(bf16[256,256]{1,0:T(8,128)(2,1)} %attend.1.refs_0_), channel_id=1, source_target_pairs={{0,1},{1,0},{2,3},{3,2},{4,5},{5,4},{6,7},{7,6},{8,9},{9,8},{10,11... | collective-permute-start | bytes 393224 | tf_op jit(solution)/shard_map/ppermute | solution.py:33
  58.9 16.6 %copy-start.1 = (bf16[4,32,3072]{2,1,0:T(8,128)(2,1)}, bf16[4,32,3072]{2,1,0:T(8,128)(2,1)S(1)}, u32[]{:S(2)}) copy-start(bf16[4,32,3072]{2,1,0:T(8,128)(2,1)S(1)} %collective-permute-done.14.refs_6_) | copy-start | bytes 2359300
  58.9 12.9 %collective-permute-start.17 = (bf16[4,32,3072]{2,1,0:T(8,128)(2,1)S(1)}, bf16[4,32,3072]{2,1,0:T(8,128)(2,1)S(1)}, u32[]{:S(2)}, u32[]{:S(2)}) collective-permute-start(bf16[4,32,3072]{2,1,0:T(8,128)(2,1)S(1)} %all-to-all-done.refs_4_), channel_id=1, source_target_pairs={{0,4},{4,0},{8,12},{12,8},{16,20},{20,16},{24,28},{28,24},{1,5},{5... | collective-permute-start | bytes 2359304 | tf_op jit(solution)/shard_map/ppermute | solution.py:33
  60.1 15.4 %copy-start.2 = (bf16[4,32,3072]{2,1,0:T(8,128)(2,1)}, bf16[4,32,3072]{2,1,0:T(8,128)(2,1)S(1)}, u32[]{:S(2)}) copy-start(bf16[4,32,3072]{2,1,0:T(8,128)(2,1)S(1)} %collective-permute-done.13.refs_5_) | copy-start | bytes 2359300
  60.2 10.4 %collective-permute-start.16 = (bf16[2,32,3072]{2,1,0:T(8,128)(2,1)S(1)}, bf16[2,32,3072]{2,1,0:T(8,128)(2,1)S(1)}, u32[]{:S(2)}, u32[]{:S(2)}) collective-permute-start(bf16[2,32,3072]{2,1,0:T(8,128)(2,1)S(1)} %slice.7), channel_id=1, source_target_pairs={{0,16},{4,20},{8,24},{12,28},{16,0},{20,4},{24,8},{28,12},{1,17},{... | collective-permute-start | bytes 1179656 | tf_op jit(solution)/shard_map/ppermute | solution.py:33
  61.8 13.7 %copy-start.19 = (bf16[256,256]{1,0:T(8,128)(2,1)}, bf16[256,256]{1,0:T(8,128)(2,1)S(1)}, u32[]{:S(2)}) copy-start(bf16[256,256]{1,0:T(8,128)(2,1)S(1)} %collective-permute-done.12.refs_3_) | copy-start | bytes 393220
  61.8 10.0 %collective-permute-start.15 = (bf16[2,32,3072]{2,1,0:T(8,128)(2,1)S(1)}, bf16[2,32,3072]{2,1,0:T(8,128)(2,1)S(1)}, u32[]{:S(2)}, u32[]{:S(2)}) collective-permute-start(bf16[2,32,3072]{2,1,0:T(8,128)(2,1)S(1)} %slice.6), channel_id=1, source_target_pairs={{0,8},{4,12},{8,0},{12,4},{16,24},{20,28},{24,16},{28,20},{1,9},{5... | collective-permute-start | bytes 1179656 | tf_op jit(solution)/shard_map/ppermute | solution.py:33
  62.3 11.2 %collective-permute-start.18 = (bf16[4,32,3072]{2,1,0:T(8,128)(2,1)S(1)}, bf16[4,32,3072]{2,1,0:T(8,128)(2,1)S(1)}, u32[]{:S(2)}, u32[]{:S(2)}) collective-permute-start(bf16[4,32,3072]{2,1,0:T(8,128)(2,1)S(1)} %collective-permute-done.13.refs_5_), channel_id=1, source_target_pairs={{0,4},{4,0},{8,12},{12,8},{16,20},{20,16},{24,28},{28,24},{1,5},{5... | collective-permute-start | bytes 2359304 | tf_op jit(solution)/shard_map/ppermute | solution.py:33
  62.3 11.2 %collective-permute-start.19 = (bf16[4,32,3072]{2,1,0:T(8,128)(2,1)S(1)}, bf16[4,32,3072]{2,1,0:T(8,128)(2,1)S(1)}, u32[]{:S(2)}, u32[]{:S(2)}) collective-permute-start(bf16[4,32,3072]{2,1,0:T(8,128)(2,1)S(1)} %collective-permute-done.14.refs_6_), channel_id=1, source_target_pairs={{0,4},{4,0},{8,12},{12,8},{16,20},{20,16},{24,28},{28,24},{1,5},{5... | collective-permute-start | bytes 2359304 | tf_op jit(solution)/shard_map/ppermute | solution.py:33
  70.6 1.7 %collective-permute-start.21 = (bf16[2,32,3072]{2,1,0:T(8,128)(2,1)S(1)}, bf16[2,32,3072]{2,1,0:T(8,128)(2,1)S(1)}, u32[]{:S(2)}, u32[]{:S(2)}) collective-permute-start(bf16[2,32,3072]{2,1,0:T(8,128)(2,1)S(1)} %collective-permute-done.16.refs_8_), channel_id=1, source_target_pairs={{0,4},{4,0},{8,12},{12,8},{16,20},{20,16},{24,28},{28,24},{1,5},{5... | collective-permute-start | bytes 1179656 | tf_op jit(solution)/shard_map/ppermute | solution.py:33
  71.8 1.7 %collective-permute-start.20 = (bf16[2,32,3072]{2,1,0:T(8,128)(2,1)S(1)}, bf16[2,32,3072]{2,1,0:T(8,128)(2,1)S(1)}, u32[]{:S(2)}, u32[]{:S(2)}) collective-permute-start(bf16[2,32,3072]{2,1,0:T(8,128)(2,1)S(1)} %collective-permute-done.15.refs_7_), channel_id=1, source_target_pairs={{0,4},{4,0},{8,12},{12,8},{16,20},{20,16},{24,28},{28,24},{1,5},{5... | collective-permute-start | bytes 1179656 | tf_op jit(solution)/shard_map/ppermute | solution.py:33
  81.9 7.0 %collective-permute-start.22 = (bf16[64,1024]{1,0:T(8,128)(2,1)}, bf16[64,1024]{1,0:T(8,128)(2,1)S(1)}, u32[]{:S(2)}, u32[]{:S(2)}) collective-permute-start(bf16[64,1024]{1,0:T(8,128)(2,1)} %get-tuple-element.34), channel_id=1, source_target_pairs={{0,1},{1,0},{2,3},{3,2},{4,5},{5,4},{6,7},{7,6},{8,9},{9,8},{10,11... | collective-permute-start | bytes 393224 | tf_op jit(solution)/shard_map/ppermute | solution.py:33
  81.9 13.2 %collective-permute-start.23 = (bf16[64,1024]{1,0:T(8,128)(2,1)}, bf16[64,1024]{1,0:T(8,128)(2,1)S(1)}, u32[]{:S(2)}, u32[]{:S(2)}) collective-permute-start(bf16[64,1024]{1,0:T(8,128)(2,1)} %get-tuple-element.35), channel_id=1, source_target_pairs={{0,2},{1,3},{2,0},{3,1},{4,6},{5,7},{6,4},{7,5},{8,10},{9,11},{10,... | collective-permute-start | bytes 393224 | tf_op jit(solution)/shard_map/ppermute | solution.py:33
  82.6 12.5 %collective-permute-start.24 = (bf16[64,1024]{1,0:T(8,128)(2,1)}, bf16[64,1024]{1,0:T(8,128)(2,1)S(1)}, u32[]{:S(2)}, u32[]{:S(2)}) collective-permute-start(bf16[64,1024]{1,0:T(8,128)(2,1)} %get-tuple-element.36), channel_id=1, source_target_pairs={{0,3},{1,2},{2,1},{3,0},{4,7},{5,6},{6,5},{7,4},{8,11},{9,10},{10,... | collective-permute-start | bytes 393224 | tf_op jit(solution)/shard_map/ppermute | solution.py:33
  (16 other events, 52.9 us)

commit v3 on v2

--- a/solution.py
+++ b/solution.py
@@ -11,7 +11,7 @@
 FLOOR_SCORE = -1e30
 HALF = jnp.bfloat16
 FULL = jnp.float32
-VMEM_GRANT = 60
+VMEM_GRANT = 32
 ATTEND_COST = 2 * 10**10
 
 VMEM = pl.BlockSpec(memory_space=pltpu.VMEM)
@@ -350,9 +350,10 @@
 
     if places == 8:
         lead = (places, ways, trainer_rows)
-        joined = stack(joined_blocks, normed, forward)
-        forward, joined = together(forward, joined)
-        held = whole_hop(joined, *first_hops(joined))
+        forward, *joined_blocks = together(forward, *joined_blocks)
+        joined = stack(joined_blocks)
+        near, far, normed = together(*first_hops(joined), normed)
+        held = whole_hop(joined, near, far)
         joined_pieces, joined_all = with_cores(held)
     else:
         lead = (features,)

time: 97.3 us -> 86.5 us (0.89)
  Pallas kernels: 21.7 us -> 11.3 us
  local copies, waits for them, and re-layouts: 3.32 us -> 8.86 us
  waiting for transfers between devices: 40.5 us -> 36.2 us
    unnamed x44 -> x32, local copies, waits for them, and re-layouts: 3.26 us -> 8.81 us
    ppermute x25, waiting for transfers between devices: 34.3 us -> 30.2 us  [swap(): return lax.ppermute(array, axis, [(i, i ^ mask) for i in range(size)])]
    pallas_call x1, Pallas kernels: 6.35 us -> 3.5 us  [shards(): pl.pallas_call(functools.partial(layer_kernel, forward_pieces, ways), nam...]
    pallas_call x1, Pallas kernels: 4.13 us -> 1.61 us  [shards(): pl.pallas_call(prepare_kernel, name='prepare', out_shape=[jax.ShapeDtypeS...]
    all_to_all x1, starting transfers between devices: 5.1 us -> 3.5 us  [owners_blocks(): lax.all_to_all(blocks, 'tensor', split_axis=0, concat_axis=0, tiled=True)]
    pallas_call x1, Pallas kernels: 1.69 us -> 0.23 us  [shards(): pl.pallas_call(joined_kernel, name='cut_joined', out_shape=[jax.ShapeDtyp...]
    pallas_call x1, Pallas kernels: 5.69 us -> 4.4 us  [shards(): pl.pallas_call(functools.partial(attend_kernel, joined_pieces), name='att...]
    pallas_call x1, Pallas kernels: 1.57 us -> 0.31 us  [stack(): pl.pallas_call(functools.partial(stack_kernel, ways), name='stack', out_s...]
  transfers between devices with their start and end apart: 26 -> 26, of which waited for: 12 -> 13; matrix products, arithmetic and copies ran while one was open for 0% -> 0% of each run, Pallas kernels for 12% -> 9%
where the time goes in v3:
time: 86.5 us; the launch traced here: 86.1 us
  waiting for transfers between devices  36.2 us (42%)
  starting transfers between devices  28.8 us (33%)
  Pallas kernels  11.3 us (13%)
  local copies, waits for them, and re-layouts  8.86 us (10%)
    ppermute x25, waiting for transfers between devices, swap(): return lax.ppermute(array, axis, [(i, i ^ mask) for i in range(size)])  30.2 us
    ppermute x25, starting transfers between devices, swap(): return lax.ppermute(array, axis, [(i, i ^ mask) for i in range(size)])  25.3 us
    unnamed x32, local copies, waits for them, and re-layouts  8.81 us
    all_to_all x1, waiting for transfers between devices, owners_blocks(): lax.all_to_all(blocks, 'tensor', split_axis=0, concat_axis=0, tiled=True)  6.02 us
    pallas_call x1, Pallas kernels, shards(): pl.pallas_call(functools.partial(attend_kernel, joined_pieces), name='att...  4.4 us
    all_to_all x1, starting transfers between devices, owners_blocks(): lax.all_to_all(blocks, 'tensor', split_axis=0, concat_axis=0, tiled=True)  3.5 us
    pallas_call x1, Pallas kernels, shards(): pl.pallas_call(functools.partial(layer_kernel, forward_pieces, ways), nam...  3.5 us
  transfers between devices with their start and end apart: 26, of which 13 were waited for; matrix products, arithmetic and copies ran while one was open for 0% of the time, Pallas kernels for 9%

profile of v3, /device:TPU:0, one launch (start us, length us, event | category | flops | bytes accessed | tf_op | source)
XLA Modules:
  0.0 86.1 jit_solution(4497425686807250515)
XLA Ops:
  0.0 1.1 %copy-done.3 = f32[32,3072]{1,0:T(8,128)S(1)} copy-done((f32[32,3072]{1,0:T(8,128)S(1)}, f32[32,3072]{1,0:T(8,128)}, u32[]{:S(2)}) %copy-start.3) | copy-done | bytes 393240
  1.3 3.1 %collective-permute-start = (bf16[32,768]{1,0:T(8,128)(2,1)S(1)}, bf16[32,768]{1,0:T(8,128)(2,1)S(1)}, u32[]{:S(2)}, u32[]{:S(2)}) collective-permute-start(bf16[32,768]{1,0:T(8,128)(2,1)S(1)} %get-tuple-element.28), channel_id=1, source_target_pairs={{0,1},{1,0},{2,3},{3,2},{4,5},{5,4},{6,7},{7,6},{8,9},{9,8},{10,11... | collective-permute-start | bytes 147464 | tf_op jit(solution)/shard_map/ppermute | solution.py:33
  4.4 2.6 %collective-permute-start.1 = (bf16[32,768]{1,0:T(8,128)(2,1)S(1)}, bf16[32,768]{1,0:T(8,128)(2,1)S(1)}, u32[]{:S(2)}, u32[]{:S(2)}) collective-permute-start(bf16[32,768]{1,0:T(8,128)(2,1)S(1)} %get-tuple-element.29), channel_id=1, source_target_pairs={{0,2},{1,3},{2,0},{3,1},{4,6},{5,7},{6,4},{7,5},{8,10},{9,11},{10,... | collective-permute-start | bytes 147464 | tf_op jit(solution)/shard_map/ppermute | solution.py:33
  7.0 1.0 %copy-done.1 = f32[32,4096]{1,0:T(8,128)S(1)} copy-done((f32[32,4096]{1,0:T(8,128)S(1)}, f32[32,4096]{1,0:T(8,128)}, u32[]{:S(2)}) %copy-start.1) | copy-done | bytes 524312
  8.0 1.0 %copy-done.2 = f32[32,4096]{1,0:T(8,128)S(1)} copy-done((f32[32,4096]{1,0:T(8,128)S(1)}, f32[32,4096]{1,0:T(8,128)}, u32[]{:S(2)}) %copy-start.2) | copy-done | bytes 524312
  10.0 1.2 %cut_forward.1 = bf16[4,32,3072]{2,1,0:T(8,128)(2,1)} custom-call(bf16[32,768]{1,0:T(8,128)(2,1)S(1)} %get-tuple-element.31.refs_0_.after, f32[32,1024]{1,0:T(8,128)S(1)} %copy-done.4, f32[32,4096]{1,0:T(8,128)S(1)} %copy-done.1, f32[32,4096]{1,0:T(8,128)S(1)} %copy-done.2), custom_call_target="tpu_custom_call" | custom-call | tf_op jit(solution)/shard_map/cut_forward/pallas_call | solution.py:309
  11.2 1.6 %collective-permute-done.2.refs_3_ = bf16[32,768]{1,0:T(8,128)(2,1)S(1)} collective-permute-done((bf16[32,768]{1,0:T(8,128)(2,1)S(1)}, bf16[32,768]{1,0:T(8,128)(2,1)S(1)}, u32[]{:S(2)}, u32[]{:S(2)}) %collective-permute-start.2) | collective-permute-done | bytes 49184 | tf_op jit(solution)/shard_map/ppermute | solution.py:33
  12.9 3.5 %all-to-all-start = ((bf16[4,32,3072]{2,1,0:T(8,128)(2,1)}), bf16[4,32,3072]{2,1,0:T(8,128)(2,1)S(1)}, u32[]{:S(2)}, u32[]{:S(2)}) async-start(bf16[4,32,3072]{2,1,0:T(8,128)(2,1)} %cut_forward.1), calls=%async_computation | async-start | bytes 1572864 | tf_op jit(solution)/shard_map/all_to_all | solution.py:265
  16.7 1.6 %collective-permute-start.3 = (bf16[4,32,768]{2,1,0:T(8,128)(2,1)S(1)}, bf16[4,32,768]{2,1,0:T(8,128)(2,1)S(1)}, u32[]{:S(2)}, u32[]{:S(2)}) collective-permute-start(bf16[4,32,768]{2,1,0:T(8,128)(2,1)S(1)} %stack.1.refs_0_), channel_id=1, source_target_pairs={{0,16},{4,20},{8,24},{12,28},{16,0},{20,4},{24,8},{28,12},{1,17},{... | collective-permute-start | bytes 589832 | tf_op jit(solution)/shard_map/ppermute | solution.py:33
  18.3 1.5 %collective-permute-start.4 = (bf16[4,32,768]{2,1,0:T(8,128)(2,1)S(1)}, bf16[4,32,768]{2,1,0:T(8,128)(2,1)S(1)}, u32[]{:S(2)}, u32[]{:S(2)}) collective-permute-start(bf16[4,32,768]{2,1,0:T(8,128)(2,1)S(1)} %stack.1.refs_0_), channel_id=1, source_target_pairs={{0,8},{4,12},{8,0},{12,4},{16,24},{20,28},{24,16},{28,20},{1,9},{5... | collective-permute-start | bytes 589832 | tf_op jit(solution)/shard_map/ppermute | solution.py:33
  19.8 1.6 %prepare.1 = (bf16[256,1024]{1,0:T(8,128)(2,1)S(1)}, f32[4,256,512]{2,1,0:T(8,128)S(1)}) custom-call(bf16[32,768]{1,0:T(8,128)(2,1)S(1)} %get-tuple-element.31.refs_0_.after, s32[8]{0:T(128)S(1)} %copy-done.8, s32[8]{0:T(128)S(1)} %copy-done.9, s32[8]{0:T(128)S(1)} %copy-done.10, bf16[256,1024]{1,0:T(8,128)(2,1)S(1)} %copy-done, f32[1,1024]{1,0:T(1,128)S(1)} %bitcast.4, ...), custom_call_target="tpu_custom_call" | custom-call | flops 100000000 | bytes 4000000 | tf_op jit(solution)/shard_map/prepare/pallas_call | solution.py:324
  21.4 1.3 %copy-done.11 = f32[4,256,512]{2,1,0:T(8,128)} copy-done((f32[4,256,512]{2,1,0:T(8,128)}, f32[4,256,512]{2,1,0:T(8,128)S(1)}, u32[]{:S(2)}) %copy-start.11) | copy-done | bytes 2097176
  22.8 1.2 %collective-permute-done.4.refs_2_ = bf16[4,32,768]{2,1,0:T(8,128)(2,1)S(1)} collective-permute-done((bf16[4,32,768]{2,1,0:T(8,128)(2,1)S(1)}, bf16[4,32,768]{2,1,0:T(8,128)(2,1)S(1)}, u32[]{:S(2)}, u32[]{:S(2)}) %collective-permute-start.4) | collective-permute-done | bytes 196640 | tf_op jit(solution)/shard_map/ppermute | solution.py:33
  23.9 1.5 %collective-permute-start.5 = (bf16[4,32,768]{2,1,0:T(8,128)(2,1)S(1)}, bf16[4,32,768]{2,1,0:T(8,128)(2,1)S(1)}, u32[]{:S(2)}, u32[]{:S(2)}) collective-permute-start(bf16[4,32,768]{2,1,0:T(8,128)(2,1)S(1)} %collective-permute-done.3.refs_1_), channel_id=1, source_target_pairs={{0,8},{4,12},{8,0},{12,4},{16,24},{20,28},{24,16},{28,20},{1,9},{5... | collective-permute-start | bytes 589832 | tf_op jit(solution)/shard_map/ppermute | solution.py:33
  25.9 3.7 %collective-permute-done.5.refs_3_ = bf16[4,32,768]{2,1,0:T(8,128)(2,1)S(1)} collective-permute-done((bf16[4,32,768]{2,1,0:T(8,128)(2,1)S(1)}, bf16[4,32,768]{2,1,0:T(8,128)(2,1)S(1)}, u32[]{:S(2)}, u32[]{:S(2)}) %collective-permute-start.5) | collective-permute-done | bytes 196640 | tf_op jit(solution)/shard_map/ppermute | solution.py:33
  29.6 6.0 %all-to-all-done.refs_4_ = bf16[4,32,3072]{2,1,0:T(8,128)(2,1)S(1)} async-done(((bf16[4,32,3072]{2,1,0:T(8,128)(2,1)}), bf16[4,32,3072]{2,1,0:T(8,128)(2,1)S(1)}, u32[]{:S(2)}, u32[]{:S(2)}) %all-to-all-start) | async-done | bytes 786464 | tf_op jit(solution)/shard_map/all_to_all | solution.py:265
  35.6 1.5 %collective-permute-start.13 = (bf16[4,32,3072]{2,1,0:T(8,128)(2,1)S(1)}, bf16[4,32,3072]{2,1,0:T(8,128)(2,1)S(1)}, u32[]{:S(2)}, u32[]{:S(2)}) collective-permute-start(bf16[4,32,3072]{2,1,0:T(8,128)(2,1)S(1)} %all-to-all-done.refs_4_), channel_id=1, source_target_pairs={{0,16},{4,20},{8,24},{12,28},{16,0},{20,4},{24,8},{28,12},{1,17},{... | collective-permute-start | bytes 2359304 | tf_op jit(solution)/shard_map/ppermute | solution.py:33
  37.1 1.5 %collective-permute-start.14 = (bf16[4,32,3072]{2,1,0:T(8,128)(2,1)S(1)}, bf16[4,32,3072]{2,1,0:T(8,128)(2,1)S(1)}, u32[]{:S(2)}, u32[]{:S(2)}) collective-permute-start(bf16[4,32,3072]{2,1,0:T(8,128)(2,1)S(1)} %all-to-all-done.refs_4_), channel_id=1, source_target_pairs={{0,8},{4,12},{8,0},{12,4},{16,24},{20,28},{24,16},{28,20},{1,9},{5... | collective-permute-start | bytes 2359304 | tf_op jit(solution)/shard_map/ppermute | solution.py:33
  38.7 1.6 %copy-done.12 = f32[4,256,512]{2,1,0:T(8,128)S(1)} copy-done((f32[4,256,512]{2,1,0:T(8,128)S(1)}, f32[4,256,512]{2,1,0:T(8,128)}, u32[]{:S(2)}) %copy-start.12) | copy-done | bytes 2097176
  42.1 4.4 %attend.1.refs_0_ = bf16[256,256]{1,0:T(8,128)(2,1)S(1)} custom-call(bf16[256,1024]{1,0:T(8,128)(2,1)S(1)} %get-tuple-element.38.normed, bf16[256,256]{1,0:T(8,128)(2,1)S(1)} %copy-done.13, bf16[256,256]{1,0:T(8,128)(2,1)S(1)} %copy-done.14, f32[4,256,512]{2,1,0:T(8,128)S(1)} %copy-done.12, bf16[4,32,768]{2,1,0:T(8,128)(2,1)S(1)} %stack.1.refs_0_, ...), custom_call_target="tpu_custom_call" | custom-call | flops 20000000000 | bytes 6000000 | tf_op jit(solution)/shard_map/attend/pallas_call | solution.py:364
  46.5 2.0 %collective-permute-start.11 = (bf16[256,256]{1,0:T(8,128)(2,1)S(1)}, bf16[256,256]{1,0:T(8,128)(2,1)S(1)}, u32[]{:S(2)}, u32[]{:S(2)}) collective-permute-start(bf16[256,256]{1,0:T(8,128)(2,1)S(1)} %attend.1.refs_0_), channel_id=1, source_target_pairs={{0,2},{1,3},{2,0},{3,1},{4,6},{5,7},{6,4},{7,5},{8,10},{9,11},{10,... | collective-permute-start | bytes 393224 | tf_op jit(solution)/shard_map/ppermute | solution.py:33
  48.6 2.4 %collective-permute-start.12 = (bf16[256,256]{1,0:T(8,128)(2,1)S(1)}, bf16[256,256]{1,0:T(8,128)(2,1)S(1)}, u32[]{:S(2)}, u32[]{:S(2)}) collective-permute-start(bf16[256,256]{1,0:T(8,128)(2,1)S(1)} %attend.1.refs_0_), channel_id=1, source_target_pairs={{0,3},{1,2},{2,1},{3,0},{4,7},{5,6},{6,5},{7,4},{8,11},{9,10},{10,... | collective-permute-start | bytes 393224 | tf_op jit(solution)/shard_map/ppermute | solution.py:33
  50.9 3.2 %collective-permute-done.13.refs_5_ = bf16[4,32,3072]{2,1,0:T(8,128)(2,1)S(1)} collective-permute-done((bf16[4,32,3072]{2,1,0:T(8,128)(2,1)S(1)}, bf16[4,32,3072]{2,1,0:T(8,128)(2,1)S(1)}, u32[]{:S(2)}, u32[]{:S(2)}) %collective-permute-start.13) | collective-permute-done | bytes 786464 | tf_op jit(solution)/shard_map/ppermute | solution.py:33
  54.1 1.2 %collective-permute-done.14.refs_6_ = bf16[4,32,3072]{2,1,0:T(8,128)(2,1)S(1)} collective-permute-done((bf16[4,32,3072]{2,1,0:T(8,128)(2,1)S(1)}, bf16[4,32,3072]{2,1,0:T(8,128)(2,1)S(1)}, u32[]{:S(2)}, u32[]{:S(2)}) %collective-permute-start.14) | collective-permute-done | bytes 786464 | tf_op jit(solution)/shard_map/ppermute | solution.py:33
  55.4 1.6 %collective-permute-start.15 = (bf16[2,32,3072]{2,1,0:T(8,128)(2,1)S(1)}, bf16[2,32,3072]{2,1,0:T(8,128)(2,1)S(1)}, u32[]{:S(2)}, u32[]{:S(2)}) collective-permute-start(bf16[2,32,3072]{2,1,0:T(8,128)(2,1)S(1)} %slice.6), channel_id=1, source_target_pairs={{0,8},{4,12},{8,0},{12,4},{16,24},{20,28},{24,16},{28,20},{1,9},{5... | collective-permute-start | bytes 1179656 | tf_op jit(solution)/shard_map/ppermute | solution.py:33
  59.0 6.8 %collective-permute-done.15.refs_7_ = bf16[2,32,3072]{2,1,0:T(8,128)(2,1)S(1)} collective-permute-done((bf16[2,32,3072]{2,1,0:T(8,128)(2,1)S(1)}, bf16[2,32,3072]{2,1,0:T(8,128)(2,1)S(1)}, u32[]{:S(2)}, u32[]{:S(2)}) %collective-permute-start.15) | collective-permute-done | bytes 393248 | tf_op jit(solution)/shard_map/ppermute | solution.py:33
  65.8 1.3 %collective-permute-done.16.refs_8_ = bf16[2,32,3072]{2,1,0:T(8,128)(2,1)S(1)} collective-permute-done((bf16[2,32,3072]{2,1,0:T(8,128)(2,1)S(1)}, bf16[2,32,3072]{2,1,0:T(8,128)(2,1)S(1)}, u32[]{:S(2)}, u32[]{:S(2)}) %collective-permute-start.16) | collective-permute-done | bytes 393248 | tf_op jit(solution)/shard_map/ppermute | solution.py:33
  67.5 1.3 %collective-permute-done.21.refs_13_ = bf16[2,32,3072]{2,1,0:T(8,128)(2,1)S(1)} collective-permute-done((bf16[2,32,3072]{2,1,0:T(8,128)(2,1)S(1)}, bf16[2,32,3072]{2,1,0:T(8,128)(2,1)S(1)}, u32[]{:S(2)}, u32[]{:S(2)}) %collective-permute-start.21) | collective-permute-done | bytes 393248 | tf_op jit(solution)/shard_map/ppermute | solution.py:33
  68.8 3.5 %layer.1 = (f32[64,1024]{1,0:T(8,128)S(1)}, bf16[64,1024]{1,0:T(8,128)(2,1)S(1)}, bf16[64,1024]{1,0:T(8,128)(2,1)S(1)}, bf16[64,1024]{1,0:T(8,128)(2,1)S(1)}) custom-call(bf16[256,1024]{1,0:T(8,128)(2,1)S(1)} %copy-done, f32[1,1024]{1,0:T(1,128)S(1)} %bitcast.7, bf16[256,256]{1,0:T(8,128)(2,1)S(1)} %attend.1.refs_0_, ...), custom_call_target="tpu_custom_call" | custom-call | flops 2000000000 | bytes 8000000 | tf_op jit(solution)/shard_map/layer/pallas_call | solution.py:381
  73.0 3.7 %collective-permute-start.24 = (bf16[64,1024]{1,0:T(8,128)(2,1)S(1)}, bf16[64,1024]{1,0:T(8,128)(2,1)S(1)}, u32[]{:S(2)}, u32[]{:S(2)}) collective-permute-start(bf16[64,1024]{1,0:T(8,128)(2,1)S(1)} %get-tuple-element.48), channel_id=1, source_target_pairs={{0,3},{1,2},{2,1},{3,0},{4,7},{5,6},{6,5},{7,4},{8,11},{9,10},{10,... | collective-permute-start | bytes 393224 | tf_op jit(solution)/shard_map/ppermute | solution.py:33
  76.8 2.4 %collective-permute-done.22 = bf16[64,1024]{1,0:T(8,128)(2,1)S(1)} collective-permute-done((bf16[64,1024]{1,0:T(8,128)(2,1)S(1)}, bf16[64,1024]{1,0:T(8,128)(2,1)S(1)}, u32[]{:S(2)}, u32[]{:S(2)}) %collective-permute-start.22) | collective-permute-done | bytes 131104 | tf_op jit(solution)/shard_map/ppermute | solution.py:33
  79.1 6.2 %collective-permute-done.23 = bf16[64,1024]{1,0:T(8,128)(2,1)S(1)} collective-permute-done((bf16[64,1024]{1,0:T(8,128)(2,1)S(1)}, bf16[64,1024]{1,0:T(8,128)(2,1)S(1)}, u32[]{:S(2)}, u32[]{:S(2)}) %collective-permute-start.23) | collective-permute-done | bytes 131104 | tf_op jit(solution)/shard_map/ppermute | solution.py:33
  (61 shorter events, 7.8 us)
Async XLA Ops:
  0.0 19.8 %copy-start = (bf16[256,1024]{1,0:T(8,128)(2,1)S(1)}, bf16[256,1024]{1,0:T(8,128)(2,1)}, u32[]{:S(2)}) copy-start(bf16[256,1024]{1,0:T(8,128)(2,1)} %tokens.3) | copy-start | bytes 1572868
  1.3 9.9 %collective-permute-start = (bf16[32,768]{1,0:T(8,128)(2,1)S(1)}, bf16[32,768]{1,0:T(8,128)(2,1)S(1)}, u32[]{:S(2)}, u32[]{:S(2)}) collective-permute-start(bf16[32,768]{1,0:T(8,128)(2,1)S(1)} %get-tuple-element.28), channel_id=1, source_target_pairs={{0,1},{1,0},{2,3},{3,2},{4,5},{5,4},{6,7},{7,6},{8,9},{9,8},{10,11... | collective-permute-start | bytes 147464 | tf_op jit(solution)/shard_map/ppermute | solution.py:33
  4.4 6.9 %collective-permute-start.1 = (bf16[32,768]{1,0:T(8,128)(2,1)S(1)}, bf16[32,768]{1,0:T(8,128)(2,1)S(1)}, u32[]{:S(2)}, u32[]{:S(2)}) collective-permute-start(bf16[32,768]{1,0:T(8,128)(2,1)S(1)} %get-tuple-element.29), channel_id=1, source_target_pairs={{0,2},{1,3},{2,0},{3,1},{4,6},{5,7},{6,4},{7,5},{8,10},{9,11},{10,... | collective-permute-start | bytes 147464 | tf_op jit(solution)/shard_map/ppermute | solution.py:33
  7.0 5.9 %collective-permute-start.2 = (bf16[32,768]{1,0:T(8,128)(2,1)S(1)}, bf16[32,768]{1,0:T(8,128)(2,1)S(1)}, u32[]{:S(2)}, u32[]{:S(2)}) collective-permute-start(bf16[32,768]{1,0:T(8,128)(2,1)S(1)} %get-tuple-element.30), channel_id=1, source_target_pairs={{0,3},{1,2},{2,1},{3,0},{4,7},{5,6},{6,5},{7,4},{8,11},{9,10},{10,... | collective-permute-start | bytes 147464 | tf_op jit(solution)/shard_map/ppermute | solution.py:33
  10.0 9.8 %copy-start.7 = (f32[32,4]{0,1:T(4,128)S(1)}, f32[32,4]{0,1:T(4,128)}, u32[]{:S(2)}) copy-start(f32[32,4]{0,1:T(4,128)} %param.23) | copy-start | bytes 1540
  10.0 9.8 %copy-start.8 = (s32[8]{0:T(128)S(1)}, s32[8]{0:T(128)}, u32[]{:S(2)}) copy-start(s32[8]{0:T(128)} %lengths.1) | copy-start | bytes 100
  10.0 9.8 %copy-start.9 = (s32[8]{0:T(128)S(1)}, s32[8]{0:T(128)}, u32[]{:S(2)}) copy-start(s32[8]{0:T(128)} %flags.1) | copy-start | bytes 100
  10.0 9.8 %copy-start.10 = (s32[8]{0:T(128)S(1)}, s32[8]{0:T(128)}, u32[]{:S(2)}) copy-start(s32[8]{0:T(128)} %counts.1) | copy-start | bytes 100
  12.9 22.8 %all-to-all-start = ((bf16[4,32,3072]{2,1,0:T(8,128)(2,1)}), bf16[4,32,3072]{2,1,0:T(8,128)(2,1)S(1)}, u32[]{:S(2)}, u32[]{:S(2)}) async-start(bf16[4,32,3072]{2,1,0:T(8,128)(2,1)} %cut_forward.1), calls=%async_computation | async-start | bytes 1572864 | tf_op jit(solution)/shard_map/all_to_all | solution.py:265
  16.7 6.1 %collective-permute-start.3 = (bf16[4,32,768]{2,1,0:T(8,128)(2,1)S(1)}, bf16[4,32,768]{2,1,0:T(8,128)(2,1)S(1)}, u32[]{:S(2)}, u32[]{:S(2)}) collective-permute-start(bf16[4,32,768]{2,1,0:T(8,128)(2,1)S(1)} %stack.1.refs_0_), channel_id=1, source_target_pairs={{0,16},{4,20},{8,24},{12,28},{16,0},{20,4},{24,8},{28,12},{1,17},{... | collective-permute-start | bytes 589832 | tf_op jit(solution)/shard_map/ppermute | solution.py:33
  18.3 5.7 %collective-permute-start.4 = (bf16[4,32,768]{2,1,0:T(8,128)(2,1)S(1)}, bf16[4,32,768]{2,1,0:T(8,128)(2,1)S(1)}, u32[]{:S(2)}, u32[]{:S(2)}) collective-permute-start(bf16[4,32,768]{2,1,0:T(8,128)(2,1)S(1)} %stack.1.refs_0_), channel_id=1, source_target_pairs={{0,8},{4,12},{8,0},{12,4},{16,24},{20,28},{24,16},{28,20},{1,9},{5... | collective-permute-start | bytes 589832 | tf_op jit(solution)/shard_map/ppermute | solution.py:33
  23.9 5.7 %collective-permute-start.5 = (bf16[4,32,768]{2,1,0:T(8,128)(2,1)S(1)}, bf16[4,32,768]{2,1,0:T(8,128)(2,1)S(1)}, u32[]{:S(2)}, u32[]{:S(2)}) collective-permute-start(bf16[4,32,768]{2,1,0:T(8,128)(2,1)S(1)} %collective-permute-done.3.refs_1_), channel_id=1, source_target_pairs={{0,8},{4,12},{8,0},{12,4},{16,24},{20,28},{24,16},{28,20},{1,9},{5... | collective-permute-start | bytes 589832 | tf_op jit(solution)/shard_map/ppermute | solution.py:33
  25.4 11.7 %collective-permute-start.6 = (bf16[4,32,768]{2,1,0:T(8,128)(2,1)S(1)}, bf16[4,32,768]{2,1,0:T(8,128)(2,1)S(1)}, u32[]{:S(2)}, u32[]{:S(2)}) collective-permute-start(bf16[4,32,768]{2,1,0:T(8,128)(2,1)S(1)} %stack.1.refs_0_), channel_id=1, source_target_pairs={{0,4},{4,0},{8,12},{12,8},{16,20},{20,16},{24,28},{28,24},{1,5},{5... | collective-permute-start | bytes 589832 | tf_op jit(solution)/shard_map/ppermute | solution.py:33
  25.4 13.2 %collective-permute-start.7 = (bf16[4,32,768]{2,1,0:T(8,128)(2,1)S(1)}, bf16[4,32,768]{2,1,0:T(8,128)(2,1)S(1)}, u32[]{:S(2)}, u32[]{:S(2)}) collective-permute-start(bf16[4,32,768]{2,1,0:T(8,128)(2,1)S(1)} %collective-permute-done.3.refs_1_), channel_id=1, source_target_pairs={{0,4},{4,0},{8,12},{12,8},{16,20},{20,16},{24,28},{28,24},{1,5},{5... | collective-permute-start | bytes 589832 | tf_op jit(solution)/shard_map/ppermute | solution.py:33
  25.9 12.7 %collective-permute-start.8 = (bf16[4,32,768]{2,1,0:T(8,128)(2,1)S(1)}, bf16[4,32,768]{2,1,0:T(8,128)(2,1)S(1)}, u32[]{:S(2)}, u32[]{:S(2)}) collective-permute-start(bf16[4,32,768]{2,1,0:T(8,128)(2,1)S(1)} %collective-permute-done.4.refs_2_), channel_id=1, source_target_pairs={{0,4},{4,0},{8,12},{12,8},{16,20},{20,16},{24,28},{28,24},{1,5},{5... | collective-permute-start | bytes 589832 | tf_op jit(solution)/shard_map/ppermute | solution.py:33
  29.6 9.0 %collective-permute-start.9 = (bf16[4,32,768]{2,1,0:T(8,128)(2,1)S(1)}, bf16[4,32,768]{2,1,0:T(8,128)(2,1)}, u32[]{:S(2)}, u32[]{:S(2)}) collective-permute-start(bf16[4,32,768]{2,1,0:T(8,128)(2,1)S(1)} %collective-permute-done.5.refs_3_), channel_id=1, source_target_pairs={{0,4},{4,0},{8,12},{12,8},{16,20},{20,16},{24,28},{28,24},{1,5},{5... | collective-permute-start | bytes 589832 | tf_op jit(solution)/shard_map/ppermute | solution.py:33
  35.6 18.5 %collective-permute-start.13 = (bf16[4,32,3072]{2,1,0:T(8,128)(2,1)S(1)}, bf16[4,32,3072]{2,1,0:T(8,128)(2,1)S(1)}, u32[]{:S(2)}, u32[]{:S(2)}) collective-permute-start(bf16[4,32,3072]{2,1,0:T(8,128)(2,1)S(1)} %all-to-all-done.refs_4_), channel_id=1, source_target_pairs={{0,16},{4,20},{8,24},{12,28},{16,0},{20,4},{24,8},{28,12},{1,17},{... | collective-permute-start | bytes 2359304 | tf_op jit(solution)/shard_map/ppermute | solution.py:33
  37.1 18.2 %collective-permute-start.14 = (bf16[4,32,3072]{2,1,0:T(8,128)(2,1)S(1)}, bf16[4,32,3072]{2,1,0:T(8,128)(2,1)S(1)}, u32[]{:S(2)}, u32[]{:S(2)}) collective-permute-start(bf16[4,32,3072]{2,1,0:T(8,128)(2,1)S(1)} %all-to-all-done.refs_4_), channel_id=1, source_target_pairs={{0,8},{4,12},{8,0},{12,4},{16,24},{20,28},{24,16},{28,20},{1,9},{5... | collective-permute-start | bytes 2359304 | tf_op jit(solution)/shard_map/ppermute | solution.py:33
  42.1 26.7 %copy-start.15 = (f32[1024]{0:T(1024)S(1)}, f32[1024]{0:T(1024)}, u32[]{:S(2)}) copy-start(f32[1024]{0:T(1024)} %param.22) | copy-start | bytes 12292
  46.5 10.5 %collective-permute-start.10 = (bf16[256,256]{1,0:T(8,128)(2,1)S(1)}, bf16[256,256]{1,0:T(8,128)(2,1)S(1)}, u32[]{:S(2)}, u32[]{:S(2)}) collective-permute-start(bf16[256,256]{1,0:T(8,128)(2,1)S(1)} %attend.1.refs_0_), channel_id=1, source_target_pairs={{0,1},{1,0},{2,3},{3,2},{4,5},{5,4},{6,7},{7,6},{8,9},{9,8},{10,11... | collective-permute-start | bytes 393224 | tf_op jit(solution)/shard_map/ppermute | solution.py:33
  46.5 11.9 %collective-permute-start.11 = (bf16[256,256]{1,0:T(8,128)(2,1)S(1)}, bf16[256,256]{1,0:T(8,128)(2,1)S(1)}, u32[]{:S(2)}, u32[]{:S(2)}) collective-permute-start(bf16[256,256]{1,0:T(8,128)(2,1)S(1)} %attend.1.refs_0_), channel_id=1, source_target_pairs={{0,2},{1,3},{2,0},{3,1},{4,6},{5,7},{6,4},{7,5},{8,10},{9,11},{10,... | collective-permute-start | bytes 393224 | tf_op jit(solution)/shard_map/ppermute | solution.py:33
  48.6 9.9 %collective-permute-start.12 = (bf16[256,256]{1,0:T(8,128)(2,1)S(1)}, bf16[256,256]{1,0:T(8,128)(2,1)S(1)}, u32[]{:S(2)}, u32[]{:S(2)}) collective-permute-start(bf16[256,256]{1,0:T(8,128)(2,1)S(1)} %attend.1.refs_0_), channel_id=1, source_target_pairs={{0,3},{1,2},{2,1},{3,0},{4,7},{5,6},{6,5},{7,4},{8,11},{9,10},{10,... | collective-permute-start | bytes 393224 | tf_op jit(solution)/shard_map/ppermute | solution.py:33
  54.1 13.0 %collective-permute-start.17 = (bf16[4,32,3072]{2,1,0:T(8,128)(2,1)S(1)}, bf16[4,32,3072]{2,1,0:T(8,128)(2,1)S(1)}, u32[]{:S(2)}, u32[]{:S(2)}) collective-permute-start(bf16[4,32,3072]{2,1,0:T(8,128)(2,1)S(1)} %all-to-all-done.refs_4_), channel_id=1, source_target_pairs={{0,4},{4,0},{8,12},{12,8},{16,20},{20,16},{24,28},{28,24},{1,5},{5... | collective-permute-start | bytes 2359304 | tf_op jit(solution)/shard_map/ppermute | solution.py:33
  55.4 10.4 %collective-permute-start.15 = (bf16[2,32,3072]{2,1,0:T(8,128)(2,1)S(1)}, bf16[2,32,3072]{2,1,0:T(8,128)(2,1)S(1)}, u32[]{:S(2)}, u32[]{:S(2)}) collective-permute-start(bf16[2,32,3072]{2,1,0:T(8,128)(2,1)S(1)} %slice.6), channel_id=1, source_target_pairs={{0,8},{4,12},{8,0},{12,4},{16,24},{20,28},{24,16},{28,20},{1,9},{5... | collective-permute-start | bytes 1179656 | tf_op jit(solution)/shard_map/ppermute | solution.py:33
  57.0 10.1 %collective-permute-start.16 = (bf16[2,32,3072]{2,1,0:T(8,128)(2,1)S(1)}, bf16[2,32,3072]{2,1,0:T(8,128)(2,1)S(1)}, u32[]{:S(2)}, u32[]{:S(2)}) collective-permute-start(bf16[2,32,3072]{2,1,0:T(8,128)(2,1)S(1)} %slice.7), channel_id=1, source_target_pairs={{0,16},{4,20},{8,24},{12,28},{16,0},{20,4},{24,8},{28,12},{1,17},{... | collective-permute-start | bytes 1179656 | tf_op jit(solution)/shard_map/ppermute | solution.py:33
  58.5 10.3 %collective-permute-start.18 = (bf16[4,32,3072]{2,1,0:T(8,128)(2,1)S(1)}, bf16[4,32,3072]{2,1,0:T(8,128)(2,1)S(1)}, u32[]{:S(2)}, u32[]{:S(2)}) collective-permute-start(bf16[4,32,3072]{2,1,0:T(8,128)(2,1)S(1)} %collective-permute-done.13.refs_5_), channel_id=1, source_target_pairs={{0,4},{4,0},{8,12},{12,8},{16,20},{20,16},{24,28},{28,24},{1,5},{5... | collective-permute-start | bytes 2359304 | tf_op jit(solution)/shard_map/ppermute | solution.py:33
  58.5 10.3 %collective-permute-start.19 = (bf16[4,32,3072]{2,1,0:T(8,128)(2,1)S(1)}, bf16[4,32,3072]{2,1,0:T(8,128)(2,1)S(1)}, u32[]{:S(2)}, u32[]{:S(2)}) collective-permute-start(bf16[4,32,3072]{2,1,0:T(8,128)(2,1)S(1)} %collective-permute-done.14.refs_6_), channel_id=1, source_target_pairs={{0,4},{4,0},{8,12},{12,8},{16,20},{20,16},{24,28},{28,24},{1,5},{5... | collective-permute-start | bytes 2359304 | tf_op jit(solution)/shard_map/ppermute | solution.py:33
  65.8 1.7 %collective-permute-start.20 = (bf16[2,32,3072]{2,1,0:T(8,128)(2,1)S(1)}, bf16[2,32,3072]{2,1,0:T(8,128)(2,1)S(1)}, u32[]{:S(2)}, u32[]{:S(2)}) collective-permute-start(bf16[2,32,3072]{2,1,0:T(8,128)(2,1)S(1)} %collective-permute-done.15.refs_7_), channel_id=1, source_target_pairs={{0,4},{4,0},{8,12},{12,8},{16,20},{20,16},{24,28},{28,24},{1,5},{5... | collective-permute-start | bytes 1179656 | tf_op jit(solution)/shard_map/ppermute | solution.py:33
  67.1 1.7 %collective-permute-start.21 = (bf16[2,32,3072]{2,1,0:T(8,128)(2,1)S(1)}, bf16[2,32,3072]{2,1,0:T(8,128)(2,1)S(1)}, u32[]{:S(2)}, u32[]{:S(2)}) collective-permute-start(bf16[2,32,3072]{2,1,0:T(8,128)(2,1)S(1)} %collective-permute-done.16.refs_8_), channel_id=1, source_target_pairs={{0,4},{4,0},{8,12},{12,8},{16,20},{20,16},{24,28},{28,24},{1,5},{5... | collective-permute-start | bytes 1179656 | tf_op jit(solution)/shard_map/ppermute | solution.py:33
  72.3 6.8 %collective-permute-start.22 = (bf16[64,1024]{1,0:T(8,128)(2,1)S(1)}, bf16[64,1024]{1,0:T(8,128)(2,1)S(1)}, u32[]{:S(2)}, u32[]{:S(2)}) collective-permute-start(bf16[64,1024]{1,0:T(8,128)(2,1)S(1)} %get-tuple-element.46), channel_id=1, source_target_pairs={{0,1},{1,0},{2,3},{3,2},{4,5},{5,4},{6,7},{7,6},{8,9},{9,8},{10,11... | collective-permute-start | bytes 393224 | tf_op jit(solution)/shard_map/ppermute | solution.py:33
  72.4 13.0 %collective-permute-start.23 = (bf16[64,1024]{1,0:T(8,128)(2,1)S(1)}, bf16[64,1024]{1,0:T(8,128)(2,1)S(1)}, u32[]{:S(2)}, u32[]{:S(2)}) collective-permute-start(bf16[64,1024]{1,0:T(8,128)(2,1)S(1)} %get-tuple-element.47), channel_id=1, source_target_pairs={{0,2},{1,3},{2,0},{3,1},{4,6},{5,7},{6,4},{7,5},{8,10},{9,11},{10,... | collective-permute-start | bytes 393224 | tf_op jit(solution)/shard_map/ppermute | solution.py:33
  73.0 12.3 %collective-permute-start.24 = (bf16[64,1024]{1,0:T(8,128)(2,1)S(1)}, bf16[64,1024]{1,0:T(8,128)(2,1)S(1)}, u32[]{:S(2)}, u32[]{:S(2)}) collective-permute-start(bf16[64,1024]{1,0:T(8,128)(2,1)S(1)} %get-tuple-element.48), channel_id=1, source_target_pairs={{0,3},{1,2},{2,1},{3,0},{4,7},{5,6},{6,5},{7,4},{8,11},{9,10},{10,... | collective-permute-start | bytes 393224 | tf_op jit(solution)/shard_map/ppermute | solution.py:33
  (10 other events, 28.4 us)

commit v4 on v3

--- a/solution.py
+++ b/solution.py
@@ -12,6 +12,7 @@
 HALF = jnp.bfloat16
 FULL = jnp.float32
 VMEM_GRANT = 32
+CUT_GRANT = 60
 ATTEND_COST = 2 * 10**10
 
 VMEM = pl.BlockSpec(memory_space=pltpu.VMEM)
@@ -56,30 +57,24 @@
         copy.wait()
 
 
-def joined_kernel(joined_source, *refs):
-    outs, (joined, sems) = refs[:-2], refs[-2:]
-    load([joined_source], [joined], sems)
+def cut_kernel(*refs):
+    sources, outs, (joined, output, upward, downward, sems) = refs[:4], refs[4:-5], refs[-5:]
+    load(sources, [joined, output, upward, downward], sems)
     mine, _ = here()
-    ways = len(outs)
-    width = outs[0].shape[1] // 3
+    blocks, forward = outs[:-1], outs[-1]
+    ways = len(blocks)
+    part = joined.shape[1] // (3 * ways)
     for k in range(ways):
-        owner = mine ^ k
-        for part in range(3):
-            start = pl.multiple_of((part * ways + owner) * width, 128)
-            outs[k][:, part * width : (part + 1) * width] = joined[:, pl.ds(start, width)].astype(HALF)
-
-
-def forward_kernel(*refs):
-    sources, (blocks, output, upward, downward, sems) = refs[-8:-5], refs[-5:]
-    load(sources, [output, upward, downward], sems)
-    ways = blocks.shape[0]
+        for i in range(3):
+            start = pl.multiple_of((i * ways + (mine ^ k)) * part, 128)
+            blocks[k][:, i * part : (i + 1) * part] = joined[:, pl.ds(start, part)].astype(HALF)
     whole = output.shape[1]
     width = upward.shape[1] // ways
     output_half = output[...].astype(HALF)
     for t in range(ways):
-        blocks[t, :, :whole] = output_half
-        blocks[t, :, whole : whole + width] = upward[:, t * width : (t + 1) * width].astype(HALF)
-        blocks[t, :, whole + width :] = downward[:, t * width : (t + 1) * width].astype(HALF)
+        forward[t, :, :whole] = output_half
+        forward[t, :, whole : whole + width] = upward[:, t * width : (t + 1) * width].astype(HALF)
+        forward[t, :, whole + width :] = downward[:, t * width : (t + 1) * width].astype(HALF)
 
 
 def rms_rows(rows, gain):
@@ -294,31 +289,18 @@
     columns = attn_width + 2 * hidden_units
     span = bucket_index.shape[0] + 1
 
-    joined_blocks = pl.pallas_call(
-        joined_kernel,
-        name="cut_joined",
-        out_shape=[jax.ShapeDtypeStruct((trainer_rows, 3 * width), HALF)] * ways,
-        in_specs=[HBM],
-        out_specs=[VMEM] * ways,
-        scratch_shapes=[
-            pltpu.VMEM(joined_weight.shape, FULL),
-            pltpu.SemaphoreType.DMA((1,)),
-        ],
-        compiler_params=params(VMEM_GRANT),
-    )(joined_weight)
-    forward = pl.pallas_call(
-        forward_kernel,
-        name="cut_forward",
-        out_shape=jax.ShapeDtypeStruct((ways, trainer_rows, columns), HALF),
-        in_specs=[ANY, HBM, HBM, HBM],
-        out_specs=VMEM,
-        scratch_shapes=[
-            pltpu.VMEM(weight.shape, FULL)
-            for weight in (output_weight, upward_weight, downward_weight)
-        ]
-        + [pltpu.SemaphoreType.DMA((3,))],
-        compiler_params=params(VMEM_GRANT),
-    )(joined_blocks[0], output_weight, upward_weight, downward_weight)
+    weights = (joined_weight, output_weight, upward_weight, downward_weight)
+    *joined_blocks, forward = pl.pallas_call(
+        cut_kernel,
+        name="cut",
+        out_shape=[jax.ShapeDtypeStruct((trainer_rows, 3 * width), HALF)] * ways
+        + [jax.ShapeDtypeStruct((ways, trainer_rows, columns), HALF)],
+        in_specs=[HBM] * 4,
+        out_specs=[VMEM] * (1 + ways),
+        scratch_shapes=[pltpu.VMEM(weight.shape, FULL) for weight in weights]
+        + [pltpu.SemaphoreType.DMA((4,))],
+        compiler_params=params(CUT_GRANT),
+    )(*weights)
     own_joined, joined_blocks = joined_blocks[0], exchange(joined_blocks)
 
     normed, bias = pl.pallas_call(
@@ -336,7 +318,7 @@
             pltpu.SemaphoreType.DMA((3,)),
         ],
         compiler_params=params(VMEM_GRANT),
-        cost_estimate=cost(10**8, 4 * 10**6),
+        cost_estimate=cost(2 * 10**10, 4 * 10**6),
     )(
         own_joined,
         cached_lengths,
@@ -350,9 +332,8 @@
 
     if places == 8:
         lead = (places, ways, trainer_rows)
-        forward, *joined_blocks = together(forward, *joined_blocks)
-        joined = stack(joined_blocks)
-        near, far, normed = together(*first_hops(joined), normed)
+        joined = stack(joined_blocks, normed)
+        near, far = first_hops(joined)
         held = whole_hop(joined, near, far)
         joined_pieces, joined_all = with_cores(held)
     else:

time: 86.5 us -> 84.6 us (0.978)
  local copies, waits for them, and re-layouts: 8.86 us -> 5.63 us
  starting transfers between devices: 28.8 us -> 30.4 us
    all_to_all x1, waiting for transfers between devices: 6.02 us -> 2.18 us  [owners_blocks(): lax.all_to_all(blocks, 'tensor', split_axis=0, concat_axis=0, tiled=True)]
    ppermute x25, waiting for transfers between devices: 30.2 us -> 33.5 us  [swap(): return lax.ppermute(array, axis, [(i, i ^ mask) for i in range(size)])]
    unnamed x32 -> x26, local copies, waits for them, and re-layouts: 8.81 us -> 5.58 us
    all_to_all x1, starting transfers between devices: 3.5 us -> 5.09 us  [owners_blocks(): lax.all_to_all(blocks, 'tensor', split_axis=0, concat_axis=0, tiled=True)]
    pallas_call x2 -> x1, Pallas kernels: 1.44 us -> 2.47 us  [shards(): pl.pallas_call(cut_kernel, name='cut', out_shape=[jax.ShapeDtypeStruct((t...]
  transfers between devices with their start and end apart: 26 -> 26, of which waited for: 13 -> 13; matrix products, arithmetic and copies ran while one was open for 0% -> 0% of each run, Pallas kernels for 9% -> 7%
where the time goes in v4:
time: 84.6 us; the launch traced here: 84.3 us
  waiting for transfers between devices  35.7 us (42%)
  starting transfers between devices  30.4 us (36%)
  Pallas kernels  11.7 us (14%)
  local copies, waits for them, and re-layouts  5.63 us (7%)
    ppermute x25, waiting for transfers between devices, swap(): return lax.ppermute(array, axis, [(i, i ^ mask) for i in range(size)])  33.5 us
    ppermute x25, starting transfers between devices, swap(): return lax.ppermute(array, axis, [(i, i ^ mask) for i in range(size)])  25.3 us
    unnamed x26, local copies, waits for them, and re-layouts  5.58 us
    all_to_all x1, starting transfers between devices, owners_blocks(): lax.all_to_all(blocks, 'tensor', split_axis=0, concat_axis=0, tiled=True)  5.09 us
    pallas_call x1, Pallas kernels, shards(): pl.pallas_call(functools.partial(attend_kernel, joined_pieces), name='att...  3.79 us
    pallas_call x1, Pallas kernels, shards(): pl.pallas_call(functools.partial(layer_kernel, forward_pieces, ways), nam...  3.5 us
    pallas_call x1, Pallas kernels, shards(): pl.pallas_call(cut_kernel, name='cut', out_shape=[jax.ShapeDtypeStruct((t...  2.47 us
    all_to_all x1, waiting for transfers between devices, owners_blocks(): lax.all_to_all(blocks, 'tensor', split_axis=0, concat_axis=0, tiled=True)  2.18 us
  transfers between devices with their start and end apart: 26, of which 13 were waited for; matrix products, arithmetic and copies ran while one was open for 0% of the time, Pallas kernels for 7%

profile of v4, /device:TPU:0, one launch (start us, length us, event | category | flops | bytes accessed | tf_op | source)
XLA Modules:
  0.0 84.3 jit_solution(7292759701705519782)
XLA Ops:
  0.0 2.5 %cut.1 = (bf16[32,768]{1,0:T(8,128)(2,1)}, bf16[32,768]{1,0:T(8,128)(2,1)}, bf16[32,768]{1,0:T(8,128)(2,1)}, bf16[32,768]{1,0:T(8,128)(2,1)}, bf16[4,32,3072]{2,1,0:T(8,128)(2,1)}) custom-call(f32[32,3072]{1,0:T(8,128)} %refs_0_.1, f32[32,1024]{1,0:T(8,128)} %refs_1_.1, f32[32,4096]{1,0:T(8,128)} %refs_2_.1, f32[32,4096]{1,0:T(8,128)} %refs_3_.1), custom_call_target="tpu_custom_call" | custom-call | tf_op jit(solution)/shard_map/cut/pallas_call | solution.py:293
  2.5 3.1 %collective-permute-start = (bf16[32,768]{1,0:T(8,128)(2,1)}, bf16[32,768]{1,0:T(8,128)(2,1)S(1)}, u32[]{:S(2)}, u32[]{:S(2)}) collective-permute-start(bf16[32,768]{1,0:T(8,128)(2,1)} %get-tuple-element.23), channel_id=1, source_target_pairs={{0,1},{1,0},{2,3},{3,2},{4,5},{5,4},{6,7},{7,6},{8,9},{9,8},{10,11... | collective-permute-start | bytes 147464 | tf_op jit(solution)/shard_map/ppermute | solution.py:34
  5.6 2.6 %collective-permute-start.1 = (bf16[32,768]{1,0:T(8,128)(2,1)}, bf16[32,768]{1,0:T(8,128)(2,1)S(1)}, u32[]{:S(2)}, u32[]{:S(2)}) collective-permute-start(bf16[32,768]{1,0:T(8,128)(2,1)} %get-tuple-element.24), channel_id=1, source_target_pairs={{0,2},{1,3},{2,0},{3,1},{4,6},{5,7},{6,4},{7,5},{8,10},{9,11},{10,... | collective-permute-start | bytes 147464 | tf_op jit(solution)/shard_map/ppermute | solution.py:34
  8.2 5.1 %all-to-all-start = ((bf16[4,32,3072]{2,1,0:T(8,128)(2,1)}), bf16[4,32,3072]{2,1,0:T(8,128)(2,1)S(1)}, u32[]{:S(2)}, u32[]{:S(2)}) async-start(bf16[4,32,3072]{2,1,0:T(8,128)(2,1)} %get-tuple-element.28), calls=%async_computation | async-start | bytes 1572864 | tf_op jit(solution)/shard_map/all_to_all | solution.py:260
  14.2 1.6 %prepare.1 = (bf16[256,1024]{1,0:T(8,128)(2,1)S(1)}, f32[4,256,512]{2,1,0:T(8,128)S(1)}) custom-call(bf16[32,768]{1,0:T(8,128)(2,1)S(1)} %copy-done, s32[8]{0:T(128)S(1)} %copy-done.8, s32[8]{0:T(128)S(1)} %copy-done.9, s32[8]{0:T(128)S(1)} %copy-done.10, bf16[256,1024]{1,0:T(8,128)(2,1)S(1)} %copy-done.1, f32[1,1024]{1,0:T(1,128)S(1)} %bitcast.4, ...), custom_call_target="tpu_custom_call" | custom-call | flops 20000000000 | bytes 4000000 | tf_op jit(solution)/shard_map/prepare/pallas_call | solution.py:306
  15.8 1.4 %copy-done.11 = f32[4,256,512]{2,1,0:T(8,128)} copy-done((f32[4,256,512]{2,1,0:T(8,128)}, f32[4,256,512]{2,1,0:T(8,128)S(1)}, u32[]{:S(2)}) %copy-start.11) | copy-done | bytes 2097176
  17.5 1.6 %collective-permute-start.3 = (bf16[4,32,768]{2,1,0:T(8,128)(2,1)S(1)}, bf16[4,32,768]{2,1,0:T(8,128)(2,1)S(1)}, u32[]{:S(2)}, u32[]{:S(2)}) collective-permute-start(bf16[4,32,768]{2,1,0:T(8,128)(2,1)S(1)} %stack.1.refs_0_), channel_id=1, source_target_pairs={{0,16},{4,20},{8,24},{12,28},{16,0},{20,4},{24,8},{28,12},{1,17},{... | collective-permute-start | bytes 589832 | tf_op jit(solution)/shard_map/ppermute | solution.py:34
  19.0 1.5 %collective-permute-start.4 = (bf16[4,32,768]{2,1,0:T(8,128)(2,1)S(1)}, bf16[4,32,768]{2,1,0:T(8,128)(2,1)S(1)}, u32[]{:S(2)}, u32[]{:S(2)}) collective-permute-start(bf16[4,32,768]{2,1,0:T(8,128)(2,1)S(1)} %stack.1.refs_0_), channel_id=1, source_target_pairs={{0,8},{4,12},{8,0},{12,4},{16,24},{20,28},{24,16},{28,20},{1,9},{5... | collective-permute-start | bytes 589832 | tf_op jit(solution)/shard_map/ppermute | solution.py:34
  20.5 2.7 %collective-permute-done.3.refs_1_ = bf16[4,32,768]{2,1,0:T(8,128)(2,1)S(1)} collective-permute-done((bf16[4,32,768]{2,1,0:T(8,128)(2,1)S(1)}, bf16[4,32,768]{2,1,0:T(8,128)(2,1)S(1)}, u32[]{:S(2)}, u32[]{:S(2)}) %collective-permute-start.3) | collective-permute-done | bytes 196640 | tf_op jit(solution)/shard_map/ppermute | solution.py:34
  23.2 1.5 %collective-permute-done.4.refs_2_ = bf16[4,32,768]{2,1,0:T(8,128)(2,1)S(1)} collective-permute-done((bf16[4,32,768]{2,1,0:T(8,128)(2,1)S(1)}, bf16[4,32,768]{2,1,0:T(8,128)(2,1)S(1)}, u32[]{:S(2)}, u32[]{:S(2)}) %collective-permute-start.4) | collective-permute-done | bytes 196640 | tf_op jit(solution)/shard_map/ppermute | solution.py:34
  24.7 1.5 %collective-permute-start.5 = (bf16[4,32,768]{2,1,0:T(8,128)(2,1)S(1)}, bf16[4,32,768]{2,1,0:T(8,128)(2,1)S(1)}, u32[]{:S(2)}, u32[]{:S(2)}) collective-permute-start(bf16[4,32,768]{2,1,0:T(8,128)(2,1)S(1)} %collective-permute-done.3.refs_1_), channel_id=1, source_target_pairs={{0,8},{4,12},{8,0},{12,4},{16,24},{20,28},{24,16},{28,20},{1,9},{5... | collective-permute-start | bytes 589832 | tf_op jit(solution)/shard_map/ppermute | solution.py:34
  26.7 3.7 %collective-permute-done.5.refs_3_ = bf16[4,32,768]{2,1,0:T(8,128)(2,1)S(1)} collective-permute-done((bf16[4,32,768]{2,1,0:T(8,128)(2,1)S(1)}, bf16[4,32,768]{2,1,0:T(8,128)(2,1)S(1)}, u32[]{:S(2)}, u32[]{:S(2)}) %collective-permute-start.5) | collective-permute-done | bytes 196640 | tf_op jit(solution)/shard_map/ppermute | solution.py:34
  30.4 2.2 %all-to-all-done.refs_4_ = bf16[4,32,3072]{2,1,0:T(8,128)(2,1)S(1)} async-done(((bf16[4,32,3072]{2,1,0:T(8,128)(2,1)}), bf16[4,32,3072]{2,1,0:T(8,128)(2,1)S(1)}, u32[]{:S(2)}, u32[]{:S(2)}) %all-to-all-start) | async-done | bytes 786464 | tf_op jit(solution)/shard_map/all_to_all | solution.py:260
  32.6 1.5 %collective-permute-start.13 = (bf16[4,32,3072]{2,1,0:T(8,128)(2,1)S(1)}, bf16[4,32,3072]{2,1,0:T(8,128)(2,1)S(1)}, u32[]{:S(2)}, u32[]{:S(2)}) collective-permute-start(bf16[4,32,3072]{2,1,0:T(8,128)(2,1)S(1)} %all-to-all-done.refs_4_), channel_id=1, source_target_pairs={{0,16},{4,20},{8,24},{12,28},{16,0},{20,4},{24,8},{28,12},{1,17},{... | collective-permute-start | bytes 2359304 | tf_op jit(solution)/shard_map/ppermute | solution.py:34
  34.1 1.5 %collective-permute-start.14 = (bf16[4,32,3072]{2,1,0:T(8,128)(2,1)S(1)}, bf16[4,32,3072]{2,1,0:T(8,128)(2,1)S(1)}, u32[]{:S(2)}, u32[]{:S(2)}) collective-permute-start(bf16[4,32,3072]{2,1,0:T(8,128)(2,1)S(1)} %all-to-all-done.refs_4_), channel_id=1, source_target_pairs={{0,8},{4,12},{8,0},{12,4},{16,24},{20,28},{24,16},{28,20},{1,9},{5... | collective-permute-start | bytes 2359304 | tf_op jit(solution)/shard_map/ppermute | solution.py:34
  35.6 0.9 %copy-done.2 = bf16[256,256]{1,0:T(8,128)(2,1)S(1)} copy-done((bf16[256,256]{1,0:T(8,128)(2,1)S(1)}, bf16[256,256]{1,0:T(8,128)(2,1)}, u32[]{:S(2)}) %copy-start.2) | copy-done | bytes 131096
  36.5 0.9 %copy-done.3 = bf16[256,256]{1,0:T(8,128)(2,1)S(1)} copy-done((bf16[256,256]{1,0:T(8,128)(2,1)S(1)}, bf16[256,256]{1,0:T(8,128)(2,1)}, u32[]{:S(2)}) %copy-start.3) | copy-done | bytes 131096
  37.4 1.6 %copy-done.12 = f32[4,256,512]{2,1,0:T(8,128)S(1)} copy-done((f32[4,256,512]{2,1,0:T(8,128)S(1)}, f32[4,256,512]{2,1,0:T(8,128)}, u32[]{:S(2)}) %copy-start.12) | copy-done | bytes 2097176
  39.0 3.8 %attend.1.refs_0_ = bf16[256,256]{1,0:T(8,128)(2,1)S(1)} custom-call(bf16[256,1024]{1,0:T(8,128)(2,1)S(1)} %get-tuple-element.21.refs_4_.normed, bf16[256,256]{1,0:T(8,128)(2,1)S(1)} %copy-done.2, bf16[256,256]{1,0:T(8,128)(2,1)S(1)} %copy-done.3, f32[4,256,512]{2,1,0:T(8,128)S(1)} %copy-done.12, bf16[4,32,768]{2,1,0:T(8,128)(2,1)S(1)} %stack.1.refs_0_, ...), custom_call_target="tpu_custom_call" | custom-call | flops 20000000000 | bytes 6000000 | tf_op jit(solution)/shard_map/attend/pallas_call | solution.py:345
  42.9 2.0 %collective-permute-start.11 = (bf16[256,256]{1,0:T(8,128)(2,1)S(1)}, bf16[256,256]{1,0:T(8,128)(2,1)S(1)}, u32[]{:S(2)}, u32[]{:S(2)}) collective-permute-start(bf16[256,256]{1,0:T(8,128)(2,1)S(1)} %attend.1.refs_0_), channel_id=1, source_target_pairs={{0,2},{1,3},{2,0},{3,1},{4,6},{5,7},{6,4},{7,5},{8,10},{9,11},{10,... | collective-permute-start | bytes 393224 | tf_op jit(solution)/shard_map/ppermute | solution.py:34
  44.9 2.4 %collective-permute-start.12 = (bf16[256,256]{1,0:T(8,128)(2,1)S(1)}, bf16[256,256]{1,0:T(8,128)(2,1)S(1)}, u32[]{:S(2)}, u32[]{:S(2)}) collective-permute-start(bf16[256,256]{1,0:T(8,128)(2,1)S(1)} %attend.1.refs_0_), channel_id=1, source_target_pairs={{0,3},{1,2},{2,1},{3,0},{4,7},{5,6},{6,5},{7,4},{8,11},{9,10},{10,... | collective-permute-start | bytes 393224 | tf_op jit(solution)/shard_map/ppermute | solution.py:34
  47.3 3.8 %collective-permute-done.13.refs_5_ = bf16[4,32,3072]{2,1,0:T(8,128)(2,1)S(1)} collective-permute-done((bf16[4,32,3072]{2,1,0:T(8,128)(2,1)S(1)}, bf16[4,32,3072]{2,1,0:T(8,128)(2,1)S(1)}, u32[]{:S(2)}, u32[]{:S(2)}) %collective-permute-start.13) | collective-permute-done | bytes 786464 | tf_op jit(solution)/shard_map/ppermute | solution.py:34
  51.1 1.2 %collective-permute-done.14.refs_6_ = bf16[4,32,3072]{2,1,0:T(8,128)(2,1)S(1)} collective-permute-done((bf16[4,32,3072]{2,1,0:T(8,128)(2,1)S(1)}, bf16[4,32,3072]{2,1,0:T(8,128)(2,1)S(1)}, u32[]{:S(2)}, u32[]{:S(2)}) %collective-permute-start.14) | collective-permute-done | bytes 786464 | tf_op jit(solution)/shard_map/ppermute | solution.py:34
  52.3 1.6 %collective-permute-start.15 = (bf16[2,32,3072]{2,1,0:T(8,128)(2,1)S(1)}, bf16[2,32,3072]{2,1,0:T(8,128)(2,1)S(1)}, u32[]{:S(2)}, u32[]{:S(2)}) collective-permute-start(bf16[2,32,3072]{2,1,0:T(8,128)(2,1)S(1)} %slice.6), channel_id=1, source_target_pairs={{0,8},{4,12},{8,0},{12,4},{16,24},{20,28},{24,16},{28,20},{1,9},{5... | collective-permute-start | bytes 1179656 | tf_op jit(solution)/shard_map/ppermute | solution.py:34
  55.3 7.4 %collective-permute-done.15.refs_7_ = bf16[2,32,3072]{2,1,0:T(8,128)(2,1)S(1)} collective-permute-done((bf16[2,32,3072]{2,1,0:T(8,128)(2,1)S(1)}, bf16[2,32,3072]{2,1,0:T(8,128)(2,1)S(1)}, u32[]{:S(2)}, u32[]{:S(2)}) %collective-permute-start.15) | collective-permute-done | bytes 393248 | tf_op jit(solution)/shard_map/ppermute | solution.py:34
  62.7 1.3 %collective-permute-done.16.refs_8_ = bf16[2,32,3072]{2,1,0:T(8,128)(2,1)S(1)} collective-permute-done((bf16[2,32,3072]{2,1,0:T(8,128)(2,1)S(1)}, bf16[2,32,3072]{2,1,0:T(8,128)(2,1)S(1)}, u32[]{:S(2)}, u32[]{:S(2)}) %collective-permute-start.16) | collective-permute-done | bytes 393248 | tf_op jit(solution)/shard_map/ppermute | solution.py:34
  64.4 1.3 %collective-permute-done.21.refs_13_ = bf16[2,32,3072]{2,1,0:T(8,128)(2,1)S(1)} collective-permute-done((bf16[2,32,3072]{2,1,0:T(8,128)(2,1)S(1)}, bf16[2,32,3072]{2,1,0:T(8,128)(2,1)S(1)}, u32[]{:S(2)}, u32[]{:S(2)}) %collective-permute-start.21) | collective-permute-done | bytes 393248 | tf_op jit(solution)/shard_map/ppermute | solution.py:34
  65.8 3.5 %layer.1 = (f32[64,1024]{1,0:T(8,128)S(1)}, bf16[64,1024]{1,0:T(8,128)(2,1)S(1)}, bf16[64,1024]{1,0:T(8,128)(2,1)S(1)}, bf16[64,1024]{1,0:T(8,128)(2,1)S(1)}) custom-call(bf16[256,1024]{1,0:T(8,128)(2,1)S(1)} %copy-done.1, f32[1,1024]{1,0:T(1,128)S(1)} %bitcast.6, bf16[256,256]{1,0:T(8,128)(2,1)S(1)} %attend.1.refs_0_, ...), custom_call_target="tpu_custom_call" | custom-call | flops 2000000000 | bytes 8000000 | tf_op jit(solution)/shard_map/layer/pallas_call | solution.py:362
  69.3 1.4 %collective-permute-start.22 = (bf16[64,1024]{1,0:T(8,128)(2,1)S(1)}, bf16[64,1024]{1,0:T(8,128)(2,1)S(1)}, u32[]{:S(2)}, u32[]{:S(2)}) collective-permute-start(bf16[64,1024]{1,0:T(8,128)(2,1)S(1)} %get-tuple-element.32), channel_id=1, source_target_pairs={{0,1},{1,0},{2,3},{3,2},{4,5},{5,4},{6,7},{7,6},{8,9},{9,8},{10,11... | collective-permute-start | bytes 393224 | tf_op jit(solution)/shard_map/ppermute | solution.py:34
  70.7 2.4 %collective-permute-start.23 = (bf16[64,1024]{1,0:T(8,128)(2,1)S(1)}, bf16[64,1024]{1,0:T(8,128)(2,1)S(1)}, u32[]{:S(2)}, u32[]{:S(2)}) collective-permute-start(bf16[64,1024]{1,0:T(8,128)(2,1)S(1)} %get-tuple-element.33), channel_id=1, source_target_pairs={{0,2},{1,3},{2,0},{3,1},{4,6},{5,7},{6,4},{7,5},{8,10},{9,11},{10,... | collective-permute-start | bytes 393224 | tf_op jit(solution)/shard_map/ppermute | solution.py:34
  73.7 3.1 %collective-permute-done.22 = bf16[64,1024]{1,0:T(8,128)(2,1)S(1)} collective-permute-done((bf16[64,1024]{1,0:T(8,128)(2,1)S(1)}, bf16[64,1024]{1,0:T(8,128)(2,1)S(1)}, u32[]{:S(2)}, u32[]{:S(2)}) %collective-permute-start.22) | collective-permute-done | bytes 131104 | tf_op jit(solution)/shard_map/ppermute | solution.py:34
  76.8 6.7 %collective-permute-done.23 = bf16[64,1024]{1,0:T(8,128)(2,1)S(1)} collective-permute-done((bf16[64,1024]{1,0:T(8,128)(2,1)S(1)}, bf16[64,1024]{1,0:T(8,128)(2,1)S(1)}, u32[]{:S(2)}, u32[]{:S(2)}) %collective-permute-start.23) | collective-permute-done | bytes 131104 | tf_op jit(solution)/shard_map/ppermute | solution.py:34
  (54 shorter events, 5.0 us)
Async XLA Ops:
  0.0 13.3 %copy-start.5 = (s32[1023]{0:T(1024)S(1)}, s32[1023]{0:T(1024)}, u32[]{:S(2)}) copy-start(s32[1023]{0:T(1024)} %param.24) | copy-start | bytes 12280
  0.0 13.3 %copy-start.1 = (bf16[256,1024]{1,0:T(8,128)(2,1)S(1)}, bf16[256,1024]{1,0:T(8,128)(2,1)}, u32[]{:S(2)}) copy-start(bf16[256,1024]{1,0:T(8,128)(2,1)} %tokens.3) | copy-start | bytes 1572868
  0.0 13.3 %copy-start.8 = (s32[8]{0:T(128)S(1)}, s32[8]{0:T(128)}, u32[]{:S(2)}) copy-start(s32[8]{0:T(128)} %lengths.1) | copy-start | bytes 100
  0.0 13.3 %copy-start.10 = (s32[8]{0:T(128)S(1)}, s32[8]{0:T(128)}, u32[]{:S(2)}) copy-start(s32[8]{0:T(128)} %counts.1) | copy-start | bytes 100
  0.0 13.3 %copy-start.9 = (s32[8]{0:T(128)S(1)}, s32[8]{0:T(128)}, u32[]{:S(2)}) copy-start(s32[8]{0:T(128)} %flags.1) | copy-start | bytes 100
  2.5 14.6 %collective-permute-start = (bf16[32,768]{1,0:T(8,128)(2,1)}, bf16[32,768]{1,0:T(8,128)(2,1)S(1)}, u32[]{:S(2)}, u32[]{:S(2)}) collective-permute-start(bf16[32,768]{1,0:T(8,128)(2,1)} %get-tuple-element.23), channel_id=1, source_target_pairs={{0,1},{1,0},{2,3},{3,2},{4,5},{5,4},{6,7},{7,6},{8,9},{9,8},{10,11... | collective-permute-start | bytes 147464 | tf_op jit(solution)/shard_map/ppermute | solution.py:34
  5.6 11.5 %collective-permute-start.1 = (bf16[32,768]{1,0:T(8,128)(2,1)}, bf16[32,768]{1,0:T(8,128)(2,1)S(1)}, u32[]{:S(2)}, u32[]{:S(2)}) collective-permute-start(bf16[32,768]{1,0:T(8,128)(2,1)} %get-tuple-element.24), channel_id=1, source_target_pairs={{0,2},{1,3},{2,0},{3,1},{4,6},{5,7},{6,4},{7,5},{8,10},{9,11},{10,... | collective-permute-start | bytes 147464 | tf_op jit(solution)/shard_map/ppermute | solution.py:34
  8.2 8.9 %collective-permute-start.2 = (bf16[32,768]{1,0:T(8,128)(2,1)}, bf16[32,768]{1,0:T(8,128)(2,1)S(1)}, u32[]{:S(2)}, u32[]{:S(2)}) collective-permute-start(bf16[32,768]{1,0:T(8,128)(2,1)} %get-tuple-element.25), channel_id=1, source_target_pairs={{0,3},{1,2},{2,1},{3,0},{4,7},{5,6},{6,5},{7,4},{8,11},{9,10},{10,... | collective-permute-start | bytes 147464 | tf_op jit(solution)/shard_map/ppermute | solution.py:34
  8.2 24.4 %all-to-all-start = ((bf16[4,32,3072]{2,1,0:T(8,128)(2,1)}), bf16[4,32,3072]{2,1,0:T(8,128)(2,1)S(1)}, u32[]{:S(2)}, u32[]{:S(2)}) async-start(bf16[4,32,3072]{2,1,0:T(8,128)(2,1)} %get-tuple-element.28), calls=%async_computation | async-start | bytes 1572864 | tf_op jit(solution)/shard_map/all_to_all | solution.py:260
  17.5 5.7 %collective-permute-start.3 = (bf16[4,32,768]{2,1,0:T(8,128)(2,1)S(1)}, bf16[4,32,768]{2,1,0:T(8,128)(2,1)S(1)}, u32[]{:S(2)}, u32[]{:S(2)}) collective-permute-start(bf16[4,32,768]{2,1,0:T(8,128)(2,1)S(1)} %stack.1.refs_0_), channel_id=1, source_target_pairs={{0,16},{4,20},{8,24},{12,28},{16,0},{20,4},{24,8},{28,12},{1,17},{... | collective-permute-start | bytes 589832 | tf_op jit(solution)/shard_map/ppermute | solution.py:34
  19.0 5.7 %collective-permute-start.4 = (bf16[4,32,768]{2,1,0:T(8,128)(2,1)S(1)}, bf16[4,32,768]{2,1,0:T(8,128)(2,1)S(1)}, u32[]{:S(2)}, u32[]{:S(2)}) collective-permute-start(bf16[4,32,768]{2,1,0:T(8,128)(2,1)S(1)} %stack.1.refs_0_), channel_id=1, source_target_pairs={{0,8},{4,12},{8,0},{12,4},{16,24},{20,28},{24,16},{28,20},{1,9},{5... | collective-permute-start | bytes 589832 | tf_op jit(solution)/shard_map/ppermute | solution.py:34
  24.7 5.7 %collective-permute-start.5 = (bf16[4,32,768]{2,1,0:T(8,128)(2,1)S(1)}, bf16[4,32,768]{2,1,0:T(8,128)(2,1)S(1)}, u32[]{:S(2)}, u32[]{:S(2)}) collective-permute-start(bf16[4,32,768]{2,1,0:T(8,128)(2,1)S(1)} %collective-permute-done.3.refs_1_), channel_id=1, source_target_pairs={{0,8},{4,12},{8,0},{12,4},{16,24},{20,28},{24,16},{28,20},{1,9},{5... | collective-permute-start | bytes 589832 | tf_op jit(solution)/shard_map/ppermute | solution.py:34
  26.2 7.9 %collective-permute-start.6 = (bf16[4,32,768]{2,1,0:T(8,128)(2,1)S(1)}, bf16[4,32,768]{2,1,0:T(8,128)(2,1)S(1)}, u32[]{:S(2)}, u32[]{:S(2)}) collective-permute-start(bf16[4,32,768]{2,1,0:T(8,128)(2,1)S(1)} %stack.1.refs_0_), channel_id=1, source_target_pairs={{0,4},{4,0},{8,12},{12,8},{16,20},{20,16},{24,28},{28,24},{1,5},{5... | collective-permute-start | bytes 589832 | tf_op jit(solution)/shard_map/ppermute | solution.py:34
  26.2 9.4 %collective-permute-start.7 = (bf16[4,32,768]{2,1,0:T(8,128)(2,1)S(1)}, bf16[4,32,768]{2,1,0:T(8,128)(2,1)S(1)}, u32[]{:S(2)}, u32[]{:S(2)}) collective-permute-start(bf16[4,32,768]{2,1,0:T(8,128)(2,1)S(1)} %collective-permute-done.3.refs_1_), channel_id=1, source_target_pairs={{0,4},{4,0},{8,12},{12,8},{16,20},{20,16},{24,28},{28,24},{1,5},{5... | collective-permute-start | bytes 589832 | tf_op jit(solution)/shard_map/ppermute | solution.py:34
  26.7 8.9 %collective-permute-start.8 = (bf16[4,32,768]{2,1,0:T(8,128)(2,1)S(1)}, bf16[4,32,768]{2,1,0:T(8,128)(2,1)S(1)}, u32[]{:S(2)}, u32[]{:S(2)}) collective-permute-start(bf16[4,32,768]{2,1,0:T(8,128)(2,1)S(1)} %collective-permute-done.4.refs_2_), channel_id=1, source_target_pairs={{0,4},{4,0},{8,12},{12,8},{16,20},{20,16},{24,28},{28,24},{1,5},{5... | collective-permute-start | bytes 589832 | tf_op jit(solution)/shard_map/ppermute | solution.py:34
  30.4 5.2 %collective-permute-start.9 = (bf16[4,32,768]{2,1,0:T(8,128)(2,1)S(1)}, bf16[4,32,768]{2,1,0:T(8,128)(2,1)S(1)}, u32[]{:S(2)}, u32[]{:S(2)}) collective-permute-start(bf16[4,32,768]{2,1,0:T(8,128)(2,1)S(1)} %collective-permute-done.5.refs_3_), channel_id=1, source_target_pairs={{0,4},{4,0},{8,12},{12,8},{16,20},{20,16},{24,28},{28,24},{1,5},{5... | collective-permute-start | bytes 589832 | tf_op jit(solution)/shard_map/ppermute | solution.py:34
  32.6 18.5 %collective-permute-start.13 = (bf16[4,32,3072]{2,1,0:T(8,128)(2,1)S(1)}, bf16[4,32,3072]{2,1,0:T(8,128)(2,1)S(1)}, u32[]{:S(2)}, u32[]{:S(2)}) collective-permute-start(bf16[4,32,3072]{2,1,0:T(8,128)(2,1)S(1)} %all-to-all-done.refs_4_), channel_id=1, source_target_pairs={{0,16},{4,20},{8,24},{12,28},{16,0},{20,4},{24,8},{28,12},{1,17},{... | collective-permute-start | bytes 2359304 | tf_op jit(solution)/shard_map/ppermute | solution.py:34
  34.1 18.2 %collective-permute-start.14 = (bf16[4,32,3072]{2,1,0:T(8,128)(2,1)S(1)}, bf16[4,32,3072]{2,1,0:T(8,128)(2,1)S(1)}, u32[]{:S(2)}, u32[]{:S(2)}) collective-permute-start(bf16[4,32,3072]{2,1,0:T(8,128)(2,1)S(1)} %all-to-all-done.refs_4_), channel_id=1, source_target_pairs={{0,8},{4,12},{8,0},{12,4},{16,24},{20,28},{24,16},{28,20},{1,9},{5... | collective-permute-start | bytes 2359304 | tf_op jit(solution)/shard_map/ppermute | solution.py:34
  39.0 26.7 %copy-start.6 = (f32[1024]{0:T(1024)S(1)}, f32[1024]{0:T(1024)}, u32[]{:S(2)}) copy-start(f32[1024]{0:T(1024)} %param.22) | copy-start | bytes 12292
  42.8 11.1 %collective-permute-start.10 = (bf16[256,256]{1,0:T(8,128)(2,1)S(1)}, bf16[256,256]{1,0:T(8,128)(2,1)S(1)}, u32[]{:S(2)}, u32[]{:S(2)}) collective-permute-start(bf16[256,256]{1,0:T(8,128)(2,1)S(1)} %attend.1.refs_0_), channel_id=1, source_target_pairs={{0,1},{1,0},{2,3},{3,2},{4,5},{5,4},{6,7},{7,6},{8,9},{9,8},{10,11... | collective-permute-start | bytes 393224 | tf_op jit(solution)/shard_map/ppermute | solution.py:34
  42.9 11.9 %collective-permute-start.11 = (bf16[256,256]{1,0:T(8,128)(2,1)S(1)}, bf16[256,256]{1,0:T(8,128)(2,1)S(1)}, u32[]{:S(2)}, u32[]{:S(2)}) collective-permute-start(bf16[256,256]{1,0:T(8,128)(2,1)S(1)} %attend.1.refs_0_), channel_id=1, source_target_pairs={{0,2},{1,3},{2,0},{3,1},{4,6},{5,7},{6,4},{7,5},{8,10},{9,11},{10,... | collective-permute-start | bytes 393224 | tf_op jit(solution)/shard_map/ppermute | solution.py:34
  44.9 9.9 %collective-permute-start.12 = (bf16[256,256]{1,0:T(8,128)(2,1)S(1)}, bf16[256,256]{1,0:T(8,128)(2,1)S(1)}, u32[]{:S(2)}, u32[]{:S(2)}) collective-permute-start(bf16[256,256]{1,0:T(8,128)(2,1)S(1)} %attend.1.refs_0_), channel_id=1, source_target_pairs={{0,3},{1,2},{2,1},{3,0},{4,7},{5,6},{6,5},{7,4},{8,11},{9,10},{10,... | collective-permute-start | bytes 393224 | tf_op jit(solution)/shard_map/ppermute | solution.py:34
  51.1 13.0 %collective-permute-start.17 = (bf16[4,32,3072]{2,1,0:T(8,128)(2,1)S(1)}, bf16[4,32,3072]{2,1,0:T(8,128)(2,1)S(1)}, u32[]{:S(2)}, u32[]{:S(2)}) collective-permute-start(bf16[4,32,3072]{2,1,0:T(8,128)(2,1)S(1)} %all-to-all-done.refs_4_), channel_id=1, source_target_pairs={{0,4},{4,0},{8,12},{12,8},{16,20},{20,16},{24,28},{28,24},{1,5},{5... | collective-permute-start | bytes 2359304 | tf_op jit(solution)/shard_map/ppermute | solution.py:34
  52.3 10.4 %collective-permute-start.15 = (bf16[2,32,3072]{2,1,0:T(8,128)(2,1)S(1)}, bf16[2,32,3072]{2,1,0:T(8,128)(2,1)S(1)}, u32[]{:S(2)}, u32[]{:S(2)}) collective-permute-start(bf16[2,32,3072]{2,1,0:T(8,128)(2,1)S(1)} %slice.6), channel_id=1, source_target_pairs={{0,8},{4,12},{8,0},{12,4},{16,24},{20,28},{24,16},{28,20},{1,9},{5... | collective-permute-start | bytes 1179656 | tf_op jit(solution)/shard_map/ppermute | solution.py:34
  53.9 10.1 %collective-permute-start.16 = (bf16[2,32,3072]{2,1,0:T(8,128)(2,1)S(1)}, bf16[2,32,3072]{2,1,0:T(8,128)(2,1)S(1)}, u32[]{:S(2)}, u32[]{:S(2)}) collective-permute-start(bf16[2,32,3072]{2,1,0:T(8,128)(2,1)S(1)} %slice.7), channel_id=1, source_target_pairs={{0,16},{4,20},{8,24},{12,28},{16,0},{20,4},{24,8},{28,12},{1,17},{... | collective-permute-start | bytes 1179656 | tf_op jit(solution)/shard_map/ppermute | solution.py:34
  54.8 10.9 %collective-permute-start.18 = (bf16[4,32,3072]{2,1,0:T(8,128)(2,1)S(1)}, bf16[4,32,3072]{2,1,0:T(8,128)(2,1)S(1)}, u32[]{:S(2)}, u32[]{:S(2)}) collective-permute-start(bf16[4,32,3072]{2,1,0:T(8,128)(2,1)S(1)} %collective-permute-done.13.refs_5_), channel_id=1, source_target_pairs={{0,4},{4,0},{8,12},{12,8},{16,20},{20,16},{24,28},{28,24},{1,5},{5... | collective-permute-start | bytes 2359304 | tf_op jit(solution)/shard_map/ppermute | solution.py:34
  54.8 10.9 %collective-permute-start.19 = (bf16[4,32,3072]{2,1,0:T(8,128)(2,1)S(1)}, bf16[4,32,3072]{2,1,0:T(8,128)(2,1)S(1)}, u32[]{:S(2)}, u32[]{:S(2)}) collective-permute-start(bf16[4,32,3072]{2,1,0:T(8,128)(2,1)S(1)} %collective-permute-done.14.refs_6_), channel_id=1, source_target_pairs={{0,4},{4,0},{8,12},{12,8},{16,20},{20,16},{24,28},{28,24},{1,5},{5... | collective-permute-start | bytes 2359304 | tf_op jit(solution)/shard_map/ppermute | solution.py:34
  62.7 1.7 %collective-permute-start.20 = (bf16[2,32,3072]{2,1,0:T(8,128)(2,1)S(1)}, bf16[2,32,3072]{2,1,0:T(8,128)(2,1)S(1)}, u32[]{:S(2)}, u32[]{:S(2)}) collective-permute-start(bf16[2,32,3072]{2,1,0:T(8,128)(2,1)S(1)} %collective-permute-done.15.refs_7_), channel_id=1, source_target_pairs={{0,4},{4,0},{8,12},{12,8},{16,20},{20,16},{24,28},{28,24},{1,5},{5... | collective-permute-start | bytes 1179656 | tf_op jit(solution)/shard_map/ppermute | solution.py:34
  64.0 1.7 %collective-permute-start.21 = (bf16[2,32,3072]{2,1,0:T(8,128)(2,1)S(1)}, bf16[2,32,3072]{2,1,0:T(8,128)(2,1)S(1)}, u32[]{:S(2)}, u32[]{:S(2)}) collective-permute-start(bf16[2,32,3072]{2,1,0:T(8,128)(2,1)S(1)} %collective-permute-done.16.refs_8_), channel_id=1, source_target_pairs={{0,4},{4,0},{8,12},{12,8},{16,20},{20,16},{24,28},{28,24},{1,5},{5... | collective-permute-start | bytes 1179656 | tf_op jit(solution)/shard_map/ppermute | solution.py:34
  69.3 7.6 %collective-permute-start.22 = (bf16[64,1024]{1,0:T(8,128)(2,1)S(1)}, bf16[64,1024]{1,0:T(8,128)(2,1)S(1)}, u32[]{:S(2)}, u32[]{:S(2)}) collective-permute-start(bf16[64,1024]{1,0:T(8,128)(2,1)S(1)} %get-tuple-element.32), channel_id=1, source_target_pairs={{0,1},{1,0},{2,3},{3,2},{4,5},{5,4},{6,7},{7,6},{8,9},{9,8},{10,11... | collective-permute-start | bytes 393224 | tf_op jit(solution)/shard_map/ppermute | solution.py:34
  70.7 12.9 %collective-permute-start.23 = (bf16[64,1024]{1,0:T(8,128)(2,1)S(1)}, bf16[64,1024]{1,0:T(8,128)(2,1)S(1)}, u32[]{:S(2)}, u32[]{:S(2)}) collective-permute-start(bf16[64,1024]{1,0:T(8,128)(2,1)S(1)} %get-tuple-element.33), channel_id=1, source_target_pairs={{0,2},{1,3},{2,0},{3,1},{4,6},{5,7},{6,4},{7,5},{8,10},{9,11},{10,... | collective-permute-start | bytes 393224 | tf_op jit(solution)/shard_map/ppermute | solution.py:34
  73.0 10.5 %collective-permute-start.24 = (bf16[64,1024]{1,0:T(8,128)(2,1)S(1)}, bf16[64,1024]{1,0:T(8,128)(2,1)S(1)}, u32[]{:S(2)}, u32[]{:S(2)}) collective-permute-start(bf16[64,1024]{1,0:T(8,128)(2,1)S(1)} %get-tuple-element.34), channel_id=1, source_target_pairs={{0,3},{1,2},{2,1},{3,0},{4,7},{5,6},{6,5},{7,4},{8,11},{9,10},{10,... | collective-permute-start | bytes 393224 | tf_op jit(solution)/shard_map/ppermute | solution.py:34
  (7 other events, 32.2 us)

commit v5 on v4

--- a/solution.py
+++ b/solution.py
@@ -332,8 +332,8 @@
 
     if places == 8:
         lead = (places, ways, trainer_rows)
-        joined = stack(joined_blocks, normed)
-        near, far = first_hops(joined)
+        joined = stack(joined_blocks)
+        near, far, normed = together(*first_hops(joined), normed)
         held = whole_hop(joined, near, far)
         joined_pieces, joined_all = with_cores(held)
     else:

time: 84.6 us -> 83.4 us (0.986)
  waiting for transfers between devices: 35.7 us -> 34.1 us
    ppermute x25, waiting for transfers between devices: 33.5 us -> 29.8 us  [swap(): return lax.ppermute(array, axis, [(i, i ^ mask) for i in range(size)])]
    all_to_all x1, waiting for transfers between devices: 2.18 us -> 4.26 us  [owners_blocks(): lax.all_to_all(blocks, 'tensor', split_axis=0, concat_axis=0, tiled=True)]
    unnamed x26 -> x30, local copies, waits for them, and re-layouts: 5.58 us -> 5.62 us
  transfers between devices with their start and end apart: 26 -> 26, of which waited for: 13 -> 12; matrix products, arithmetic and copies ran while one was open for 0% -> 0% of each run, Pallas kernels for 7% -> 7%
where the time goes in v5:
time: 83.4 us; the launch traced here: 83 us
  waiting for transfers between devices  34.1 us (41%)
  starting transfers between devices  30.7 us (37%)
  Pallas kernels  11.7 us (14%)
  local copies, waits for them, and re-layouts  5.68 us (7%)
    ppermute x25, waiting for transfers between devices, swap(): return lax.ppermute(array, axis, [(i, i ^ mask) for i in range(size)])  29.8 us
    ppermute x25, starting transfers between devices, swap(): return lax.ppermute(array, axis, [(i, i ^ mask) for i in range(size)])  25.6 us
    unnamed x30, local copies, waits for them, and re-layouts  5.62 us
    all_to_all x1, starting transfers between devices, owners_blocks(): lax.all_to_all(blocks, 'tensor', split_axis=0, concat_axis=0, tiled=True)  5.09 us
    all_to_all x1, waiting for transfers between devices, owners_blocks(): lax.all_to_all(blocks, 'tensor', split_axis=0, concat_axis=0, tiled=True)  4.26 us
    pallas_call x1, Pallas kernels, shards(): pl.pallas_call(functools.partial(attend_kernel, joined_pieces), name='att...  3.82 us
    pallas_call x1, Pallas kernels, shards(): pl.pallas_call(functools.partial(layer_kernel, forward_pieces, ways), nam...  3.5 us
    pallas_call x1, Pallas kernels, shards(): pl.pallas_call(cut_kernel, name='cut', out_shape=[jax.ShapeDtypeStruct((t...  2.47 us
  transfers between devices with their start and end apart: 26, of which 12 were waited for; matrix products, arithmetic and copies ran while one was open for 0% of the time, Pallas kernels for 7%

profile of v5, /device:TPU:0, one launch (start us, length us, event | category | flops | bytes accessed | tf_op | source)
XLA Modules:
  0.0 83.0 jit_solution(11181549688982902564)
XLA Ops:
  0.0 2.5 %cut.1 = (bf16[32,768]{1,0:T(8,128)(2,1)}, bf16[32,768]{1,0:T(8,128)(2,1)}, bf16[32,768]{1,0:T(8,128)(2,1)}, bf16[32,768]{1,0:T(8,128)(2,1)}, bf16[4,32,3072]{2,1,0:T(8,128)(2,1)}) custom-call(f32[32,3072]{1,0:T(8,128)} %refs_0_.1, f32[32,1024]{1,0:T(8,128)} %refs_1_.1, f32[32,4096]{1,0:T(8,128)} %refs_2_.1, f32[32,4096]{1,0:T(8,128)} %refs_3_.1), custom_call_target="tpu_custom_call" | custom-call | tf_op jit(solution)/shard_map/cut/pallas_call | solution.py:293
  2.5 3.1 %collective-permute-start = (bf16[32,768]{1,0:T(8,128)(2,1)}, bf16[32,768]{1,0:T(8,128)(2,1)S(1)}, u32[]{:S(2)}, u32[]{:S(2)}) collective-permute-start(bf16[32,768]{1,0:T(8,128)(2,1)} %get-tuple-element.24), channel_id=1, source_target_pairs={{0,1},{1,0},{2,3},{3,2},{4,5},{5,4},{6,7},{7,6},{8,9},{9,8},{10,11... | collective-permute-start | bytes 147464 | tf_op jit(solution)/shard_map/ppermute | solution.py:34
  5.6 2.6 %collective-permute-start.1 = (bf16[32,768]{1,0:T(8,128)(2,1)}, bf16[32,768]{1,0:T(8,128)(2,1)S(1)}, u32[]{:S(2)}, u32[]{:S(2)}) collective-permute-start(bf16[32,768]{1,0:T(8,128)(2,1)} %get-tuple-element.25), channel_id=1, source_target_pairs={{0,2},{1,3},{2,0},{3,1},{4,6},{5,7},{6,4},{7,5},{8,10},{9,11},{10,... | collective-permute-start | bytes 147464 | tf_op jit(solution)/shard_map/ppermute | solution.py:34
  8.2 5.1 %all-to-all-start = ((bf16[4,32,3072]{2,1,0:T(8,128)(2,1)}), bf16[4,32,3072]{2,1,0:T(8,128)(2,1)S(1)}, u32[]{:S(2)}, u32[]{:S(2)}) async-start(bf16[4,32,3072]{2,1,0:T(8,128)(2,1)} %get-tuple-element.34), calls=%async_computation | async-start | bytes 1572864 | tf_op jit(solution)/shard_map/all_to_all | solution.py:260
  13.3 1.0 %collective-permute-done.2.refs_3_ = bf16[32,768]{1,0:T(8,128)(2,1)S(1)} collective-permute-done((bf16[32,768]{1,0:T(8,128)(2,1)}, bf16[32,768]{1,0:T(8,128)(2,1)S(1)}, u32[]{:S(2)}, u32[]{:S(2)}) %collective-permute-start.2) | collective-permute-done | bytes 49184 | tf_op jit(solution)/shard_map/ppermute | solution.py:34
  14.3 0.8 copy-done
  15.4 1.6 %collective-permute-start.3 = (bf16[4,32,768]{2,1,0:T(8,128)(2,1)S(1)}, bf16[4,32,768]{2,1,0:T(8,128)(2,1)S(1)}, u32[]{:S(2)}, u32[]{:S(2)}) collective-permute-start(bf16[4,32,768]{2,1,0:T(8,128)(2,1)S(1)} %stack.1.refs_0_), channel_id=1, source_target_pairs={{0,16},{4,20},{8,24},{12,28},{16,0},{20,4},{24,8},{28,12},{1,17},{... | collective-permute-start | bytes 589832 | tf_op jit(solution)/shard_map/ppermute | solution.py:34
  17.0 1.5 %collective-permute-start.4 = (bf16[4,32,768]{2,1,0:T(8,128)(2,1)S(1)}, bf16[4,32,768]{2,1,0:T(8,128)(2,1)S(1)}, u32[]{:S(2)}, u32[]{:S(2)}) collective-permute-start(bf16[4,32,768]{2,1,0:T(8,128)(2,1)S(1)} %stack.1.refs_0_), channel_id=1, source_target_pairs={{0,8},{4,12},{8,0},{12,4},{16,24},{20,28},{24,16},{28,20},{1,9},{5... | collective-permute-start | bytes 589832 | tf_op jit(solution)/shard_map/ppermute | solution.py:34
  18.5 1.6 %prepare.1 = (bf16[256,1024]{1,0:T(8,128)(2,1)S(1)}, f32[4,256,512]{2,1,0:T(8,128)S(1)}) custom-call(bf16[32,768]{1,0:T(8,128)(2,1)S(1)} %copy-done, s32[8]{0:T(128)S(1)} %copy-done.8, s32[8]{0:T(128)S(1)} %copy-done.9, s32[8]{0:T(128)S(1)} %copy-done.10, bf16[256,1024]{1,0:T(8,128)(2,1)S(1)} %copy-done.1, f32[1,1024]{1,0:T(1,128)S(1)} %bitcast.4, ...), custom_call_target="tpu_custom_call" | custom-call | flops 20000000000 | bytes 4000000 | tf_op jit(solution)/shard_map/prepare/pallas_call | solution.py:306
  20.1 1.3 %copy-done.11 = f32[4,256,512]{2,1,0:T(8,128)} copy-done((f32[4,256,512]{2,1,0:T(8,128)}, f32[4,256,512]{2,1,0:T(8,128)S(1)}, u32[]{:S(2)}) %copy-start.11) | copy-done | bytes 2097176
  21.5 0.8 copy-done.13
  22.6 1.7 %collective-permute-start.5 = (bf16[4,32,768]{2,1,0:T(8,128)(2,1)S(1)}, bf16[4,32,768]{2,1,0:T(8,128)(2,1)S(1)}, u32[]{:S(2)}, u32[]{:S(2)}) collective-permute-start(bf16[4,32,768]{2,1,0:T(8,128)(2,1)S(1)} %collective-permute-done.3.refs_1_), channel_id=1, source_target_pairs={{0,8},{4,12},{8,0},{12,4},{16,24},{20,28},{24,16},{28,20},{1,9},{5... | collective-permute-start | bytes 589832 | tf_op jit(solution)/shard_map/ppermute | solution.py:34
  24.9 3.4 %collective-permute-done.5.refs_3_ = bf16[4,32,768]{2,1,0:T(8,128)(2,1)S(1)} collective-permute-done((bf16[4,32,768]{2,1,0:T(8,128)(2,1)S(1)}, bf16[4,32,768]{2,1,0:T(8,128)(2,1)S(1)}, u32[]{:S(2)}, u32[]{:S(2)}) %collective-permute-start.5) | collective-permute-done | bytes 196640 | tf_op jit(solution)/shard_map/ppermute | solution.py:34
  28.3 4.3 %all-to-all-done.refs_4_ = bf16[4,32,3072]{2,1,0:T(8,128)(2,1)S(1)} async-done(((bf16[4,32,3072]{2,1,0:T(8,128)(2,1)}), bf16[4,32,3072]{2,1,0:T(8,128)(2,1)S(1)}, u32[]{:S(2)}, u32[]{:S(2)}) %all-to-all-start) | async-done | bytes 786464 | tf_op jit(solution)/shard_map/all_to_all | solution.py:260
  32.6 1.5 %collective-permute-start.13 = (bf16[4,32,3072]{2,1,0:T(8,128)(2,1)S(1)}, bf16[4,32,3072]{2,1,0:T(8,128)(2,1)S(1)}, u32[]{:S(2)}, u32[]{:S(2)}) collective-permute-start(bf16[4,32,3072]{2,1,0:T(8,128)(2,1)S(1)} %all-to-all-done.refs_4_), channel_id=1, source_target_pairs={{0,16},{4,20},{8,24},{12,28},{16,0},{20,4},{24,8},{28,12},{1,17},{... | collective-permute-start | bytes 2359304 | tf_op jit(solution)/shard_map/ppermute | solution.py:34
  34.1 1.5 %collective-permute-start.14 = (bf16[4,32,3072]{2,1,0:T(8,128)(2,1)S(1)}, bf16[4,32,3072]{2,1,0:T(8,128)(2,1)S(1)}, u32[]{:S(2)}, u32[]{:S(2)}) collective-permute-start(bf16[4,32,3072]{2,1,0:T(8,128)(2,1)S(1)} %all-to-all-done.refs_4_), channel_id=1, source_target_pairs={{0,8},{4,12},{8,0},{12,4},{16,24},{20,28},{24,16},{28,20},{1,9},{5... | collective-permute-start | bytes 2359304 | tf_op jit(solution)/shard_map/ppermute | solution.py:34
  35.6 1.6 %copy-done.12 = f32[4,256,512]{2,1,0:T(8,128)S(1)} copy-done((f32[4,256,512]{2,1,0:T(8,128)S(1)}, f32[4,256,512]{2,1,0:T(8,128)}, u32[]{:S(2)}) %copy-start.12) | copy-done | bytes 2097176
  37.2 1.0 %copy-done.14 = bf16[256,1024]{1,0:T(8,128)(2,1)S(1)} copy-done((bf16[256,1024]{1,0:T(8,128)(2,1)S(1)}, bf16[256,1024]{1,0:T(8,128)(2,1)}, u32[]{:S(2)}) %copy-start.14) | copy-done | bytes 524312
  38.3 3.8 %attend.1.refs_0_ = bf16[256,256]{1,0:T(8,128)(2,1)S(1)} custom-call(bf16[256,1024]{1,0:T(8,128)(2,1)S(1)} %copy-done.14, bf16[256,256]{1,0:T(8,128)(2,1)S(1)} %copy-done.2, bf16[256,256]{1,0:T(8,128)(2,1)S(1)} %copy-done.3, f32[4,256,512]{2,1,0:T(8,128)S(1)} %copy-done.12, bf16[4,32,768]{2,1,0:T(8,128)(2,1)S(1)} %stack.1.refs_0_, ...), custom_call_target="tpu_custom_call" | custom-call | flops 20000000000 | bytes 6000000 | tf_op jit(solution)/shard_map/attend/pallas_call | solution.py:345
  42.2 2.0 %collective-permute-start.11 = (bf16[256,256]{1,0:T(8,128)(2,1)S(1)}, bf16[256,256]{1,0:T(8,128)(2,1)S(1)}, u32[]{:S(2)}, u32[]{:S(2)}) collective-permute-start(bf16[256,256]{1,0:T(8,128)(2,1)S(1)} %attend.1.refs_0_), channel_id=1, source_target_pairs={{0,2},{1,3},{2,0},{3,1},{4,6},{5,7},{6,4},{7,5},{8,10},{9,11},{10,... | collective-permute-start | bytes 393224 | tf_op jit(solution)/shard_map/ppermute | solution.py:34
  44.2 2.4 %collective-permute-start.12 = (bf16[256,256]{1,0:T(8,128)(2,1)S(1)}, bf16[256,256]{1,0:T(8,128)(2,1)S(1)}, u32[]{:S(2)}, u32[]{:S(2)}) collective-permute-start(bf16[256,256]{1,0:T(8,128)(2,1)S(1)} %attend.1.refs_0_), channel_id=1, source_target_pairs={{0,3},{1,2},{2,1},{3,0},{4,7},{5,6},{6,5},{7,4},{8,11},{9,10},{10,... | collective-permute-start | bytes 393224 | tf_op jit(solution)/shard_map/ppermute | solution.py:34
  46.5 4.5 %collective-permute-done.13.refs_5_ = bf16[4,32,3072]{2,1,0:T(8,128)(2,1)S(1)} collective-permute-done((bf16[4,32,3072]{2,1,0:T(8,128)(2,1)S(1)}, bf16[4,32,3072]{2,1,0:T(8,128)(2,1)S(1)}, u32[]{:S(2)}, u32[]{:S(2)}) %collective-permute-start.13) | collective-permute-done | bytes 786464 | tf_op jit(solution)/shard_map/ppermute | solution.py:34
  51.1 1.2 %collective-permute-done.14.refs_6_ = bf16[4,32,3072]{2,1,0:T(8,128)(2,1)S(1)} collective-permute-done((bf16[4,32,3072]{2,1,0:T(8,128)(2,1)S(1)}, bf16[4,32,3072]{2,1,0:T(8,128)(2,1)S(1)}, u32[]{:S(2)}, u32[]{:S(2)}) %collective-permute-start.14) | collective-permute-done | bytes 786464 | tf_op jit(solution)/shard_map/ppermute | solution.py:34
  52.3 1.6 %collective-permute-start.15 = (bf16[2,32,3072]{2,1,0:T(8,128)(2,1)S(1)}, bf16[2,32,3072]{2,1,0:T(8,128)(2,1)S(1)}, u32[]{:S(2)}, u32[]{:S(2)}) collective-permute-start(bf16[2,32,3072]{2,1,0:T(8,128)(2,1)S(1)} %slice.6), channel_id=1, source_target_pairs={{0,8},{4,12},{8,0},{12,4},{16,24},{20,28},{24,16},{28,20},{1,9},{5... | collective-permute-start | bytes 1179656 | tf_op jit(solution)/shard_map/ppermute | solution.py:34
  55.0 7.7 %collective-permute-done.15.refs_7_ = bf16[2,32,3072]{2,1,0:T(8,128)(2,1)S(1)} collective-permute-done((bf16[2,32,3072]{2,1,0:T(8,128)(2,1)S(1)}, bf16[2,32,3072]{2,1,0:T(8,128)(2,1)S(1)}, u32[]{:S(2)}, u32[]{:S(2)}) %collective-permute-start.15) | collective-permute-done | bytes 393248 | tf_op jit(solution)/shard_map/ppermute | solution.py:34
  62.7 1.3 %collective-permute-done.16.refs_8_ = bf16[2,32,3072]{2,1,0:T(8,128)(2,1)S(1)} collective-permute-done((bf16[2,32,3072]{2,1,0:T(8,128)(2,1)S(1)}, bf16[2,32,3072]{2,1,0:T(8,128)(2,1)S(1)}, u32[]{:S(2)}, u32[]{:S(2)}) %collective-permute-start.16) | collective-permute-done | bytes 393248 | tf_op jit(solution)/shard_map/ppermute | solution.py:34
  64.4 1.3 %collective-permute-done.21.refs_13_ = bf16[2,32,3072]{2,1,0:T(8,128)(2,1)S(1)} collective-permute-done((bf16[2,32,3072]{2,1,0:T(8,128)(2,1)S(1)}, bf16[2,32,3072]{2,1,0:T(8,128)(2,1)S(1)}, u32[]{:S(2)}, u32[]{:S(2)}) %collective-permute-start.21) | collective-permute-done | bytes 393248 | tf_op jit(solution)/shard_map/ppermute | solution.py:34
  65.8 3.5 %layer.1 = (f32[64,1024]{1,0:T(8,128)S(1)}, bf16[64,1024]{1,0:T(8,128)(2,1)S(1)}, bf16[64,1024]{1,0:T(8,128)(2,1)S(1)}, bf16[64,1024]{1,0:T(8,128)(2,1)S(1)}) custom-call(bf16[256,1024]{1,0:T(8,128)(2,1)S(1)} %copy-done.1, f32[1,1024]{1,0:T(1,128)S(1)} %bitcast.6, bf16[256,256]{1,0:T(8,128)(2,1)S(1)} %attend.1.refs_0_, ...), custom_call_target="tpu_custom_call" | custom-call | flops 2000000000 | bytes 8000000 | tf_op jit(solution)/shard_map/layer/pallas_call | solution.py:362
  70.0 3.7 %collective-permute-start.24 = (bf16[64,1024]{1,0:T(8,128)(2,1)S(1)}, bf16[64,1024]{1,0:T(8,128)(2,1)S(1)}, u32[]{:S(2)}, u32[]{:S(2)}) collective-permute-start(bf16[64,1024]{1,0:T(8,128)(2,1)S(1)} %get-tuple-element.40), channel_id=1, source_target_pairs={{0,3},{1,2},{2,1},{3,0},{4,7},{5,6},{6,5},{7,4},{8,11},{9,10},{10,... | collective-permute-start | bytes 393224 | tf_op jit(solution)/shard_map/ppermute | solution.py:34
  73.7 2.4 %collective-permute-done.22 = bf16[64,1024]{1,0:T(8,128)(2,1)S(1)} collective-permute-done((bf16[64,1024]{1,0:T(8,128)(2,1)S(1)}, bf16[64,1024]{1,0:T(8,128)(2,1)S(1)}, u32[]{:S(2)}, u32[]{:S(2)}) %collective-permute-start.22) | collective-permute-done | bytes 131104 | tf_op jit(solution)/shard_map/ppermute | solution.py:34
  76.1 6.2 %collective-permute-done.23 = bf16[64,1024]{1,0:T(8,128)(2,1)S(1)} collective-permute-done((bf16[64,1024]{1,0:T(8,128)(2,1)S(1)}, bf16[64,1024]{1,0:T(8,128)(2,1)S(1)}, u32[]{:S(2)}, u32[]{:S(2)}) %collective-permute-start.23) | collective-permute-done | bytes 131104 | tf_op jit(solution)/shard_map/ppermute | solution.py:34
  82.3 0.7 add_convert_fusion
  (58 shorter events, 3.5 us)
Async XLA Ops:
  0.0 18.5 %copy-start.5 = (s32[1023]{0:T(1024)S(1)}, s32[1023]{0:T(1024)}, u32[]{:S(2)}) copy-start(s32[1023]{0:T(1024)} %param.24) | copy-start | bytes 12280
  0.0 18.5 %copy-start.1 = (bf16[256,1024]{1,0:T(8,128)(2,1)S(1)}, bf16[256,1024]{1,0:T(8,128)(2,1)}, u32[]{:S(2)}) copy-start(bf16[256,1024]{1,0:T(8,128)(2,1)} %tokens.3) | copy-start | bytes 1572868
  0.0 18.5 %copy-start.8 = (s32[8]{0:T(128)S(1)}, s32[8]{0:T(128)}, u32[]{:S(2)}) copy-start(s32[8]{0:T(128)} %lengths.1) | copy-start | bytes 100
  0.0 18.5 %copy-start.10 = (s32[8]{0:T(128)S(1)}, s32[8]{0:T(128)}, u32[]{:S(2)}) copy-start(s32[8]{0:T(128)} %counts.1) | copy-start | bytes 100
  0.0 18.5 %copy-start.9 = (s32[8]{0:T(128)S(1)}, s32[8]{0:T(128)}, u32[]{:S(2)}) copy-start(s32[8]{0:T(128)} %flags.1) | copy-start | bytes 100
  2.5 10.8 %collective-permute-start = (bf16[32,768]{1,0:T(8,128)(2,1)}, bf16[32,768]{1,0:T(8,128)(2,1)S(1)}, u32[]{:S(2)}, u32[]{:S(2)}) collective-permute-start(bf16[32,768]{1,0:T(8,128)(2,1)} %get-tuple-element.24), channel_id=1, source_target_pairs={{0,1},{1,0},{2,3},{3,2},{4,5},{5,4},{6,7},{7,6},{8,9},{9,8},{10,11... | collective-permute-start | bytes 147464 | tf_op jit(solution)/shard_map/ppermute | solution.py:34
  5.6 7.7 %collective-permute-start.1 = (bf16[32,768]{1,0:T(8,128)(2,1)}, bf16[32,768]{1,0:T(8,128)(2,1)S(1)}, u32[]{:S(2)}, u32[]{:S(2)}) collective-permute-start(bf16[32,768]{1,0:T(8,128)(2,1)} %get-tuple-element.25), channel_id=1, source_target_pairs={{0,2},{1,3},{2,0},{3,1},{4,6},{5,7},{6,4},{7,5},{8,10},{9,11},{10,... | collective-permute-start | bytes 147464 | tf_op jit(solution)/shard_map/ppermute | solution.py:34
  8.2 6.1 %collective-permute-start.2 = (bf16[32,768]{1,0:T(8,128)(2,1)}, bf16[32,768]{1,0:T(8,128)(2,1)S(1)}, u32[]{:S(2)}, u32[]{:S(2)}) collective-permute-start(bf16[32,768]{1,0:T(8,128)(2,1)} %get-tuple-element.26), channel_id=1, source_target_pairs={{0,3},{1,2},{2,1},{3,0},{4,7},{5,6},{6,5},{7,4},{8,11},{9,10},{10,... | collective-permute-start | bytes 147464 | tf_op jit(solution)/shard_map/ppermute | solution.py:34
  8.2 24.4 %all-to-all-start = ((bf16[4,32,3072]{2,1,0:T(8,128)(2,1)}), bf16[4,32,3072]{2,1,0:T(8,128)(2,1)S(1)}, u32[]{:S(2)}, u32[]{:S(2)}) async-start(bf16[4,32,3072]{2,1,0:T(8,128)(2,1)} %get-tuple-element.34), calls=%async_computation | async-start | bytes 1572864 | tf_op jit(solution)/shard_map/all_to_all | solution.py:260
  15.4 6.9 %collective-permute-start.3 = (bf16[4,32,768]{2,1,0:T(8,128)(2,1)S(1)}, bf16[4,32,768]{2,1,0:T(8,128)(2,1)S(1)}, u32[]{:S(2)}, u32[]{:S(2)}) collective-permute-start(bf16[4,32,768]{2,1,0:T(8,128)(2,1)S(1)} %stack.1.refs_0_), channel_id=1, source_target_pairs={{0,16},{4,20},{8,24},{12,28},{16,0},{20,4},{24,8},{28,12},{1,17},{... | collective-permute-start | bytes 589832 | tf_op jit(solution)/shard_map/ppermute | solution.py:34
  17.0 5.7 %collective-permute-start.4 = (bf16[4,32,768]{2,1,0:T(8,128)(2,1)S(1)}, bf16[4,32,768]{2,1,0:T(8,128)(2,1)S(1)}, u32[]{:S(2)}, u32[]{:S(2)}) collective-permute-start(bf16[4,32,768]{2,1,0:T(8,128)(2,1)S(1)} %stack.1.refs_0_), channel_id=1, source_target_pairs={{0,8},{4,12},{8,0},{12,4},{16,24},{20,28},{24,16},{28,20},{1,9},{5... | collective-permute-start | bytes 589832 | tf_op jit(solution)/shard_map/ppermute | solution.py:34
  22.6 5.7 %collective-permute-start.5 = (bf16[4,32,768]{2,1,0:T(8,128)(2,1)S(1)}, bf16[4,32,768]{2,1,0:T(8,128)(2,1)S(1)}, u32[]{:S(2)}, u32[]{:S(2)}) collective-permute-start(bf16[4,32,768]{2,1,0:T(8,128)(2,1)S(1)} %collective-permute-done.3.refs_1_), channel_id=1, source_target_pairs={{0,8},{4,12},{8,0},{12,4},{16,24},{20,28},{24,16},{28,20},{1,9},{5... | collective-permute-start | bytes 589832 | tf_op jit(solution)/shard_map/ppermute | solution.py:34
  24.4 9.7 %collective-permute-start.6 = (bf16[4,32,768]{2,1,0:T(8,128)(2,1)S(1)}, bf16[4,32,768]{2,1,0:T(8,128)(2,1)S(1)}, u32[]{:S(2)}, u32[]{:S(2)}) collective-permute-start(bf16[4,32,768]{2,1,0:T(8,128)(2,1)S(1)} %stack.1.refs_0_), channel_id=1, source_target_pairs={{0,4},{4,0},{8,12},{12,8},{16,20},{20,16},{24,28},{28,24},{1,5},{5... | collective-permute-start | bytes 589832 | tf_op jit(solution)/shard_map/ppermute | solution.py:34
  24.4 11.2 %collective-permute-start.7 = (bf16[4,32,768]{2,1,0:T(8,128)(2,1)S(1)}, bf16[4,32,768]{2,1,0:T(8,128)(2,1)S(1)}, u32[]{:S(2)}, u32[]{:S(2)}) collective-permute-start(bf16[4,32,768]{2,1,0:T(8,128)(2,1)S(1)} %collective-permute-done.3.refs_1_), channel_id=1, source_target_pairs={{0,4},{4,0},{8,12},{12,8},{16,20},{20,16},{24,28},{28,24},{1,5},{5... | collective-permute-start | bytes 589832 | tf_op jit(solution)/shard_map/ppermute | solution.py:34
  24.9 10.7 %collective-permute-start.8 = (bf16[4,32,768]{2,1,0:T(8,128)(2,1)S(1)}, bf16[4,32,768]{2,1,0:T(8,128)(2,1)S(1)}, u32[]{:S(2)}, u32[]{:S(2)}) collective-permute-start(bf16[4,32,768]{2,1,0:T(8,128)(2,1)S(1)} %collective-permute-done.4.refs_2_), channel_id=1, source_target_pairs={{0,4},{4,0},{8,12},{12,8},{16,20},{20,16},{24,28},{28,24},{1,5},{5... | collective-permute-start | bytes 589832 | tf_op jit(solution)/shard_map/ppermute | solution.py:34
  28.3 7.3 %collective-permute-start.9 = (bf16[4,32,768]{2,1,0:T(8,128)(2,1)S(1)}, bf16[4,32,768]{2,1,0:T(8,128)(2,1)S(1)}, u32[]{:S(2)}, u32[]{:S(2)}) collective-permute-start(bf16[4,32,768]{2,1,0:T(8,128)(2,1)S(1)} %collective-permute-done.5.refs_3_), channel_id=1, source_target_pairs={{0,4},{4,0},{8,12},{12,8},{16,20},{20,16},{24,28},{28,24},{1,5},{5... | collective-permute-start | bytes 589832 | tf_op jit(solution)/shard_map/ppermute | solution.py:34
  32.6 18.5 %collective-permute-start.13 = (bf16[4,32,3072]{2,1,0:T(8,128)(2,1)S(1)}, bf16[4,32,3072]{2,1,0:T(8,128)(2,1)S(1)}, u32[]{:S(2)}, u32[]{:S(2)}) collective-permute-start(bf16[4,32,3072]{2,1,0:T(8,128)(2,1)S(1)} %all-to-all-done.refs_4_), channel_id=1, source_target_pairs={{0,16},{4,20},{8,24},{12,28},{16,0},{20,4},{24,8},{28,12},{1,17},{... | collective-permute-start | bytes 2359304 | tf_op jit(solution)/shard_map/ppermute | solution.py:34
  34.1 18.2 %collective-permute-start.14 = (bf16[4,32,3072]{2,1,0:T(8,128)(2,1)S(1)}, bf16[4,32,3072]{2,1,0:T(8,128)(2,1)S(1)}, u32[]{:S(2)}, u32[]{:S(2)}) collective-permute-start(bf16[4,32,3072]{2,1,0:T(8,128)(2,1)S(1)} %all-to-all-done.refs_4_), channel_id=1, source_target_pairs={{0,8},{4,12},{8,0},{12,4},{16,24},{20,28},{24,16},{28,20},{1,9},{5... | collective-permute-start | bytes 2359304 | tf_op jit(solution)/shard_map/ppermute | solution.py:34
  38.3 27.5 %copy-start.6 = (f32[1024]{0:T(1024)S(1)}, f32[1024]{0:T(1024)}, u32[]{:S(2)}) copy-start(f32[1024]{0:T(1024)} %param.22) | copy-start | bytes 12292
  42.1 11.8 %collective-permute-start.10 = (bf16[256,256]{1,0:T(8,128)(2,1)S(1)}, bf16[256,256]{1,0:T(8,128)(2,1)S(1)}, u32[]{:S(2)}, u32[]{:S(2)}) collective-permute-start(bf16[256,256]{1,0:T(8,128)(2,1)S(1)} %attend.1.refs_0_), channel_id=1, source_target_pairs={{0,1},{1,0},{2,3},{3,2},{4,5},{5,4},{6,7},{7,6},{8,9},{9,8},{10,11... | collective-permute-start | bytes 393224 | tf_op jit(solution)/shard_map/ppermute | solution.py:34
  42.2 12.4 %collective-permute-start.11 = (bf16[256,256]{1,0:T(8,128)(2,1)S(1)}, bf16[256,256]{1,0:T(8,128)(2,1)S(1)}, u32[]{:S(2)}, u32[]{:S(2)}) collective-permute-start(bf16[256,256]{1,0:T(8,128)(2,1)S(1)} %attend.1.refs_0_), channel_id=1, source_target_pairs={{0,2},{1,3},{2,0},{3,1},{4,6},{5,7},{6,4},{7,5},{8,10},{9,11},{10,... | collective-permute-start | bytes 393224 | tf_op jit(solution)/shard_map/ppermute | solution.py:34
  44.2 10.3 %collective-permute-start.12 = (bf16[256,256]{1,0:T(8,128)(2,1)S(1)}, bf16[256,256]{1,0:T(8,128)(2,1)S(1)}, u32[]{:S(2)}, u32[]{:S(2)}) collective-permute-start(bf16[256,256]{1,0:T(8,128)(2,1)S(1)} %attend.1.refs_0_), channel_id=1, source_target_pairs={{0,3},{1,2},{2,1},{3,0},{4,7},{5,6},{6,5},{7,4},{8,11},{9,10},{10,... | collective-permute-start | bytes 393224 | tf_op jit(solution)/shard_map/ppermute | solution.py:34
  51.1 13.0 %collective-permute-start.17 = (bf16[4,32,3072]{2,1,0:T(8,128)(2,1)S(1)}, bf16[4,32,3072]{2,1,0:T(8,128)(2,1)S(1)}, u32[]{:S(2)}, u32[]{:S(2)}) collective-permute-start(bf16[4,32,3072]{2,1,0:T(8,128)(2,1)S(1)} %all-to-all-done.refs_4_), channel_id=1, source_target_pairs={{0,4},{4,0},{8,12},{12,8},{16,20},{20,16},{24,28},{28,24},{1,5},{5... | collective-permute-start | bytes 2359304 | tf_op jit(solution)/shard_map/ppermute | solution.py:34
  52.3 10.4 %collective-permute-start.15 = (bf16[2,32,3072]{2,1,0:T(8,128)(2,1)S(1)}, bf16[2,32,3072]{2,1,0:T(8,128)(2,1)S(1)}, u32[]{:S(2)}, u32[]{:S(2)}) collective-permute-start(bf16[2,32,3072]{2,1,0:T(8,128)(2,1)S(1)} %slice.6), channel_id=1, source_target_pairs={{0,8},{4,12},{8,0},{12,4},{16,24},{20,28},{24,16},{28,20},{1,9},{5... | collective-permute-start | bytes 1179656 | tf_op jit(solution)/shard_map/ppermute | solution.py:34
  53.9 10.1 %collective-permute-start.16 = (bf16[2,32,3072]{2,1,0:T(8,128)(2,1)S(1)}, bf16[2,32,3072]{2,1,0:T(8,128)(2,1)S(1)}, u32[]{:S(2)}, u32[]{:S(2)}) collective-permute-start(bf16[2,32,3072]{2,1,0:T(8,128)(2,1)S(1)} %slice.7), channel_id=1, source_target_pairs={{0,16},{4,20},{8,24},{12,28},{16,0},{20,4},{24,8},{28,12},{1,17},{... | collective-permute-start | bytes 1179656 | tf_op jit(solution)/shard_map/ppermute | solution.py:34
  54.5 11.2 %collective-permute-start.18 = (bf16[4,32,3072]{2,1,0:T(8,128)(2,1)S(1)}, bf16[4,32,3072]{2,1,0:T(8,128)(2,1)S(1)}, u32[]{:S(2)}, u32[]{:S(2)}) collective-permute-start(bf16[4,32,3072]{2,1,0:T(8,128)(2,1)S(1)} %collective-permute-done.13.refs_5_), channel_id=1, source_target_pairs={{0,4},{4,0},{8,12},{12,8},{16,20},{20,16},{24,28},{28,24},{1,5},{5... | collective-permute-start | bytes 2359304 | tf_op jit(solution)/shard_map/ppermute | solution.py:34
  54.5 11.2 %collective-permute-start.19 = (bf16[4,32,3072]{2,1,0:T(8,128)(2,1)S(1)}, bf16[4,32,3072]{2,1,0:T(8,128)(2,1)S(1)}, u32[]{:S(2)}, u32[]{:S(2)}) collective-permute-start(bf16[4,32,3072]{2,1,0:T(8,128)(2,1)S(1)} %collective-permute-done.14.refs_6_), channel_id=1, source_target_pairs={{0,4},{4,0},{8,12},{12,8},{16,20},{20,16},{24,28},{28,24},{1,5},{5... | collective-permute-start | bytes 2359304 | tf_op jit(solution)/shard_map/ppermute | solution.py:34
  62.7 1.7 %collective-permute-start.20 = (bf16[2,32,3072]{2,1,0:T(8,128)(2,1)S(1)}, bf16[2,32,3072]{2,1,0:T(8,128)(2,1)S(1)}, u32[]{:S(2)}, u32[]{:S(2)}) collective-permute-start(bf16[2,32,3072]{2,1,0:T(8,128)(2,1)S(1)} %collective-permute-done.15.refs_7_), channel_id=1, source_target_pairs={{0,4},{4,0},{8,12},{12,8},{16,20},{20,16},{24,28},{28,24},{1,5},{5... | collective-permute-start | bytes 1179656 | tf_op jit(solution)/shard_map/ppermute | solution.py:34
  64.0 1.7 %collective-permute-start.21 = (bf16[2,32,3072]{2,1,0:T(8,128)(2,1)S(1)}, bf16[2,32,3072]{2,1,0:T(8,128)(2,1)S(1)}, u32[]{:S(2)}, u32[]{:S(2)}) collective-permute-start(bf16[2,32,3072]{2,1,0:T(8,128)(2,1)S(1)} %collective-permute-done.16.refs_8_), channel_id=1, source_target_pairs={{0,4},{4,0},{8,12},{12,8},{16,20},{20,16},{24,28},{28,24},{1,5},{5... | collective-permute-start | bytes 1179656 | tf_op jit(solution)/shard_map/ppermute | solution.py:34
  69.3 6.8 %collective-permute-start.22 = (bf16[64,1024]{1,0:T(8,128)(2,1)S(1)}, bf16[64,1024]{1,0:T(8,128)(2,1)S(1)}, u32[]{:S(2)}, u32[]{:S(2)}) collective-permute-start(bf16[64,1024]{1,0:T(8,128)(2,1)S(1)} %get-tuple-element.38), channel_id=1, source_target_pairs={{0,1},{1,0},{2,3},{3,2},{4,5},{5,4},{6,7},{7,6},{8,9},{9,8},{10,11... | collective-permute-start | bytes 393224 | tf_op jit(solution)/shard_map/ppermute | solution.py:34
  69.3 13.0 %collective-permute-start.23 = (bf16[64,1024]{1,0:T(8,128)(2,1)S(1)}, bf16[64,1024]{1,0:T(8,128)(2,1)S(1)}, u32[]{:S(2)}, u32[]{:S(2)}) collective-permute-start(bf16[64,1024]{1,0:T(8,128)(2,1)S(1)} %get-tuple-element.39), channel_id=1, source_target_pairs={{0,2},{1,3},{2,0},{3,1},{4,6},{5,7},{6,4},{7,5},{8,10},{9,11},{10,... | collective-permute-start | bytes 393224 | tf_op jit(solution)/shard_map/ppermute | solution.py:34
  70.0 12.3 %collective-permute-start.24 = (bf16[64,1024]{1,0:T(8,128)(2,1)S(1)}, bf16[64,1024]{1,0:T(8,128)(2,1)S(1)}, u32[]{:S(2)}, u32[]{:S(2)}) collective-permute-start(bf16[64,1024]{1,0:T(8,128)(2,1)S(1)} %get-tuple-element.40), channel_id=1, source_target_pairs={{0,3},{1,2},{2,1},{3,0},{4,7},{5,6},{6,5},{7,4},{8,11},{9,10},{10,... | collective-permute-start | bytes 393224 | tf_op jit(solution)/shard_map/ppermute | solution.py:34
  (9 other events, 76.7 us)

commit v6 on v5

--- a/solution.py
+++ b/solution.py
@@ -379,9 +379,11 @@
         cost_estimate=cost(2 * 10**9, 8 * 10**6),
     )(tokens, second_gain.reshape(1, features), *attended, *forward_all)
 
+    shared = [swap(send, "tensor", k) for k, send in enumerate(sends, 1) if k > 1]
+    neighbour, shared[0] = together(sends[0], shared[0])
     total = own
-    for k, send in enumerate(sends, 1):
-        total = total + swap(send, "tensor", k).astype(FULL)
+    for block in [swap(neighbour, "tensor", 1)] + shared:
+        total = total + block.astype(FULL)
     return total.astype(HALF)
 
 

time: 83.4 us -> 85.4 us (1.024)
  waiting for transfers between devices: 34.1 us -> 39.9 us
  starting transfers between devices: 30.7 us -> 27 us
    ppermute x25, waiting for transfers between devices: 29.8 us -> 35.6 us  [swap(): return lax.ppermute(array, axis, [(i, i ^ mask) for i in range(size)])]
    ppermute x25, starting transfers between devices: 25.6 us -> 21.9 us  [swap(): return lax.ppermute(array, axis, [(i, i ^ mask) for i in range(size)])]
where the time goes in v6:
time: 85.4 us; the launch traced here: 85.1 us
  waiting for transfers between devices  39.9 us (47%)
  starting transfers between devices  27 us (32%)
  Pallas kernels  11.7 us (14%)
  local copies, waits for them, and re-layouts  5.68 us (7%)
    ppermute x25, waiting for transfers between devices, swap(): return lax.ppermute(array, axis, [(i, i ^ mask) for i in range(size)])  35.6 us
    ppermute x25, starting transfers between devices, swap(): return lax.ppermute(array, axis, [(i, i ^ mask) for i in range(size)])  21.9 us
    unnamed x30, local copies, waits for them, and re-layouts  5.62 us
    all_to_all x1, starting transfers between devices, owners_blocks(): lax.all_to_all(blocks, 'tensor', split_axis=0, concat_axis=0, tiled=True)  5.09 us
    all_to_all x1, waiting for transfers between devices, owners_blocks(): lax.all_to_all(blocks, 'tensor', split_axis=0, concat_axis=0, tiled=True)  4.26 us
    pallas_call x1, Pallas kernels, shards(): pl.pallas_call(functools.partial(attend_kernel, joined_pieces), name='att...  3.82 us
    pallas_call x1, Pallas kernels, shards(): pl.pallas_call(functools.partial(layer_kernel, forward_pieces, ways), nam...  3.5 us
    pallas_call x1, Pallas kernels, shards(): pl.pallas_call(cut_kernel, name='cut', out_shape=[jax.ShapeDtypeStruct((t...  2.47 us
  transfers between devices with their start and end apart: 26, of which 12 were waited for; matrix products, arithmetic and copies ran while one was open for 0% of the time, Pallas kernels for 7%

profile of v6, /device:TPU:0, one launch (start us, length us, event | category | flops | bytes accessed | tf_op | source)
XLA Modules:
  0.0 85.1 jit_solution(6668851518982927538)
XLA Ops:
  0.0 2.5 %cut.1 = (bf16[32,768]{1,0:T(8,128)(2,1)}, bf16[32,768]{1,0:T(8,128)(2,1)}, bf16[32,768]{1,0:T(8,128)(2,1)}, bf16[32,768]{1,0:T(8,128)(2,1)}, bf16[4,32,3072]{2,1,0:T(8,128)(2,1)}) custom-call(f32[32,3072]{1,0:T(8,128)} %refs_0_.1, f32[32,1024]{1,0:T(8,128)} %refs_1_.1, f32[32,4096]{1,0:T(8,128)} %refs_2_.1, f32[32,4096]{1,0:T(8,128)} %refs_3_.1), custom_call_target="tpu_custom_call" | custom-call | tf_op jit(solution)/shard_map/cut/pallas_call | solution.py:293
  2.5 3.1 %collective-permute-start = (bf16[32,768]{1,0:T(8,128)(2,1)}, bf16[32,768]{1,0:T(8,128)(2,1)S(1)}, u32[]{:S(2)}, u32[]{:S(2)}) collective-permute-start(bf16[32,768]{1,0:T(8,128)(2,1)} %get-tuple-element.26), channel_id=1, source_target_pairs={{0,1},{1,0},{2,3},{3,2},{4,5},{5,4},{6,7},{7,6},{8,9},{9,8},{10,11... | collective-permute-start | bytes 147464 | tf_op jit(solution)/shard_map/ppermute | solution.py:34
  5.6 2.6 %collective-permute-start.1 = (bf16[32,768]{1,0:T(8,128)(2,1)}, bf16[32,768]{1,0:T(8,128)(2,1)S(1)}, u32[]{:S(2)}, u32[]{:S(2)}) collective-permute-start(bf16[32,768]{1,0:T(8,128)(2,1)} %get-tuple-element.27), channel_id=1, source_target_pairs={{0,2},{1,3},{2,0},{3,1},{4,6},{5,7},{6,4},{7,5},{8,10},{9,11},{10,... | collective-permute-start | bytes 147464 | tf_op jit(solution)/shard_map/ppermute | solution.py:34
  8.2 5.1 %all-to-all-start = ((bf16[4,32,3072]{2,1,0:T(8,128)(2,1)}), bf16[4,32,3072]{2,1,0:T(8,128)(2,1)S(1)}, u32[]{:S(2)}, u32[]{:S(2)}) async-start(bf16[4,32,3072]{2,1,0:T(8,128)(2,1)} %get-tuple-element.36), calls=%async_computation | async-start | bytes 1572864 | tf_op jit(solution)/shard_map/all_to_all | solution.py:260
  13.3 1.0 %collective-permute-done.2.refs_3_ = bf16[32,768]{1,0:T(8,128)(2,1)S(1)} collective-permute-done((bf16[32,768]{1,0:T(8,128)(2,1)}, bf16[32,768]{1,0:T(8,128)(2,1)S(1)}, u32[]{:S(2)}, u32[]{:S(2)}) %collective-permute-start.2) | collective-permute-done | bytes 49184 | tf_op jit(solution)/shard_map/ppermute | solution.py:34
  14.3 0.8 copy-done
  15.4 1.6 %collective-permute-start.3 = (bf16[4,32,768]{2,1,0:T(8,128)(2,1)S(1)}, bf16[4,32,768]{2,1,0:T(8,128)(2,1)S(1)}, u32[]{:S(2)}, u32[]{:S(2)}) collective-permute-start(bf16[4,32,768]{2,1,0:T(8,128)(2,1)S(1)} %stack.1.refs_0_), channel_id=1, source_target_pairs={{0,16},{4,20},{8,24},{12,28},{16,0},{20,4},{24,8},{28,12},{1,17},{... | collective-permute-start | bytes 589832 | tf_op jit(solution)/shard_map/ppermute | solution.py:34
  17.0 1.5 %collective-permute-start.4 = (bf16[4,32,768]{2,1,0:T(8,128)(2,1)S(1)}, bf16[4,32,768]{2,1,0:T(8,128)(2,1)S(1)}, u32[]{:S(2)}, u32[]{:S(2)}) collective-permute-start(bf16[4,32,768]{2,1,0:T(8,128)(2,1)S(1)} %stack.1.refs_0_), channel_id=1, source_target_pairs={{0,8},{4,12},{8,0},{12,4},{16,24},{20,28},{24,16},{28,20},{1,9},{5... | collective-permute-start | bytes 589832 | tf_op jit(solution)/shard_map/ppermute | solution.py:34
  18.5 1.6 %prepare.1 = (bf16[256,1024]{1,0:T(8,128)(2,1)S(1)}, f32[4,256,512]{2,1,0:T(8,128)S(1)}) custom-call(bf16[32,768]{1,0:T(8,128)(2,1)S(1)} %copy-done, s32[8]{0:T(128)S(1)} %copy-done.8, s32[8]{0:T(128)S(1)} %copy-done.9, s32[8]{0:T(128)S(1)} %copy-done.10, bf16[256,1024]{1,0:T(8,128)(2,1)S(1)} %copy-done.1, f32[1,1024]{1,0:T(1,128)S(1)} %bitcast.4, ...), custom_call_target="tpu_custom_call" | custom-call | flops 20000000000 | bytes 4000000 | tf_op jit(solution)/shard_map/prepare/pallas_call | solution.py:306
  20.1 1.3 %copy-done.11 = f32[4,256,512]{2,1,0:T(8,128)} copy-done((f32[4,256,512]{2,1,0:T(8,128)}, f32[4,256,512]{2,1,0:T(8,128)S(1)}, u32[]{:S(2)}) %copy-start.11) | copy-done | bytes 2097176
  21.5 0.8 copy-done.13
  22.6 1.7 %collective-permute-start.5 = (bf16[4,32,768]{2,1,0:T(8,128)(2,1)S(1)}, bf16[4,32,768]{2,1,0:T(8,128)(2,1)S(1)}, u32[]{:S(2)}, u32[]{:S(2)}) collective-permute-start(bf16[4,32,768]{2,1,0:T(8,128)(2,1)S(1)} %collective-permute-done.3.refs_1_), channel_id=1, source_target_pairs={{0,8},{4,12},{8,0},{12,4},{16,24},{20,28},{24,16},{28,20},{1,9},{5... | collective-permute-start | bytes 589832 | tf_op jit(solution)/shard_map/ppermute | solution.py:34
  24.9 3.4 %collective-permute-done.5.refs_3_ = bf16[4,32,768]{2,1,0:T(8,128)(2,1)S(1)} collective-permute-done((bf16[4,32,768]{2,1,0:T(8,128)(2,1)S(1)}, bf16[4,32,768]{2,1,0:T(8,128)(2,1)S(1)}, u32[]{:S(2)}, u32[]{:S(2)}) %collective-permute-start.5) | collective-permute-done | bytes 196640 | tf_op jit(solution)/shard_map/ppermute | solution.py:34
  28.3 4.3 %all-to-all-done.refs_4_ = bf16[4,32,3072]{2,1,0:T(8,128)(2,1)S(1)} async-done(((bf16[4,32,3072]{2,1,0:T(8,128)(2,1)}), bf16[4,32,3072]{2,1,0:T(8,128)(2,1)S(1)}, u32[]{:S(2)}, u32[]{:S(2)}) %all-to-all-start) | async-done | bytes 786464 | tf_op jit(solution)/shard_map/all_to_all | solution.py:260
  32.6 1.5 %collective-permute-start.13 = (bf16[4,32,3072]{2,1,0:T(8,128)(2,1)S(1)}, bf16[4,32,3072]{2,1,0:T(8,128)(2,1)S(1)}, u32[]{:S(2)}, u32[]{:S(2)}) collective-permute-start(bf16[4,32,3072]{2,1,0:T(8,128)(2,1)S(1)} %all-to-all-done.refs_4_), channel_id=1, source_target_pairs={{0,16},{4,20},{8,24},{12,28},{16,0},{20,4},{24,8},{28,12},{1,17},{... | collective-permute-start | bytes 2359304 | tf_op jit(solution)/shard_map/ppermute | solution.py:34
  34.1 1.5 %collective-permute-start.14 = (bf16[4,32,3072]{2,1,0:T(8,128)(2,1)S(1)}, bf16[4,32,3072]{2,1,0:T(8,128)(2,1)S(1)}, u32[]{:S(2)}, u32[]{:S(2)}) collective-permute-start(bf16[4,32,3072]{2,1,0:T(8,128)(2,1)S(1)} %all-to-all-done.refs_4_), channel_id=1, source_target_pairs={{0,8},{4,12},{8,0},{12,4},{16,24},{20,28},{24,16},{28,20},{1,9},{5... | collective-permute-start | bytes 2359304 | tf_op jit(solution)/shard_map/ppermute | solution.py:34
  35.6 1.6 %copy-done.12 = f32[4,256,512]{2,1,0:T(8,128)S(1)} copy-done((f32[4,256,512]{2,1,0:T(8,128)S(1)}, f32[4,256,512]{2,1,0:T(8,128)}, u32[]{:S(2)}) %copy-start.12) | copy-done | bytes 2097176
  37.2 1.0 %copy-done.14 = bf16[256,1024]{1,0:T(8,128)(2,1)S(1)} copy-done((bf16[256,1024]{1,0:T(8,128)(2,1)S(1)}, bf16[256,1024]{1,0:T(8,128)(2,1)}, u32[]{:S(2)}) %copy-start.14) | copy-done | bytes 524312
  38.3 3.8 %attend.1.refs_0_ = bf16[256,256]{1,0:T(8,128)(2,1)S(1)} custom-call(bf16[256,1024]{1,0:T(8,128)(2,1)S(1)} %copy-done.14, bf16[256,256]{1,0:T(8,128)(2,1)S(1)} %copy-done.2, bf16[256,256]{1,0:T(8,128)(2,1)S(1)} %copy-done.3, f32[4,256,512]{2,1,0:T(8,128)S(1)} %copy-done.12, bf16[4,32,768]{2,1,0:T(8,128)(2,1)S(1)} %stack.1.refs_0_, ...), custom_call_target="tpu_custom_call" | custom-call | flops 20000000000 | bytes 6000000 | tf_op jit(solution)/shard_map/attend/pallas_call | solution.py:345
  42.2 2.0 %collective-permute-start.11 = (bf16[256,256]{1,0:T(8,128)(2,1)S(1)}, bf16[256,256]{1,0:T(8,128)(2,1)S(1)}, u32[]{:S(2)}, u32[]{:S(2)}) collective-permute-start(bf16[256,256]{1,0:T(8,128)(2,1)S(1)} %attend.1.refs_0_), channel_id=1, source_target_pairs={{0,2},{1,3},{2,0},{3,1},{4,6},{5,7},{6,4},{7,5},{8,10},{9,11},{10,... | collective-permute-start | bytes 393224 | tf_op jit(solution)/shard_map/ppermute | solution.py:34
  44.2 2.4 %collective-permute-start.12 = (bf16[256,256]{1,0:T(8,128)(2,1)S(1)}, bf16[256,256]{1,0:T(8,128)(2,1)S(1)}, u32[]{:S(2)}, u32[]{:S(2)}) collective-permute-start(bf16[256,256]{1,0:T(8,128)(2,1)S(1)} %attend.1.refs_0_), channel_id=1, source_target_pairs={{0,3},{1,2},{2,1},{3,0},{4,7},{5,6},{6,5},{7,4},{8,11},{9,10},{10,... | collective-permute-start | bytes 393224 | tf_op jit(solution)/shard_map/ppermute | solution.py:34
  46.5 4.5 %collective-permute-done.13.refs_5_ = bf16[4,32,3072]{2,1,0:T(8,128)(2,1)S(1)} collective-permute-done((bf16[4,32,3072]{2,1,0:T(8,128)(2,1)S(1)}, bf16[4,32,3072]{2,1,0:T(8,128)(2,1)S(1)}, u32[]{:S(2)}, u32[]{:S(2)}) %collective-permute-start.13) | collective-permute-done | bytes 786464 | tf_op jit(solution)/shard_map/ppermute | solution.py:34
  51.1 1.2 %collective-permute-done.14.refs_6_ = bf16[4,32,3072]{2,1,0:T(8,128)(2,1)S(1)} collective-permute-done((bf16[4,32,3072]{2,1,0:T(8,128)(2,1)S(1)}, bf16[4,32,3072]{2,1,0:T(8,128)(2,1)S(1)}, u32[]{:S(2)}, u32[]{:S(2)}) %collective-permute-start.14) | collective-permute-done | bytes 786464 | tf_op jit(solution)/shard_map/ppermute | solution.py:34
  52.3 1.6 %collective-permute-start.15 = (bf16[2,32,3072]{2,1,0:T(8,128)(2,1)S(1)}, bf16[2,32,3072]{2,1,0:T(8,128)(2,1)S(1)}, u32[]{:S(2)}, u32[]{:S(2)}) collective-permute-start(bf16[2,32,3072]{2,1,0:T(8,128)(2,1)S(1)} %slice.6), channel_id=1, source_target_pairs={{0,8},{4,12},{8,0},{12,4},{16,24},{20,28},{24,16},{28,20},{1,9},{5... | collective-permute-start | bytes 1179656 | tf_op jit(solution)/shard_map/ppermute | solution.py:34
  55.0 7.7 %collective-permute-done.15.refs_7_ = bf16[2,32,3072]{2,1,0:T(8,128)(2,1)S(1)} collective-permute-done((bf16[2,32,3072]{2,1,0:T(8,128)(2,1)S(1)}, bf16[2,32,3072]{2,1,0:T(8,128)(2,1)S(1)}, u32[]{:S(2)}, u32[]{:S(2)}) %collective-permute-start.15) | collective-permute-done | bytes 393248 | tf_op jit(solution)/shard_map/ppermute | solution.py:34
  62.7 1.3 %collective-permute-done.16.refs_8_ = bf16[2,32,3072]{2,1,0:T(8,128)(2,1)S(1)} collective-permute-done((bf16[2,32,3072]{2,1,0:T(8,128)(2,1)S(1)}, bf16[2,32,3072]{2,1,0:T(8,128)(2,1)S(1)}, u32[]{:S(2)}, u32[]{:S(2)}) %collective-permute-start.16) | collective-permute-done | bytes 393248 | tf_op jit(solution)/shard_map/ppermute | solution.py:34
  64.4 1.3 %collective-permute-done.21.refs_13_ = bf16[2,32,3072]{2,1,0:T(8,128)(2,1)S(1)} collective-permute-done((bf16[2,32,3072]{2,1,0:T(8,128)(2,1)S(1)}, bf16[2,32,3072]{2,1,0:T(8,128)(2,1)S(1)}, u32[]{:S(2)}, u32[]{:S(2)}) %collective-permute-start.21) | collective-permute-done | bytes 393248 | tf_op jit(solution)/shard_map/ppermute | solution.py:34
  65.8 3.5 %layer.1 = (f32[64,1024]{1,0:T(8,128)S(1)}, bf16[64,1024]{1,0:T(8,128)(2,1)S(1)}, bf16[64,1024]{1,0:T(8,128)(2,1)S(1)}, bf16[64,1024]{1,0:T(8,128)(2,1)S(1)}) custom-call(bf16[256,1024]{1,0:T(8,128)(2,1)S(1)} %copy-done.1, f32[1,1024]{1,0:T(1,128)S(1)} %bitcast.6, bf16[256,256]{1,0:T(8,128)(2,1)S(1)} %attend.1.refs_0_, ...), custom_call_target="tpu_custom_call" | custom-call | flops 2000000000 | bytes 8000000 | tf_op jit(solution)/shard_map/layer/pallas_call | solution.py:362
  69.3 0.6 collective-permute-start.24
  70.0 9.4 %collective-permute-done.22 = bf16[64,1024]{1,0:T(8,128)(2,1)S(1)} collective-permute-done((bf16[64,1024]{1,0:T(8,128)(2,1)S(1)}, bf16[64,1024]{1,0:T(8,128)(2,1)S(1)}, u32[]{:S(2)}, u32[]{:S(2)}) %collective-permute-start.22) | collective-permute-done | bytes 131104 | tf_op jit(solution)/shard_map/ppermute | solution.py:34
  79.5 4.9 %collective-permute-done.23 = bf16[64,1024]{1,0:T(8,128)(2,1)S(1)} collective-permute-done((bf16[64,1024]{1,0:T(8,128)(2,1)S(1)}, bf16[64,1024]{1,0:T(8,128)(2,1)S(1)}, u32[]{:S(2)}, u32[]{:S(2)}) %collective-permute-start.23) | collective-permute-done | bytes 131104 | tf_op jit(solution)/shard_map/ppermute | solution.py:34
  84.4 0.7 add_convert_fusion
  (58 shorter events, 2.9 us)
Async XLA Ops:
  0.0 18.5 %copy-start.5 = (s32[1023]{0:T(1024)S(1)}, s32[1023]{0:T(1024)}, u32[]{:S(2)}) copy-start(s32[1023]{0:T(1024)} %param.24) | copy-start | bytes 12280
  0.0 18.5 %copy-start.1 = (bf16[256,1024]{1,0:T(8,128)(2,1)S(1)}, bf16[256,1024]{1,0:T(8,128)(2,1)}, u32[]{:S(2)}) copy-start(bf16[256,1024]{1,0:T(8,128)(2,1)} %tokens.3) | copy-start | bytes 1572868
  0.0 18.5 %copy-start.8 = (s32[8]{0:T(128)S(1)}, s32[8]{0:T(128)}, u32[]{:S(2)}) copy-start(s32[8]{0:T(128)} %lengths.1) | copy-start | bytes 100
  0.0 18.5 %copy-start.10 = (s32[8]{0:T(128)S(1)}, s32[8]{0:T(128)}, u32[]{:S(2)}) copy-start(s32[8]{0:T(128)} %counts.1) | copy-start | bytes 100
  0.0 18.5 %copy-start.9 = (s32[8]{0:T(128)S(1)}, s32[8]{0:T(128)}, u32[]{:S(2)}) copy-start(s32[8]{0:T(128)} %flags.1) | copy-start | bytes 100
  2.5 10.8 %collective-permute-start = (bf16[32,768]{1,0:T(8,128)(2,1)}, bf16[32,768]{1,0:T(8,128)(2,1)S(1)}, u32[]{:S(2)}, u32[]{:S(2)}) collective-permute-start(bf16[32,768]{1,0:T(8,128)(2,1)} %get-tuple-element.26), channel_id=1, source_target_pairs={{0,1},{1,0},{2,3},{3,2},{4,5},{5,4},{6,7},{7,6},{8,9},{9,8},{10,11... | collective-permute-start | bytes 147464 | tf_op jit(solution)/shard_map/ppermute | solution.py:34
  5.6 7.7 %collective-permute-start.1 = (bf16[32,768]{1,0:T(8,128)(2,1)}, bf16[32,768]{1,0:T(8,128)(2,1)S(1)}, u32[]{:S(2)}, u32[]{:S(2)}) collective-permute-start(bf16[32,768]{1,0:T(8,128)(2,1)} %get-tuple-element.27), channel_id=1, source_target_pairs={{0,2},{1,3},{2,0},{3,1},{4,6},{5,7},{6,4},{7,5},{8,10},{9,11},{10,... | collective-permute-start | bytes 147464 | tf_op jit(solution)/shard_map/ppermute | solution.py:34
  8.2 6.1 %collective-permute-start.2 = (bf16[32,768]{1,0:T(8,128)(2,1)}, bf16[32,768]{1,0:T(8,128)(2,1)S(1)}, u32[]{:S(2)}, u32[]{:S(2)}) collective-permute-start(bf16[32,768]{1,0:T(8,128)(2,1)} %get-tuple-element.28), channel_id=1, source_target_pairs={{0,3},{1,2},{2,1},{3,0},{4,7},{5,6},{6,5},{7,4},{8,11},{9,10},{10,... | collective-permute-start | bytes 147464 | tf_op jit(solution)/shard_map/ppermute | solution.py:34
  8.2 24.4 %all-to-all-start = ((bf16[4,32,3072]{2,1,0:T(8,128)(2,1)}), bf16[4,32,3072]{2,1,0:T(8,128)(2,1)S(1)}, u32[]{:S(2)}, u32[]{:S(2)}) async-start(bf16[4,32,3072]{2,1,0:T(8,128)(2,1)} %get-tuple-element.36), calls=%async_computation | async-start | bytes 1572864 | tf_op jit(solution)/shard_map/all_to_all | solution.py:260
  15.4 6.9 %collective-permute-start.3 = (bf16[4,32,768]{2,1,0:T(8,128)(2,1)S(1)}, bf16[4,32,768]{2,1,0:T(8,128)(2,1)S(1)}, u32[]{:S(2)}, u32[]{:S(2)}) collective-permute-start(bf16[4,32,768]{2,1,0:T(8,128)(2,1)S(1)} %stack.1.refs_0_), channel_id=1, source_target_pairs={{0,16},{4,20},{8,24},{12,28},{16,0},{20,4},{24,8},{28,12},{1,17},{... | collective-permute-start | bytes 589832 | tf_op jit(solution)/shard_map/ppermute | solution.py:34
  17.0 5.7 %collective-permute-start.4 = (bf16[4,32,768]{2,1,0:T(8,128)(2,1)S(1)}, bf16[4,32,768]{2,1,0:T(8,128)(2,1)S(1)}, u32[]{:S(2)}, u32[]{:S(2)}) collective-permute-start(bf16[4,32,768]{2,1,0:T(8,128)(2,1)S(1)} %stack.1.refs_0_), channel_id=1, source_target_pairs={{0,8},{4,12},{8,0},{12,4},{16,24},{20,28},{24,16},{28,20},{1,9},{5... | collective-permute-start | bytes 589832 | tf_op jit(solution)/shard_map/ppermute | solution.py:34
  22.6 5.7 %collective-permute-start.5 = (bf16[4,32,768]{2,1,0:T(8,128)(2,1)S(1)}, bf16[4,32,768]{2,1,0:T(8,128)(2,1)S(1)}, u32[]{:S(2)}, u32[]{:S(2)}) collective-permute-start(bf16[4,32,768]{2,1,0:T(8,128)(2,1)S(1)} %collective-permute-done.3.refs_1_), channel_id=1, source_target_pairs={{0,8},{4,12},{8,0},{12,4},{16,24},{20,28},{24,16},{28,20},{1,9},{5... | collective-permute-start | bytes 589832 | tf_op jit(solution)/shard_map/ppermute | solution.py:34
  24.4 9.7 %collective-permute-start.6 = (bf16[4,32,768]{2,1,0:T(8,128)(2,1)S(1)}, bf16[4,32,768]{2,1,0:T(8,128)(2,1)S(1)}, u32[]{:S(2)}, u32[]{:S(2)}) collective-permute-start(bf16[4,32,768]{2,1,0:T(8,128)(2,1)S(1)} %stack.1.refs_0_), channel_id=1, source_target_pairs={{0,4},{4,0},{8,12},{12,8},{16,20},{20,16},{24,28},{28,24},{1,5},{5... | collective-permute-start | bytes 589832 | tf_op jit(solution)/shard_map/ppermute | solution.py:34
  24.4 11.2 %collective-permute-start.7 = (bf16[4,32,768]{2,1,0:T(8,128)(2,1)S(1)}, bf16[4,32,768]{2,1,0:T(8,128)(2,1)S(1)}, u32[]{:S(2)}, u32[]{:S(2)}) collective-permute-start(bf16[4,32,768]{2,1,0:T(8,128)(2,1)S(1)} %collective-permute-done.3.refs_1_), channel_id=1, source_target_pairs={{0,4},{4,0},{8,12},{12,8},{16,20},{20,16},{24,28},{28,24},{1,5},{5... | collective-permute-start | bytes 589832 | tf_op jit(solution)/shard_map/ppermute | solution.py:34
  24.9 10.7 %collective-permute-start.8 = (bf16[4,32,768]{2,1,0:T(8,128)(2,1)S(1)}, bf16[4,32,768]{2,1,0:T(8,128)(2,1)S(1)}, u32[]{:S(2)}, u32[]{:S(2)}) collective-permute-start(bf16[4,32,768]{2,1,0:T(8,128)(2,1)S(1)} %collective-permute-done.4.refs_2_), channel_id=1, source_target_pairs={{0,4},{4,0},{8,12},{12,8},{16,20},{20,16},{24,28},{28,24},{1,5},{5... | collective-permute-start | bytes 589832 | tf_op jit(solution)/shard_map/ppermute | solution.py:34
  28.3 7.3 %collective-permute-start.9 = (bf16[4,32,768]{2,1,0:T(8,128)(2,1)S(1)}, bf16[4,32,768]{2,1,0:T(8,128)(2,1)S(1)}, u32[]{:S(2)}, u32[]{:S(2)}) collective-permute-start(bf16[4,32,768]{2,1,0:T(8,128)(2,1)S(1)} %collective-permute-done.5.refs_3_), channel_id=1, source_target_pairs={{0,4},{4,0},{8,12},{12,8},{16,20},{20,16},{24,28},{28,24},{1,5},{5... | collective-permute-start | bytes 589832 | tf_op jit(solution)/shard_map/ppermute | solution.py:34
  32.6 18.5 %collective-permute-start.13 = (bf16[4,32,3072]{2,1,0:T(8,128)(2,1)S(1)}, bf16[4,32,3072]{2,1,0:T(8,128)(2,1)S(1)}, u32[]{:S(2)}, u32[]{:S(2)}) collective-permute-start(bf16[4,32,3072]{2,1,0:T(8,128)(2,1)S(1)} %all-to-all-done.refs_4_), channel_id=1, source_target_pairs={{0,16},{4,20},{8,24},{12,28},{16,0},{20,4},{24,8},{28,12},{1,17},{... | collective-permute-start | bytes 2359304 | tf_op jit(solution)/shard_map/ppermute | solution.py:34
  34.1 18.2 %collective-permute-start.14 = (bf16[4,32,3072]{2,1,0:T(8,128)(2,1)S(1)}, bf16[4,32,3072]{2,1,0:T(8,128)(2,1)S(1)}, u32[]{:S(2)}, u32[]{:S(2)}) collective-permute-start(bf16[4,32,3072]{2,1,0:T(8,128)(2,1)S(1)} %all-to-all-done.refs_4_), channel_id=1, source_target_pairs={{0,8},{4,12},{8,0},{12,4},{16,24},{20,28},{24,16},{28,20},{1,9},{5... | collective-permute-start | bytes 2359304 | tf_op jit(solution)/shard_map/ppermute | solution.py:34
  38.3 27.5 %copy-start.6 = (f32[1024]{0:T(1024)S(1)}, f32[1024]{0:T(1024)}, u32[]{:S(2)}) copy-start(f32[1024]{0:T(1024)} %param.22) | copy-start | bytes 12292
  42.1 11.8 %collective-permute-start.10 = (bf16[256,256]{1,0:T(8,128)(2,1)S(1)}, bf16[256,256]{1,0:T(8,128)(2,1)S(1)}, u32[]{:S(2)}, u32[]{:S(2)}) collective-permute-start(bf16[256,256]{1,0:T(8,128)(2,1)S(1)} %attend.1.refs_0_), channel_id=1, source_target_pairs={{0,1},{1,0},{2,3},{3,2},{4,5},{5,4},{6,7},{7,6},{8,9},{9,8},{10,11... | collective-permute-start | bytes 393224 | tf_op jit(solution)/shard_map/ppermute | solution.py:34
  42.2 12.4 %collective-permute-start.11 = (bf16[256,256]{1,0:T(8,128)(2,1)S(1)}, bf16[256,256]{1,0:T(8,128)(2,1)S(1)}, u32[]{:S(2)}, u32[]{:S(2)}) collective-permute-start(bf16[256,256]{1,0:T(8,128)(2,1)S(1)} %attend.1.refs_0_), channel_id=1, source_target_pairs={{0,2},{1,3},{2,0},{3,1},{4,6},{5,7},{6,4},{7,5},{8,10},{9,11},{10,... | collective-permute-start | bytes 393224 | tf_op jit(solution)/shard_map/ppermute | solution.py:34
  44.2 10.3 %collective-permute-start.12 = (bf16[256,256]{1,0:T(8,128)(2,1)S(1)}, bf16[256,256]{1,0:T(8,128)(2,1)S(1)}, u32[]{:S(2)}, u32[]{:S(2)}) collective-permute-start(bf16[256,256]{1,0:T(8,128)(2,1)S(1)} %attend.1.refs_0_), channel_id=1, source_target_pairs={{0,3},{1,2},{2,1},{3,0},{4,7},{5,6},{6,5},{7,4},{8,11},{9,10},{10,... | collective-permute-start | bytes 393224 | tf_op jit(solution)/shard_map/ppermute | solution.py:34
  51.1 13.0 %collective-permute-start.17 = (bf16[4,32,3072]{2,1,0:T(8,128)(2,1)S(1)}, bf16[4,32,3072]{2,1,0:T(8,128)(2,1)S(1)}, u32[]{:S(2)}, u32[]{:S(2)}) collective-permute-start(bf16[4,32,3072]{2,1,0:T(8,128)(2,1)S(1)} %all-to-all-done.refs_4_), channel_id=1, source_target_pairs={{0,4},{4,0},{8,12},{12,8},{16,20},{20,16},{24,28},{28,24},{1,5},{5... | collective-permute-start | bytes 2359304 | tf_op jit(solution)/shard_map/ppermute | solution.py:34
  52.3 10.4 %collective-permute-start.15 = (bf16[2,32,3072]{2,1,0:T(8,128)(2,1)S(1)}, bf16[2,32,3072]{2,1,0:T(8,128)(2,1)S(1)}, u32[]{:S(2)}, u32[]{:S(2)}) collective-permute-start(bf16[2,32,3072]{2,1,0:T(8,128)(2,1)S(1)} %slice.6), channel_id=1, source_target_pairs={{0,8},{4,12},{8,0},{12,4},{16,24},{20,28},{24,16},{28,20},{1,9},{5... | collective-permute-start | bytes 1179656 | tf_op jit(solution)/shard_map/ppermute | solution.py:34
  53.9 10.1 %collective-permute-start.16 = (bf16[2,32,3072]{2,1,0:T(8,128)(2,1)S(1)}, bf16[2,32,3072]{2,1,0:T(8,128)(2,1)S(1)}, u32[]{:S(2)}, u32[]{:S(2)}) collective-permute-start(bf16[2,32,3072]{2,1,0:T(8,128)(2,1)S(1)} %slice.7), channel_id=1, source_target_pairs={{0,16},{4,20},{8,24},{12,28},{16,0},{20,4},{24,8},{28,12},{1,17},{... | collective-permute-start | bytes 1179656 | tf_op jit(solution)/shard_map/ppermute | solution.py:34
  54.5 11.2 %collective-permute-start.18 = (bf16[4,32,3072]{2,1,0:T(8,128)(2,1)S(1)}, bf16[4,32,3072]{2,1,0:T(8,128)(2,1)S(1)}, u32[]{:S(2)}, u32[]{:S(2)}) collective-permute-start(bf16[4,32,3072]{2,1,0:T(8,128)(2,1)S(1)} %collective-permute-done.13.refs_5_), channel_id=1, source_target_pairs={{0,4},{4,0},{8,12},{12,8},{16,20},{20,16},{24,28},{28,24},{1,5},{5... | collective-permute-start | bytes 2359304 | tf_op jit(solution)/shard_map/ppermute | solution.py:34
  54.5 11.2 %collective-permute-start.19 = (bf16[4,32,3072]{2,1,0:T(8,128)(2,1)S(1)}, bf16[4,32,3072]{2,1,0:T(8,128)(2,1)S(1)}, u32[]{:S(2)}, u32[]{:S(2)}) collective-permute-start(bf16[4,32,3072]{2,1,0:T(8,128)(2,1)S(1)} %collective-permute-done.14.refs_6_), channel_id=1, source_target_pairs={{0,4},{4,0},{8,12},{12,8},{16,20},{20,16},{24,28},{28,24},{1,5},{5... | collective-permute-start | bytes 2359304 | tf_op jit(solution)/shard_map/ppermute | solution.py:34
  62.7 1.7 %collective-permute-start.20 = (bf16[2,32,3072]{2,1,0:T(8,128)(2,1)S(1)}, bf16[2,32,3072]{2,1,0:T(8,128)(2,1)S(1)}, u32[]{:S(2)}, u32[]{:S(2)}) collective-permute-start(bf16[2,32,3072]{2,1,0:T(8,128)(2,1)S(1)} %collective-permute-done.15.refs_7_), channel_id=1, source_target_pairs={{0,4},{4,0},{8,12},{12,8},{16,20},{20,16},{24,28},{28,24},{1,5},{5... | collective-permute-start | bytes 1179656 | tf_op jit(solution)/shard_map/ppermute | solution.py:34
  64.0 1.7 %collective-permute-start.21 = (bf16[2,32,3072]{2,1,0:T(8,128)(2,1)S(1)}, bf16[2,32,3072]{2,1,0:T(8,128)(2,1)S(1)}, u32[]{:S(2)}, u32[]{:S(2)}) collective-permute-start(bf16[2,32,3072]{2,1,0:T(8,128)(2,1)S(1)} %collective-permute-done.16.refs_8_), channel_id=1, source_target_pairs={{0,4},{4,0},{8,12},{12,8},{16,20},{20,16},{24,28},{28,24},{1,5},{5... | collective-permute-start | bytes 1179656 | tf_op jit(solution)/shard_map/ppermute | solution.py:34
  69.3 10.1 %collective-permute-start.22 = (bf16[64,1024]{1,0:T(8,128)(2,1)S(1)}, bf16[64,1024]{1,0:T(8,128)(2,1)S(1)}, u32[]{:S(2)}, u32[]{:S(2)}) collective-permute-start(bf16[64,1024]{1,0:T(8,128)(2,1)S(1)} %get-tuple-element.41), channel_id=1, source_target_pairs={{0,2},{1,3},{2,0},{3,1},{4,6},{5,7},{6,4},{7,5},{8,10},{9,11},{10,... | collective-permute-start | bytes 393224 | tf_op jit(solution)/shard_map/ppermute | solution.py:34
  69.3 10.1 %collective-permute-start.24 = (bf16[64,1024]{1,0:T(8,128)(2,1)S(1)}, bf16[64,1024]{1,0:T(8,128)(2,1)S(1)}, u32[]{:S(2)}, u32[]{:S(2)}) collective-permute-start(bf16[64,1024]{1,0:T(8,128)(2,1)S(1)} %get-tuple-element.44), channel_id=1, source_target_pairs={{0,3},{1,2},{2,1},{3,0},{4,7},{5,6},{6,5},{7,4},{8,11},{9,10},{10,... | collective-permute-start | bytes 393224 | tf_op jit(solution)/shard_map/ppermute | solution.py:34
  79.4 5.0 %collective-permute-start.23 = (bf16[64,1024]{1,0:T(8,128)(2,1)S(1)}, bf16[64,1024]{1,0:T(8,128)(2,1)S(1)}, u32[]{:S(2)}, u32[]{:S(2)}) collective-permute-start(bf16[64,1024]{1,0:T(8,128)(2,1)S(1)} %get-tuple-element.42), channel_id=1, source_target_pairs={{0,1},{1,0},{2,3},{3,2},{4,5},{5,4},{6,7},{7,6},{8,9},{9,8},{10,11... | collective-permute-start | bytes 393224 | tf_op jit(solution)/shard_map/ppermute | solution.py:34
  (9 other events, 76.7 us)
